TPU v7x, 256 devices: a whole 4x4x8 slice. The times are simulated.
256 devices in a mesh: sub: 64 (over z_hi, x, y), freq: 4 (over z_lo, core).
Axes of the slice: x: 4, y: 4, z: 8 (z_hi: 4, z_lo: 2; z = z_hi * 2 + z_lo), core: 2. Of those that a mesh axis runs over, the one named last changes fastest.
Arguments:
- source: float32 [64, 2, 3, 32, 32, 128], P('sub'), may hold values from -6 to 6
- adjoint_source: float32 [4, 64, 2, 3, 32, 32, 128], P('freq', 'sub'), may hold values from -6 to 6
- sigma_h: float32 [64, 32, 32, 128], P('sub'), may hold values from 0.3 to 3
- sigma_v: float32 [64, 32, 32, 128], P('sub'), may hold values from 0.1 to 1
- seafloor: int32 [64, 32, 32], P('sub'), may hold values from 0 to 63
- links: int32 [64, 4], P('sub'), may hold values from 0 to 1, as said below
- freq_index: int32 [4], P('freq'), may hold values from 0 to 3, each once
Outputs:
- forward_field: float32 [4, 64, 2, 3, 32, 32, 128], P('freq', 'sub')
- grad_h: float32 [64, 32, 32, 128], P('sub')
- grad_v: float32 [64, 32, 32, 128], P('sub')
Inputs may be any that keep to these rules, and one draw needn't show every extreme that they name: links is symmetric between lateral neighbours (the high x face of subdomain i and the low x face of subdomain i + 1, the high y face of i and the low y face of i + 8) and zero on the slab's outer faces.
All inputs are finite; a program needn't handle non-finite values.
Results may differ from a plain program's by a relative error of at most 0.0001.
Values sent between devices are 32-bit elements; how exact they have to be, the bound alone decides.
No kernel may reach another device: no remote copies, remote signals or barrier semaphores. Data moves between devices by JAX's collectives and lax.ppermute only.
A program may use at most 64 MiB of HBM per device.

v0:
```python
import jax
import jax.numpy as jnp
from jax import lax
from jax.sharding import PartitionSpec as P

SX = 8
ITERS = 2


P_ROBIN = 0.25
OMEGA0 = 0.5


def shifted(shard, axis, by):
    size = lax.axis_size(axis)
    pairs = [(i, i + by) for i in range(size) if 0 <= i + by < size]
    return lax.ppermute(shard, axis, pairs)


def update(rhs, shift3, mask):
    real_part = rhs[..., 0, :, :, :, :]
    imag_part = rhs[..., 1, :, :, :, :]
    denom = 36.0 + shift3 * shift3
    new_real = (6.0 * real_part + shift3 * imag_part) / denom
    new_imag = (6.0 * imag_part - shift3 * real_part) / denom
    return jnp.stack([new_real, new_imag], axis=-5) * mask[..., None, None, :, :, :]


def stencil_sum(field, ghost_lo_x, ghost_hi_x, ghost_lo_y, ghost_hi_y):
    along_x = jnp.concatenate(
        [ghost_lo_x[..., None, :, :], field, ghost_hi_x[..., None, :, :]], axis=-3
    )
    total = along_x[..., :-2, :, :] + along_x[..., 2:, :, :]
    along_y = jnp.concatenate(
        [ghost_lo_y[..., :, None, :], field, ghost_hi_y[..., :, None, :]], axis=-2
    )
    total = total + along_y[..., :, :-2, :] + along_y[..., :, 2:, :]
    zero_plane = jnp.zeros_like(field[..., :1])
    along_z = jnp.concatenate([zero_plane, field, zero_plane], axis=-1)
    return total + along_z[..., :-2] + along_z[..., 2:]


def trade_faces(field, link_flags):
    low_x = (1.0 + P_ROBIN) * field[..., 0, :, :] - P_ROBIN * field[..., 1, :, :]
    high_x = (1.0 + P_ROBIN) * field[..., -1, :, :] - P_ROBIN * field[..., -2, :, :]
    low_y = (1.0 + P_ROBIN) * field[..., :, 0, :] - P_ROBIN * field[..., :, 1, :]
    high_y = (1.0 + P_ROBIN) * field[..., :, -1, :] - P_ROBIN * field[..., :, -2, :]
    ghost_hi_x = shifted(low_x, "sub", -1) * link_flags[1]
    ghost_lo_x = shifted(high_x, "sub", 1) * link_flags[0]
    ghost_hi_y = shifted(low_y, "sub", -SX) * link_flags[3]
    ghost_lo_y = shifted(high_y, "sub", SX) * link_flags[2]
    return (ghost_lo_x, ghost_hi_x, ghost_lo_y, ghost_hi_y)


def relax(rhs_source, shift3, mask, link_flags):
    field = update(rhs_source, shift3, mask)
    for sweep in range(ITERS):
        ghosts = trade_faces(field, link_flags)
        field = update(rhs_source + stencil_sum(field, *ghosts), shift3, mask)
    return field


def on_device(source, adjoint_source, sigma_h, sigma_v, seafloor, links, freq_index):
    src_field = source[0]
    adj_field = adjoint_source[0, 0]
    cond_h = sigma_h[0]
    cond_v = sigma_v[0]
    depth = lax.broadcasted_iota(jnp.int32, cond_h.shape, 2)
    mask = (depth >= seafloor[0][:, :, None]).astype(jnp.float32)
    link_flags = links[0].astype(jnp.float32)
    scale = OMEGA0 * jnp.exp2(freq_index[0].astype(jnp.float32))
    shift3 = scale * jnp.stack([cond_h, cond_h, cond_v], axis=0)
    forward = relax(src_field, shift3, mask, link_flags)
    adjoint = relax(adj_field, shift3, mask, link_flags)
    product = adjoint[0] * forward[1] + adjoint[1] * forward[0]
    term_h = scale * (product[0] + product[1])
    term_v = scale * product[2]
    total_h, total_v = lax.psum((term_h, term_v), "freq")
    grad_h = cond_h * mask * total_h
    grad_v = cond_v * mask * total_v
    return (forward[None, None], grad_h[None], grad_v[None])


def solution(mesh):
    return jax.shard_map(
        on_device,
        mesh=mesh,
        in_specs=(
            P("sub", None, None, None, None, None),
            P("freq", "sub", None, None, None, None, None),
            P("sub", None, None, None),
            P("sub", None, None, None),
            P("sub", None, None),
            P("sub", None),
            P("freq"),
        ),
        out_specs=(
            P("freq", "sub", None, None, None, None, None),
            P("sub", None, None, None),
            P("sub", None, None, None),
        ),
        check_vma=False,
    )
```

profile of v0, /device:TPU:71, one launch (start us, length us, event | category | flops | bytes accessed | tf_op | source)
XLA Modules:
  0.0 209.9 jit_solution(5871434651568891004)
XLA Ops:
  7.2 5.4 %copy.524 = f32[1,1,2,3,32,32,128]{6,4,5,3,2,1,0:T(8,128)} copy(f32[1,1,2,3,32,32,128]{6,5,4,3,2,1,0:T(8,128)} %param.8) | data formatting | bytes 6291456 | tf_op args[1]
  14.3 2.5 %add_divide_fusion.2 = (f32[1,3,32,32,128]{4,2,3,1,0:T(8,128)S(1)}, f32[1,3,32,32,128]{4,2,3,1,0:T(8,128)S(1)}) fusion(f32[1,1,2,3,32,32,128]{6,4,5,3,2,1,0:T(8,128)} %copy.524, f32[1,1,32,32,128]{4,2,3,1,0:T(8,128)S(1)} %get-tuple-element.95, f32[1,1,32,32,128]{4,2,3,1,0:T(8,128)S(1)} %get-tuple-element.96, f32[]{:T(128)} %bitcast.3), kind=kLoop, calls=%fused_computation.69 | loop fusion | flops 5111808 | bytes 7340036 | tf_op jit(solution)/shard_map/div | solution.py:24
  17.5 3.2 %collective-permute-start.11 = (f32[2,3,32,128]{3,2,1,0:T(8,128)S(1)}, f32[2,3,32,128]{3,2,1,0:T(8,128)S(1)}, u32[]{:S(2)}, u32[]{:S(2)}) collective-permute-start(f32[2,3,32,128]{3,2,1,0:T(8,128)S(1)} %get-tuple-element.70), channel_id=1, source_target_pairs={{32,0},{36,4},{40,8},{44,12},{48,16},{52,20},{56,24},{60,28},{64,3... | collective-permute-start | bytes 294920 | tf_op jit(solution)/shard_map/ppermute | solution.py:17
  20.7 6.8 %collective-permute-start.10 = (f32[2,3,32,128]{3,2,1,0:T(8,128)S(1)}, f32[2,3,32,128]{3,2,1,0:T(8,128)S(1)}, u32[]{:S(2)}, u32[]{:S(2)}) collective-permute-start(f32[2,3,32,128]{3,2,1,0:T(8,128)S(1)} %get-tuple-element.69), channel_id=1, source_target_pairs={{0,32},{4,36},{8,40},{12,44},{16,48},{20,52},{24,56},{28,60},{32,6... | collective-permute-start | bytes 294920 | tf_op jit(solution)/shard_map/ppermute | solution.py:17
  27.8 4.9 %collective-permute-start.9 = (f32[2,3,32,128]{3,2,1,0:T(8,128)S(1)}, f32[2,3,32,128]{3,2,1,0:T(8,128)S(1)}, u32[]{:S(2)}, u32[]{:S(2)}) collective-permute-start(f32[2,3,32,128]{3,2,1,0:T(8,128)S(1)} %subtract_bitcast_fusion.2), channel_id=1, source_target_pairs={{4,0},{8,4},{12,8},{16,12},{20,16},{24,20},{28,24},{32,28},{36,32}... | collective-permute-start | bytes 294920 | tf_op jit(solution)/shard_map/ppermute | solution.py:17
  32.7 1.9 collective-permute-start.8
  36.2 0.7 multiply_bitcast_fusion.2
  36.9 0.7 multiply_bitcast_fusion.3
  38.1 2.1 collective-permute-done.8
  40.2 0.7 broadcast_multiply_fusion.4
  40.9 3.7 %fusion.8 = f32[2,3,32,32,128]{4,2,3,1,0:T(8,128)S(1)} fusion(f32[2,3,32,32,128]{4,2,3,1,0:T(8,128)S(1)} %maximum_multiply_fusion.2, f32[2,3,32,1,128]{4,2,3,1,0:T(8,128)S(1)} %multiply_bitcast_fusion.2, f32[2,3,32,1,128]{4,2,3,1,0:T(8,128)S(1)} %multiply_bitcast_fusion.3, f32[2,3,1,32,128]{4,2,3,1,0:T(1,128)S(1)} %bitcast.160, ...), kind=kLoop, calls=%fused_computation.16 | loop fusion | flops 7864320 | bytes 9830400 | tf_op jit(solution)/shard_map/add | solution.py:59
  46.2 1.9 collective-permute-start.15
  48.1 7.9 %collective-permute-start.14 = (f32[2,3,32,128]{3,2,1,0:T(8,128)S(1)}, f32[2,3,32,128]{3,2,1,0:T(8,128)S(1)}, u32[]{:S(2)}, u32[]{:S(2)}) collective-permute-start(f32[2,3,32,128]{3,2,1,0:T(8,128)S(1)} %get-tuple-element.63), channel_id=1, source_target_pairs={{0,32},{4,36},{8,40},{12,44},{16,48},{20,52},{24,56},{28,60},{32,6... | collective-permute-start | bytes 294920 | tf_op jit(solution)/shard_map/ppermute | solution.py:17
  56.0 3.4 %collective-permute-start.13 = (f32[2,3,32,128]{3,2,1,0:T(8,128)S(1)}, f32[2,3,32,128]{3,2,1,0:T(8,128)S(1)}, u32[]{:S(2)}, u32[]{:S(2)}) collective-permute-start(f32[2,3,32,128]{3,2,1,0:T(8,128)S(1)} %subtract_bitcast_fusion), channel_id=1, source_target_pairs={{4,0},{8,4},{12,8},{16,12},{20,16},{24,20},{28,24},{32,28},{36,32}... | collective-permute-start | bytes 294920 | tf_op jit(solution)/shard_map/ppermute | solution.py:17
  59.5 2.1 %collective-permute-start.12 = (f32[2,3,32,128]{3,2,1,0:T(8,128)S(1)}, f32[2,3,32,128]{3,2,1,0:T(8,128)S(1)}, u32[]{:S(2)}, u32[]{:S(2)}) collective-permute-start(f32[2,3,32,128]{3,2,1,0:T(8,128)S(1)} %subtract_bitcast_fusion.1), channel_id=1, source_target_pairs={{0,4},{4,8},{8,12},{12,16},{16,20},{20,24},{24,28},{28,32},{32,36}... | collective-permute-start | bytes 294920 | tf_op jit(solution)/shard_map/ppermute | solution.py:17
  61.6 0.7 multiply_bitcast_fusion
  62.3 0.7 multiply_bitcast_fusion.1
  63.5 3.4 %collective-permute-done.12 = f32[2,3,32,128]{3,2,1,0:T(8,128)S(1)} collective-permute-done((f32[2,3,32,128]{3,2,1,0:T(8,128)S(1)}, f32[2,3,32,128]{3,2,1,0:T(8,128)S(1)}, u32[]{:S(2)}, u32[]{:S(2)}) %collective-permute-start.12) | collective-permute-done | bytes 98336 | tf_op jit(solution)/shard_map/ppermute | solution.py:17
  67.6 3.7 %fusion.11 = f32[2,3,32,32,128]{4,2,3,1,0:T(8,128)S(1)} fusion(f32[2,3,32,32,128]{4,2,3,1,0:T(8,128)S(1)} %maximum_multiply_fusion.3, f32[2,3,32,1,128]{4,2,3,1,0:T(8,128)S(1)} %multiply_bitcast_fusion, f32[2,3,32,1,128]{4,2,3,1,0:T(8,128)S(1)} %multiply_bitcast_fusion.1, f32[2,3,1,32,128]{4,2,3,1,0:T(1,128)S(1)} %bitcast.161, ...), kind=kLoop, calls=%fused_computation.19 | loop fusion | flops 7864320 | bytes 9830400 | tf_op jit(solution)/shard_map/add | solution.py:59
  71.3 1.0 add_divide_fusion
  72.3 1.9 add_divide_fusion.5
  75.1 1.9 collective-permute-start.3
  77.1 7.9 %collective-permute-start.2 = (f32[2,3,32,128]{3,2,1,0:T(8,128)S(1)}, f32[2,3,32,128]{3,2,1,0:T(8,128)S(1)}, u32[]{:S(2)}, u32[]{:S(2)}) collective-permute-start(f32[2,3,32,128]{3,2,1,0:T(8,128)S(1)} %bitcast.178), channel_id=1, source_target_pairs={{0,32},{4,36},{8,40},{12,44},{16,48},{20,52},{24,56},{28,60},{32,6... | collective-permute-start | bytes 294920 | tf_op jit(solution)/shard_map/ppermute | solution.py:17
  84.9 2.0 collective-permute-start.1
  87.0 3.2 %collective-permute-start = (f32[2,3,32,128]{3,2,1,0:T(8,128)S(1)}, f32[2,3,32,128]{3,2,1,0:T(8,128)S(1)}, u32[]{:S(2)}, u32[]{:S(2)}) collective-permute-start(f32[2,3,32,128]{3,2,1,0:T(8,128)S(1)} %get-tuple-element.77), channel_id=1, source_target_pairs={{0,4},{4,8},{8,12},{12,16},{16,20},{20,24},{24,28},{28,32},{32,36}... | collective-permute-start | bytes 294920 | tf_op jit(solution)/shard_map/ppermute | solution.py:17
  90.3 0.7 multiply_bitcast_fusion.6
  90.9 0.7 multiply_bitcast_fusion.7
  92.4 2.1 collective-permute-done
  95.1 2.6 %fusion.2 = f32[2,3,32,32,128]{4,3,1,0,2:T(8,128)S(1)} fusion(f32[2,3,32,32,128]{4,3,1,0,2:T(8,128)S(1)} %maximum_multiply_fusion, f32[2,3,32,1,128]{4,3,1,0,2:T(1,128)S(1)} %copy.507, f32[2,3,32,1,128]{4,3,1,0,2:T(1,128)S(1)} %copy.503, f32[2,3,1,32,128]{4,3,1,0,2:T(8,128)S(1)} %multiply_bitcast_fusion.8, ...), kind=kLoop, calls=%fused_computation.10 | loop fusion | flops 7864320 | bytes 9830400 | tf_op jit(solution)/shard_map/add | solution.py:59
  97.8 1.9 add_divide_fusion.4
  100.1 2.0 maximum_multiply_fusion.4
  102.5 1.9 collective-permute-start.7
  104.4 8.1 %collective-permute-start.6 = (f32[2,3,32,128]{3,2,1,0:T(8,128)S(1)}, f32[2,3,32,128]{3,2,1,0:T(8,128)S(1)}, u32[]{:S(2)}, u32[]{:S(2)}) collective-permute-start(f32[2,3,32,128]{3,2,1,0:T(8,128)S(1)} %get-tuple-element.75), channel_id=1, source_target_pairs={{0,32},{4,36},{8,40},{12,44},{16,48},{20,52},{24,56},{28,60},{32,6... | collective-permute-start | bytes 294920 | tf_op jit(solution)/shard_map/ppermute | solution.py:17
  112.5 2.8 %collective-permute-start.5 = (f32[2,3,32,128]{3,2,1,0:T(8,128)S(1)}, f32[2,3,32,128]{3,2,1,0:T(8,128)S(1)}, u32[]{:S(2)}, u32[]{:S(2)}) collective-permute-start(f32[2,3,32,128]{3,2,1,0:T(8,128)S(1)} %subtract_bitcast_fusion.4), channel_id=1, source_target_pairs={{4,0},{8,4},{12,8},{16,12},{20,16},{24,20},{28,24},{32,28},{36,32}... | collective-permute-start | bytes 294920 | tf_op jit(solution)/shard_map/ppermute | solution.py:17
  115.4 2.5 %collective-permute-start.4 = (f32[2,3,32,128]{3,2,1,0:T(8,128)S(1)}, f32[2,3,32,128]{3,2,1,0:T(8,128)S(1)}, u32[]{:S(2)}, u32[]{:S(2)}) collective-permute-start(f32[2,3,32,128]{3,2,1,0:T(8,128)S(1)} %subtract_bitcast_fusion.5), channel_id=1, source_target_pairs={{0,4},{4,8},{8,12},{12,16},{16,20},{20,24},{24,28},{28,32},{32,36}... | collective-permute-start | bytes 294920 | tf_op jit(solution)/shard_map/ppermute | solution.py:17
  117.9 0.7 multiply_bitcast_fusion.4
  118.5 0.7 multiply_bitcast_fusion.5
  119.8 6.4 %collective-permute-done.4 = f32[2,3,32,128]{3,2,1,0:T(8,128)S(1)} collective-permute-done((f32[2,3,32,128]{3,2,1,0:T(8,128)S(1)}, f32[2,3,32,128]{3,2,1,0:T(8,128)S(1)}, u32[]{:S(2)}, u32[]{:S(2)}) %collective-permute-start.4) | collective-permute-done | bytes 98336 | tf_op jit(solution)/shard_map/ppermute | solution.py:17
  126.8 3.7 %fusion.5 = f32[2,3,32,32,128]{4,2,3,1,0:T(8,128)S(1)} fusion(f32[2,3,32,32,128]{4,2,3,1,0:T(8,128)S(1)} %get-tuple-element.88, f32[2,3,32,1,128]{4,2,3,1,0:T(8,128)S(1)} %multiply_bitcast_fusion.4, f32[2,3,32,1,128]{4,2,3,1,0:T(8,128)S(1)} %multiply_bitcast_fusion.5, f32[2,3,1,32,128]{4,2,3,1,0:T(1,128)S(1)} %bitcast.159, ...), kind=kLoop, calls=%fused_computation.13 | loop fusion | flops 7864320 | bytes 9830400 | tf_op jit(solution)/shard_map/add | solution.py:59
  131.5 0.7 copy-done.2
  132.2 0.8 fusion.24
  133.0 1.1 fusion.25
  134.1 1.9 maximum_multiply_fusion.1
  136.0 3.5 %copy.544 = f32[1,1,2,3,32,32,128]{6,5,4,3,2,1,0:T(8,128)} copy(f32[1,1,2,3,32,32,128]{6,4,5,3,2,1,0:T(8,128)S(1)} %maximum_multiply_fusion.1) | data formatting | bytes 6291456
  139.5 59.4 %all-reduce.11.cloned.1.call-done = (f32[32,32,128]{2,0,1:T(8,128)}, f32[32,32,128]{2,0,1:T(8,128)}) async-done(((f32[32,32,128]{2,0,1:T(8,128)}, f32[32,32,128]{2,0,1:T(8,128)}), (f32[32,32,128]{2,0,1:T(8,128)}, f32[32,32,128]{2,0,1:T(8,128)})) %all-reduce.11.cloned.1.call-update) | async-done | bytes 1048592 | tf_op jit(solution)/shard_map/psum | solution.py:78
  198.9 1.9 fusion.29
  200.9 1.1 copy.545
  202.0 1.1 copy.546
  (70 shorter events, 12.2 us)
Async XLA Ops:
  7.2 6.2 %copy-start.7 = (s32[1,32,32]{2,1,0:T(8,128)S(1)}, s32[1,32,32]{2,1,0:T(8,128)}, u32[]{:S(2)}) copy-start(s32[1,32,32]{2,1,0:T(8,128)} %param.11) | copy-start | bytes 12292
  7.2 6.5 %copy-start.3 = (f32[1,32,32,128]{3,2,1,0:T(8,128)S(1)}, f32[1,32,32,128]{3,2,1,0:T(8,128)}, u32[]{:S(2)}) copy-start(f32[1,32,32,128]{3,2,1,0:T(8,128)} %param.10) | copy-start | bytes 1572868
  7.2 6.5 %copy-start.5 = (f32[1,32,32,128]{3,2,1,0:T(8,128)S(1)}, f32[1,32,32,128]{3,2,1,0:T(8,128)}, u32[]{:S(2)}) copy-start(f32[1,32,32,128]{3,2,1,0:T(8,128)} %param.9) | copy-start | bytes 1572868
  7.2 191.7 %all-reduce.11.cloned.1.call-start = ((), (), s32[]{:S(2)}) async-start(), calls=%async_computation | async-start | bytes 2097152 | tf_op jit(solution)/shard_map/psum | solution.py:78
  16.8 18.2 %copy-start.8 = (s32[1,4]{1,0:T(1,128)S(1)}, s32[1,4]{1,0:T(1,128)}, u32[]{:S(2)}) copy-start(s32[1,4]{1,0:T(1,128)} %param.12) | copy-start | bytes 52
  16.8 18.2 %copy-start.1 = (f32[1,2,3,32,32,128]{5,4,3,2,1,0:T(8,128)S(1)}, f32[1,2,3,32,32,128]{5,4,3,2,1,0:T(8,128)}, u32[]{:S(2)}) copy-start(f32[1,2,3,32,32,128]{5,4,3,2,1,0:T(8,128)} %param.7) | copy-start | bytes 9437188
  17.5 18.7 %collective-permute-start.11 = (f32[2,3,32,128]{3,2,1,0:T(8,128)S(1)}, f32[2,3,32,128]{3,2,1,0:T(8,128)S(1)}, u32[]{:S(2)}, u32[]{:S(2)}) collective-permute-start(f32[2,3,32,128]{3,2,1,0:T(8,128)S(1)} %get-tuple-element.70), channel_id=1, source_target_pairs={{32,0},{36,4},{40,8},{44,12},{48,16},{52,20},{56,24},{60,28},{64,3... | collective-permute-start | bytes 294920 | tf_op jit(solution)/shard_map/ppermute | solution.py:17
  20.7 16.2 %collective-permute-start.10 = (f32[2,3,32,128]{3,2,1,0:T(8,128)S(1)}, f32[2,3,32,128]{3,2,1,0:T(8,128)S(1)}, u32[]{:S(2)}, u32[]{:S(2)}) collective-permute-start(f32[2,3,32,128]{3,2,1,0:T(8,128)S(1)} %get-tuple-element.69), channel_id=1, source_target_pairs={{0,32},{4,36},{8,40},{12,44},{16,48},{20,52},{24,56},{28,60},{32,6... | collective-permute-start | bytes 294920 | tf_op jit(solution)/shard_map/ppermute | solution.py:17
  27.8 9.7 %collective-permute-start.9 = (f32[2,3,32,128]{3,2,1,0:T(8,128)S(1)}, f32[2,3,32,128]{3,2,1,0:T(8,128)S(1)}, u32[]{:S(2)}, u32[]{:S(2)}) collective-permute-start(f32[2,3,32,128]{3,2,1,0:T(8,128)S(1)} %subtract_bitcast_fusion.2), channel_id=1, source_target_pairs={{4,0},{8,4},{12,8},{16,12},{20,16},{24,20},{28,24},{32,28},{36,32}... | collective-permute-start | bytes 294920 | tf_op jit(solution)/shard_map/ppermute | solution.py:17
  32.7 7.5 %collective-permute-start.8 = (f32[2,3,32,128]{3,2,1,0:T(8,128)S(1)}, f32[2,3,32,128]{3,2,1,0:T(8,128)S(1)}, u32[]{:S(2)}, u32[]{:S(2)}) collective-permute-start(f32[2,3,32,128]{3,2,1,0:T(8,128)S(1)} %subtract_bitcast_fusion.3), channel_id=1, source_target_pairs={{0,4},{4,8},{8,12},{12,16},{16,20},{20,24},{24,28},{28,32},{32,36}... | collective-permute-start | bytes 294920 | tf_op jit(solution)/shard_map/ppermute | solution.py:17
  35.0 5.9 %copy-start = (f32[1,1,2,3,32,32,128]{6,5,4,3,2,1,0:T(8,128)S(1)}, f32[1,1,2,3,32,32,128]{6,5,4,3,2,1,0:T(8,128)}, u32[]{:S(2)}) copy-start(f32[1,1,2,3,32,32,128]{6,5,4,3,2,1,0:T(8,128)} %param.8) | copy-start | bytes 9437188
  46.2 15.4 %collective-permute-start.15 = (f32[2,3,32,128]{3,2,1,0:T(8,128)S(1)}, f32[2,3,32,128]{3,2,1,0:T(8,128)S(1)}, u32[]{:S(2)}, u32[]{:S(2)}) collective-permute-start(f32[2,3,32,128]{3,2,1,0:T(8,128)S(1)} %get-tuple-element.64), channel_id=1, source_target_pairs={{32,0},{36,4},{40,8},{44,12},{48,16},{52,20},{56,24},{60,28},{64,3... | collective-permute-start | bytes 294920 | tf_op jit(solution)/shard_map/ppermute | solution.py:17
  48.1 14.1 %collective-permute-start.14 = (f32[2,3,32,128]{3,2,1,0:T(8,128)S(1)}, f32[2,3,32,128]{3,2,1,0:T(8,128)S(1)}, u32[]{:S(2)}, u32[]{:S(2)}) collective-permute-start(f32[2,3,32,128]{3,2,1,0:T(8,128)S(1)} %get-tuple-element.63), channel_id=1, source_target_pairs={{0,32},{4,36},{8,40},{12,44},{16,48},{20,52},{24,56},{28,60},{32,6... | collective-permute-start | bytes 294920 | tf_op jit(solution)/shard_map/ppermute | solution.py:17
  56.0 6.9 %collective-permute-start.13 = (f32[2,3,32,128]{3,2,1,0:T(8,128)S(1)}, f32[2,3,32,128]{3,2,1,0:T(8,128)S(1)}, u32[]{:S(2)}, u32[]{:S(2)}) collective-permute-start(f32[2,3,32,128]{3,2,1,0:T(8,128)S(1)} %subtract_bitcast_fusion), channel_id=1, source_target_pairs={{4,0},{8,4},{12,8},{16,12},{20,16},{24,20},{28,24},{32,28},{36,32}... | collective-permute-start | bytes 294920 | tf_op jit(solution)/shard_map/ppermute | solution.py:17
  59.5 7.5 %collective-permute-start.12 = (f32[2,3,32,128]{3,2,1,0:T(8,128)S(1)}, f32[2,3,32,128]{3,2,1,0:T(8,128)S(1)}, u32[]{:S(2)}, u32[]{:S(2)}) collective-permute-start(f32[2,3,32,128]{3,2,1,0:T(8,128)S(1)} %subtract_bitcast_fusion.1), channel_id=1, source_target_pairs={{0,4},{4,8},{8,12},{12,16},{16,20},{20,24},{24,28},{28,32},{32,36}... | collective-permute-start | bytes 294920 | tf_op jit(solution)/shard_map/ppermute | solution.py:17
  75.1 15.2 %collective-permute-start.3 = (f32[2,3,32,128]{3,2,1,0:T(8,128)S(1)}, f32[2,3,32,128]{3,2,1,0:T(8,128)S(1)}, u32[]{:S(2)}, u32[]{:S(2)}) collective-permute-start(f32[2,3,32,128]{3,2,1,0:T(8,128)S(1)} %bitcast.177), channel_id=1, source_target_pairs={{32,0},{36,4},{40,8},{44,12},{48,16},{52,20},{56,24},{60,28},{64,3... | collective-permute-start | bytes 294920 | tf_op jit(solution)/shard_map/ppermute | solution.py:17
  77.1 13.9 %collective-permute-start.2 = (f32[2,3,32,128]{3,2,1,0:T(8,128)S(1)}, f32[2,3,32,128]{3,2,1,0:T(8,128)S(1)}, u32[]{:S(2)}, u32[]{:S(2)}) collective-permute-start(f32[2,3,32,128]{3,2,1,0:T(8,128)S(1)} %bitcast.178), channel_id=1, source_target_pairs={{0,32},{4,36},{8,40},{12,44},{16,48},{20,52},{24,56},{28,60},{32,6... | collective-permute-start | bytes 294920 | tf_op jit(solution)/shard_map/ppermute | solution.py:17
  84.9 6.6 %collective-permute-start.1 = (f32[2,3,32,128]{3,2,1,0:T(8,128)S(1)}, f32[2,3,32,128]{3,2,1,0:T(8,128)S(1)}, u32[]{:S(2)}, u32[]{:S(2)}) collective-permute-start(f32[2,3,32,128]{3,2,1,0:T(8,128)S(1)} %get-tuple-element.78), channel_id=1, source_target_pairs={{4,0},{8,4},{12,8},{16,12},{20,16},{24,20},{28,24},{32,28},{36,32}... | collective-permute-start | bytes 294920 | tf_op jit(solution)/shard_map/ppermute | solution.py:17
  87.0 7.5 %collective-permute-start = (f32[2,3,32,128]{3,2,1,0:T(8,128)S(1)}, f32[2,3,32,128]{3,2,1,0:T(8,128)S(1)}, u32[]{:S(2)}, u32[]{:S(2)}) collective-permute-start(f32[2,3,32,128]{3,2,1,0:T(8,128)S(1)} %get-tuple-element.77), channel_id=1, source_target_pairs={{0,4},{4,8},{8,12},{12,16},{16,20},{20,24},{24,28},{28,32},{32,36}... | collective-permute-start | bytes 294920 | tf_op jit(solution)/shard_map/ppermute | solution.py:17
  102.5 15.4 %collective-permute-start.7 = (f32[2,3,32,128]{3,2,1,0:T(8,128)S(1)}, f32[2,3,32,128]{3,2,1,0:T(8,128)S(1)}, u32[]{:S(2)}, u32[]{:S(2)}) collective-permute-start(f32[2,3,32,128]{3,2,1,0:T(8,128)S(1)} %get-tuple-element.76), channel_id=1, source_target_pairs={{32,0},{36,4},{40,8},{44,12},{48,16},{52,20},{56,24},{60,28},{64,3... | collective-permute-start | bytes 294920 | tf_op jit(solution)/shard_map/ppermute | solution.py:17
  104.4 14.1 %collective-permute-start.6 = (f32[2,3,32,128]{3,2,1,0:T(8,128)S(1)}, f32[2,3,32,128]{3,2,1,0:T(8,128)S(1)}, u32[]{:S(2)}, u32[]{:S(2)}) collective-permute-start(f32[2,3,32,128]{3,2,1,0:T(8,128)S(1)} %get-tuple-element.75), channel_id=1, source_target_pairs={{0,32},{4,36},{8,40},{12,44},{16,48},{20,52},{24,56},{28,60},{32,6... | collective-permute-start | bytes 294920 | tf_op jit(solution)/shard_map/ppermute | solution.py:17
  112.5 6.7 %collective-permute-start.5 = (f32[2,3,32,128]{3,2,1,0:T(8,128)S(1)}, f32[2,3,32,128]{3,2,1,0:T(8,128)S(1)}, u32[]{:S(2)}, u32[]{:S(2)}) collective-permute-start(f32[2,3,32,128]{3,2,1,0:T(8,128)S(1)} %subtract_bitcast_fusion.4), channel_id=1, source_target_pairs={{4,0},{8,4},{12,8},{16,12},{20,16},{24,20},{28,24},{32,28},{36,32}... | collective-permute-start | bytes 294920 | tf_op jit(solution)/shard_map/ppermute | solution.py:17
  115.4 10.7 %collective-permute-start.4 = (f32[2,3,32,128]{3,2,1,0:T(8,128)S(1)}, f32[2,3,32,128]{3,2,1,0:T(8,128)S(1)}, u32[]{:S(2)}, u32[]{:S(2)}) collective-permute-start(f32[2,3,32,128]{3,2,1,0:T(8,128)S(1)} %subtract_bitcast_fusion.5), channel_id=1, source_target_pairs={{0,4},{4,8},{8,12},{12,16},{16,20},{20,24},{24,28},{28,32},{32,36}... | collective-permute-start | bytes 294920 | tf_op jit(solution)/shard_map/ppermute | solution.py:17
  131.0 1.2 copy-start.2
  136.0 62.9 %copy-start.4 = (f32[1,32,32,128]{3,2,1,0:T(8,128)S(1)}, f32[1,32,32,128]{3,2,1,0:T(8,128)}, u32[]{:S(2)}) copy-start(f32[1,32,32,128]{3,2,1,0:T(8,128)} %param.10) | copy-start | bytes 1572868
  136.0 62.9 %copy-start.6 = (f32[1,32,32,128]{3,2,1,0:T(8,128)S(1)}, f32[1,32,32,128]{3,2,1,0:T(8,128)}, u32[]{:S(2)}) copy-start(f32[1,32,32,128]{3,2,1,0:T(8,128)} %param.9) | copy-start | bytes 1572868
Sparse Core Ops, SparseCore 0:
  134.3 64.6 all-reduce.10
where the time goes:
time: 212 us; the launch traced here: 210 us
  waiting for transfers between devices  73.5 us (35%)
  starting transfers between devices  62.5 us (29%)
  other arithmetic  43.3 us (20%)
  between operations  15.5 us (7%)
  local copies, waits for them, and re-layouts  15.2 us (7%)
    ppermute x16, starting transfers between devices, shifted(): return lax.ppermute(shard, axis, pairs)  62.4 us
    psum x1, waiting for transfers between devices, on_device(): total_h, total_v = lax.psum((term_h, term_v), 'freq')  59.4 us
    ppermute x16, waiting for transfers between devices, shifted(): return lax.ppermute(shard, axis, pairs)  14 us
    add x4, other arithmetic, relax(): field = update(rhs_source + stencil_sum(field, *ghosts), shift3, mask)  13.6 us
    unnamed x23, local copies, waits for them, and re-layouts  12.2 us
    div x6, other arithmetic, update(): new_real = (6.0 * real_part + shift3 * imag_part) / denom  8.51 us
    mul x6, other arithmetic, update(): jnp.stack([new_real, new_imag], axis=-5) * mask[..., None, None, :, :, :]  6.18 us
  transfers between devices with their start and end apart: 17, of which 5 were waited for; matrix products, arithmetic and copies ran while one was open for 7% of the time, Pallas kernels for 0%

commit v1 on v0

v1 whole, which is shorter than its diff:
```python
import jax
import jax.numpy as jnp
from jax import lax
from jax.experimental import pallas as pl
from jax.experimental.pallas import tpu as pltpu
from jax.sharding import PartitionSpec as P

SX = 8
SUBS = 64
N = 32
NZ = 128
PLANE = 40
ROWS = 34 * PLANE
STEP = 8
BLOCK = STEP * N
CELLS = N * N
NF = 12
FACE = NF * N
X_V, X_S, X_R, X_C, X_ROWS = FACE, 2 * FACE, 2 * FACE + 64, 2 * FACE + 112, 2 * FACE + 120
Y_ROWS = 2 * FACE + 64
T_ROWS = 72

P_ROBIN = 0.25
OMEGA0 = 0.5
KEEP = 1.0 + P_ROBIN
f32 = jnp.float32


def whole(space=pltpu.VMEM):
    return pl.BlockSpec(memory_space=space)


def params(steps=0):
    kind = {"dimension_semantics": ("arbitrary",)} if steps else {}
    return pltpu.CompilerParams(vmem_limit_bytes=30 * 2**20, **kind)


def cost(flops, size):
    return pl.CostEstimate(flops=flops, bytes_accessed=size, transcendentals=0)


def base(x):
    return (x + 1) * PLANE


def scale_of(freq_ref):
    return OMEGA0 * jnp.left_shift(jnp.int32(1), freq_ref[0]).astype(f32)


def lane_neighbours(u):
    lane = lax.broadcasted_iota(jnp.int32, u.shape, 1)
    before = jnp.where(lane == 0, 0.0, pltpu.roll(u, 1, 1))
    after = jnp.where(lane == NZ - 1, 0.0, pltpu.roll(u, NZ - 1, 1))
    return before + after


def row_neighbours(u):
    row = lax.broadcasted_iota(jnp.int32, u.shape, 0)
    before = jnp.where(row == 0, 0.0, pltpu.roll(u, 1, 0))
    after = jnp.where(row == N - 1, 0.0, pltpu.roll(u, N - 1, 0))
    return before + after


def factors(shift):
    inverse = 1.0 / (36.0 + shift * shift)
    return jnp.where(shift > 0.0, 6.0 * inverse, 0.0), shift * inverse


def times(ab, re, im):
    a, b = ab
    return a * re + b * im, a * im - b * re


def pairs():
    for solve in range(2):
        for comp in range(3):
            yield solve * 6 + comp, solve * 6 + 3 + comp, comp // 2


def trace(outer, inner):
    return KEEP * outer - P_ROBIN * inner


def stencil(ref, f, x):
    start = base(x)
    centre = ref[f, pl.ds(start, N), :]
    total = ref[f, pl.ds(start - PLANE, N), :] + ref[f, pl.ds(start + PLANE, N), :]
    total = total + (ref[f, pl.ds(start - 1, N), :] + ref[f, pl.ds(start + 1, N), :])
    return total + lane_neighbours(centre)


def first_kernel(
    freq_ref, links_ref, floor_ref, src_ref, adj_ref, sh_ref, sv_ref,
    u_ref, v_ref, ab_ref, px0_ref, px1_ref, py0_ref, py1_ref,
    shift_ref, xl_ref, xh_ref, yl_ref, yh_ref,
):
    step = pl.program_id(0)
    scale = scale_of(freq_ref)

    @pl.when(step == 0)
    def _():
        zeros = jnp.zeros((PLANE, NZ), f32)
        for f in range(NF):
            for ref in (u_ref, v_ref):
                ref[f, 0:PLANE, :] = zeros
                ref[f, ROWS - PLANE:ROWS, :] = zeros

    @pl.when(step < N // STEP)
    def _():
        def plane(j, carry):
            x = step * STEP + j
            here = pl.ds(pl.multiple_of(j * N, N), N)
            there = pl.ds(pl.multiple_of(x * N, N), N)
            start = pl.multiple_of(base(x), 8)
            floor = floor_ref[pl.ds(x, 1), :].astype(f32)
            row = lax.broadcasted_iota(jnp.int32, (N, N), 0)
            col = lax.broadcasted_iota(jnp.int32, (N, N), 1)
            column = jnp.sum(jnp.where(row == col, floor, 0.0), axis=1, keepdims=True)
            depth = lax.broadcasted_iota(jnp.int32, (N, NZ), 1).astype(f32)
            mask = (depth >= column).astype(f32)
            ab = []
            for k, ref in enumerate((sh_ref, sv_ref)):
                shift = scale * ref[here, :] * mask
                shift_ref[k, there, :] = shift
                ab.append(factors(shift))
                ab_ref[2 * k, there, :] = ab[k][0]
                ab_ref[2 * k + 1, there, :] = ab[k][1]
            zeros = jnp.zeros((8, NZ), f32)
            for fr, fi, k in pairs():
                ref, g = (src_ref, 0) if fr < 6 else (adj_ref, 6)
                re, im = times(ab[k], ref[fr - g, here, :], ref[fi - g, here, :])
                for f, value in ((fr, re), (fi, im)):
                    u_ref[f, pl.ds(start, N), :] = value
                    u_ref[f, pl.ds(start + N, 8), :] = zeros
                    v_ref[f, pl.ds(start + N, 8), :] = zeros
            return carry

        lax.fori_loop(0, STEP, plane, 0)

    @pl.when(step > 0)
    def _():
        def plane(j, carry):
            x = (step - 1) * STEP + j
            there = pl.ds(pl.multiple_of(x * N, N), N)
            start = pl.multiple_of(base(x), 8)
            ab = [(ab_ref[2 * k, there, :], ab_ref[2 * k + 1, there, :]) for k in range(2)]
            for fr, fi, k in pairs():
                re, im = times(ab[k], stencil(u_ref, fr, x), stencil(u_ref, fi, x))
                v_ref[fr, pl.ds(start, N), :] = u_ref[fr, pl.ds(start, N), :] + re
                v_ref[fi, pl.ds(start, N), :] = u_ref[fi, pl.ds(start, N), :] + im
            return carry

        lax.fori_loop(0, STEP, plane, 0)

    @pl.when(step == N // STEP)
    def _():
        link_y = [links_ref[0, 2].astype(f32), links_ref[0, 3].astype(f32)]

        def field(f, carry):
            for ref, at in ((u_ref, 0), (v_ref, FACE)):
                out = pl.ds(pl.multiple_of(at + f * N, N), N)
                layer = [ref[f, pl.ds(base(x), N), :] for x in (0, 1, N - 2, N - 1)]
                xl_ref[out, :] = trace(layer[0], layer[1])
                xh_ref[out, :] = trace(layer[3], layer[2])
                for b in range(N // 8):
                    out = pl.ds(pl.multiple_of(at + f * N + b * 8, 8), 8)
                    layer = [ref[f, pl.ds(base(b * 8) + y, 8, stride=PLANE), :] for y in (0, 1, N - 2, N - 1)]
                    yl_ref[out, :] = trace(layer[0], layer[1])
                    yh_ref[out, :] = trace(layer[3], layer[2])
            return carry

        lax.fori_loop(0, NF, field, 0)
        for k in range(2):
            out = slice(X_S + k * N, X_S + (k + 1) * N)
            xl_ref[out, :] = shift_ref[k, 0:N, :]
            xh_ref[out, :] = shift_ref[k, CELLS - N:CELLS, :]
            yl_ref[out, :] = shift_ref[k, pl.ds(0, N, stride=N), :]
            yh_ref[out, :] = shift_ref[k, pl.ds(N - 1, N, stride=N), :]
        for e, y_ref in enumerate((yl_ref, yh_ref)):
            for f in range(NF):
                at = X_R + e * 24 + f * 2
                xl_ref[at:at + 2, :] = y_ref[f * N:f * N + 2, :] * link_y[e]
                xh_ref[at:at + 2, :] = y_ref[f * N + 30:f * N + 32, :] * link_y[e]
            for k in range(2):
                for layer in range(2):
                    at = X_C + e * 4 + k * 2 + layer
                    y = e * (N - 1)
                    low = layer * N + y
                    high = (N - 1 - layer) * N + y
                    xl_ref[at:at + 1, :] = shift_ref[k, low:low + 1, :]
                    xh_ref[at:at + 1, :] = shift_ref[k, high:high + 1, :]
        sub = lax.axis_index("sub")
        odd_x = lax.rem(sub, 2) == 1
        odd_y = lax.rem(lax.div(sub, SX), 2) == 1
        low, high = xl_ref[...], xh_ref[...]
        px0_ref[...] = jnp.where(odd_x, low, high)
        px1_ref[...] = jnp.where(odd_x, high, low)
        low, high = yl_ref[...], yh_ref[...]
        py0_ref[...] = jnp.where(odd_y, low, high)
        py1_ref[...] = jnp.where(odd_y, high, low)


def second_kernel(freq_ref, u_ref, v_ref, ab_ref, w_ref, keep_ref, send_ref):
    step = pl.program_id(0)
    scale = scale_of(freq_ref)
    odd_core = lax.rem(lax.axis_index("freq"), 2) == 1

    def plane(j, carry):
        x = step * STEP + j
        here = pl.ds(pl.multiple_of(j * N, N), N)
        there = pl.ds(pl.multiple_of(x * N, N), N)
        start = pl.multiple_of(base(x), 8)
        ab = [(ab_ref[2 * k, there, :], ab_ref[2 * k + 1, there, :]) for k in range(2)]
        term = [None, None]
        for comp in range(3):
            k = comp // 2
            new = []
            for solve in range(2):
                fr, fi = solve * 6 + comp, solve * 6 + 3 + comp
                re, im = times(ab[k], stencil(v_ref, fr, x), stencil(v_ref, fi, x))
                re = re + u_ref[fr, pl.ds(start, N), :]
                im = im + u_ref[fi, pl.ds(start, N), :]
                w_ref[fr, there, :] = re
                w_ref[fi, there, :] = im
                new.append((re, im))
            product = new[1][0] * new[0][1] + new[1][1] * new[0][0]
            term[k] = product if term[k] is None else term[k] + product
        term_h, term_v = scale * term[0], scale * term[1]
        keep_ref[here, :] = jnp.where(odd_core, term_v, term_h)
        send_ref[here, :] = jnp.where(odd_core, term_h, term_v)
        return carry

    lax.fori_loop(0, STEP, plane, 0)


def edge_kernel(links_ref, ab_ref, rx0_ref, rx1_ref, ty0_ref, ty1_ref, tl_ref, th_ref):
    sub = lax.axis_index("sub")
    odd_x = lax.rem(sub, 2) == 1
    odd_y = lax.rem(lax.div(sub, SX), 2) == 1

    def from_x(side, rows):
        first, second = rx0_ref[rows, :], rx1_ref[rows, :]
        return jnp.where(odd_x, first, second) if side == 0 else jnp.where(odd_x, second, first)

    for e, t_ref in enumerate((tl_ref, th_ref)):
        outer, inner = (0, 1) if e == 0 else (N - 1, N - 2)
        for side in range(2):
            link = links_ref[0, side].astype(f32)
            x = side * (N - 1)
            for fr, fi, k in pairs():
                layers = []
                for y in (outer, inner):
                    at = x * N + y
                    ab = (ab_ref[2 * k, at:at + 1, :], ab_ref[2 * k + 1, at:at + 1, :])
                    re = link * from_x(side, slice(fr * N + y, fr * N + y + 1))
                    im = link * from_x(side, slice(fi * N + y, fi * N + y + 1))
                    layers.append(times(ab, re, im))
                t_ref[side * NF + fr:side * NF + fr + 1, :] = trace(layers[0][0], layers[1][0])
                t_ref[side * NF + fi:side * NF + fi + 1, :] = trace(layers[0][1], layers[1][1])
            at = X_R + e * 24
            t_ref[24 + side * 24:48 + side * 24, :] = from_x(side, slice(at, at + 24))
    low, high = tl_ref[...], th_ref[...]
    ty0_ref[...] = jnp.where(odd_y, low, high)
    ty1_ref[...] = jnp.where(odd_y, high, low)


def boundary_kernel(
    freq_ref, links_ref, u_ref, ab_ref, w_ref, rx0_ref, rx1_ref, ry0_ref, ry1_ref, rt0_ref, rt1_ref,
    planes_ref, rows_ref, keep_ref, send_ref,
):
    scale = scale_of(freq_ref)
    sub = lax.axis_index("sub")
    odd_x = lax.rem(sub, 2) == 1
    odd_y = lax.rem(lax.div(sub, SX), 2) == 1
    odd_core = lax.rem(lax.axis_index("freq"), 2) == 1
    link = [links_ref[0, k].astype(f32) for k in range(4)]
    row = lax.broadcasted_iota(jnp.int32, (N, NZ), 0)

    def pick(odd, side, first_ref, second_ref, rows):
        first, second = first_ref[rows, :], second_ref[rows, :]
        return jnp.where(odd, first, second) if side == 0 else jnp.where(odd, second, first)

    def from_x(side, at, size):
        return pick(odd_x, side, rx0_ref, rx1_ref, slice(at, at + size))

    def from_y(side, at, size):
        return pick(odd_y, side, ry0_ref, ry1_ref, slice(at, at + size))

    def from_t(side, at, size):
        return pick(odd_y, side, rt0_ref, rt1_ref, slice(at, at + size))

    def ends(first, last):
        return jnp.where(row == 0, first, jnp.where(row == N - 1, last, 0.0))

    def ab_plane(k, x):
        return ab_ref[2 * k, x * N:(x + 1) * N, :], ab_ref[2 * k + 1, x * N:(x + 1) * N, :]

    def ab_row(k, y):
        return ab_ref[2 * k, pl.ds(y, N, stride=N), :], ab_ref[2 * k + 1, pl.ds(y, N, stride=N), :]

    near_x = [[factors(from_x(s, X_S + k * N, N)) for k in range(2)] for s in range(2)]
    near_y = [[factors(from_y(s, X_S + k * N, N)) for k in range(2)] for s in range(2)]
    corner = [[[[factors(from_x(s, X_C + e * 4 + k * 2 + layer, 1)) for layer in range(2)]
                for k in range(2)] for e in range(2)] for s in range(2)]

    for fr, fi, k in pairs():
        both = (fr, fi)
        edge, ghost_y = [], []
        for e in range(2):
            outer, inner = (0, 1) if e == 0 else (N - 1, N - 2)
            g1 = [link[2 + e] * from_y(e, f * N, N) for f in both]
            edge.append((g1, times(ab_row(k, outer), *g1)))
            own = [trace(u_ref[f, pl.ds(base(0) + outer, N, stride=PLANE), :],
                         u_ref[f, pl.ds(base(0) + inner, N, stride=PLANE), :]) for f in both]
            back = times(near_y[e][k], *own)
            ghost_y.append([
                link[2 + e] * (from_y(e, FACE + f * N, N) + KEEP * back[c] + ends(from_t(e, f, 1), from_t(e, NF + f, 1)))
                for c, f in enumerate(both)
            ])
        for s in range(2):
            x0, x1, x2 = (0, 1, 2) if s == 0 else (N - 1, N - 2, N - 3)
            g1 = [link[s] * from_x(s, f * N, N) + ends(edge[0][0][c][x0:x0 + 1, :], edge[1][0][c][x0:x0 + 1, :])
                  for c, f in enumerate(both)]
            ab0, ab1 = ab_plane(k, x0), ab_plane(k, x1)
            w0 = times(ab0, *g1)
            own = [trace(u_ref[f, base(x0):base(x0) + N, :], u_ref[f, base(x1):base(x1) + N, :]) for f in both]
            back = times(near_x[s][k], *own)
            corners = []
            for e in range(2):
                layers = []
                for layer in range(2):
                    col = layer if s == 1 else 1 - layer
                    relay = [from_t(e, 24 + s * 24 + f * 2 + col, 1) for f in both]
                    layers.append(times(corner[s][e][k][layer], *relay))
                corners.append([trace(layers[0][c], layers[1][c]) for c in range(2)])
            rhs0, rhs1 = [], []
            for c, f in enumerate(both):
                ghost = link[s] * (from_x(s, FACE + f * N, N) + KEEP * back[c] + ends(corners[0][c], corners[1][c]))
                m1 = ends(edge[0][1][c][x1:x1 + 1, :], edge[1][1][c][x1:x1 + 1, :])
                m2 = ends(edge[0][1][c][x2:x2 + 1, :], edge[1][1][c][x2:x2 + 1, :])
                side0 = ends(ghost_y[0][c][x0:x0 + 1, :], ghost_y[1][c][x0:x0 + 1, :])
                side1 = ends(ghost_y[0][c][x1:x1 + 1, :], ghost_y[1][c][x1:x1 + 1, :])
                rhs0.append(row_neighbours(w0[c]) + lane_neighbours(w0[c]) + m1 + ghost + side0)
                rhs1.append(w0[c] + m2 + row_neighbours(m1) + lane_neighbours(m1) + side1)
            fix0, fix1 = times(ab0, *rhs0), times(ab1, *rhs1)
            at0, at1 = (0, 1) if s == 0 else (3, 2)
            for c, f in enumerate(both):
                planes_ref[f, at0 * N:(at0 + 1) * N, :] = w_ref[f, x0 * N:(x0 + 1) * N, :] + fix0[c]
                planes_ref[f, at1 * N:(at1 + 1) * N, :] = w_ref[f, x1 * N:(x1 + 1) * N, :] + fix1[c]
        for e in range(2):
            outer, inner = (0, 1) if e == 0 else (N - 1, N - 2)
            w0 = edge[e][1]
            rhs = [row_neighbours(w0[c]) + lane_neighbours(w0[c]) + ghost_y[e][c] for c in range(2)]
            fix0 = times(ab_row(k, outer), *rhs)
            fix1 = times(ab_row(k, inner), *w0)
            at0, at1 = (0, 1) if e == 0 else (3, 2)
            for c, f in enumerate(both):
                rows_ref[f, at0 * N:(at0 + 1) * N, :] = w_ref[f, pl.ds(outer, N, stride=N), :] + fix0[c]
                rows_ref[f, at1 * N:(at1 + 1) * N, :] = w_ref[f, pl.ds(inner, N, stride=N), :] + fix1[c]
    for ref, at in ((planes_ref, 0), (rows_ref, 4 * N)):
        term = [None, None]
        for comp in range(3):
            product = ref[6 + comp] * ref[3 + comp] + ref[9 + comp] * ref[comp]
            term[comp // 2] = product if comp % 2 == 0 else term[0] + product
        term_h, term_v = scale * term[0], scale * term[1]
        keep_ref[at:at + 4 * N, :] = jnp.where(odd_core, term_v, term_h)
        send_ref[at:at + 4 * N, :] = jnp.where(odd_core, term_h, term_v)


def put_boundary(step, block_ref, index, planes, rows):
    for at, y in enumerate((0, 1, N - 2, N - 1)):
        block_ref[(*index, pl.ds(y, STEP, stride=N), slice(None))] = rows(at)

    @pl.when(step == 0)
    def _():
        block_ref[(*index, slice(0, 2 * N), slice(None))] = planes(0)

    @pl.when(step == N // STEP - 1)
    def _():
        block_ref[(*index, slice(BLOCK - 2 * N, BLOCK), slice(None))] = planes(2 * N)


def field_kernel(w_ref, planes_ref, rows_ref, out_ref):
    step = pl.program_id(0)
    out_ref[...] = w_ref[0:6, pl.ds(pl.multiple_of(step * BLOCK, BLOCK), BLOCK), :]
    for f in range(6):
        put_boundary(
            step, out_ref, (f,),
            lambda at, f=f: planes_ref[f, at:at + 2 * N, :],
            lambda at, f=f: rows_ref[f, pl.ds(pl.multiple_of(at * N + step * STEP, 8), STEP), :],
        )


def gradient_kernel(mine_ref, other_ref, mine_b_ref, other_b_ref, ab_ref, sh_ref, sv_ref, gh_ref, gv_ref, total_ref):
    step = pl.program_id(0)
    odd_core = lax.rem(lax.axis_index("freq"), 2) == 1
    mask = (ab_ref[0, pl.ds(pl.multiple_of(step * BLOCK, BLOCK), BLOCK), :] > 0.0).astype(f32)
    for k, (sigma_ref, out_ref) in enumerate(((sh_ref, gh_ref), (sv_ref, gv_ref))):
        first = odd_core if k == 1 else jnp.logical_not(odd_core)
        total_ref[...] = jnp.where(first, mine_ref[...], other_ref[...])

        def boundary(rows):
            return jnp.where(first, mine_b_ref[rows, :], other_b_ref[rows, :])

        put_boundary(
            step, total_ref, (),
            lambda at: boundary(slice(at, at + 2 * N)),
            lambda at: boundary(pl.ds(pl.multiple_of((4 + at) * N + step * STEP, 8), STEP)),
        )
        out_ref[...] = sigma_ref[...] * mask * total_ref[...]


def swap_pairs(axis, odd):
    pairs_of = []
    for i in range(SUBS):
        at = [i % SX, i // SX]
        at[axis] += 1 if at[axis] % 2 == odd else -1
        if 0 <= at[axis] < SX:
            pairs_of.append((i, at[1] * SX + at[0]))
    return pairs_of


def swap(value, axis, odd):
    return lax.ppermute(value, "sub", swap_pairs(axis, odd))


def swap_freq(value, flip):
    return lax.ppermute(value, "freq", [(i, i ^ flip) for i in range(4)])


def sds(*shape):
    return jax.ShapeDtypeStruct(shape, f32)


def on_device(source, adjoint_source, sigma_h, sigma_v, seafloor, links, freq_index):
    steps = N // STEP
    src = source.reshape(6, CELLS, NZ)
    adj = adjoint_source.reshape(6, CELLS, NZ)
    cond_h = sigma_h.reshape(CELLS, NZ)
    cond_v = sigma_v.reshape(CELLS, NZ)
    floor = seafloor.reshape(N, N)

    def block3(size):
        return pl.BlockSpec((size, BLOCK, NZ), lambda i: (0, jnp.minimum(i, steps - 1), 0))

    block2 = pl.BlockSpec((BLOCK, NZ), lambda i: (jnp.minimum(i, steps - 1), 0))
    u, v, ab, px0, px1, py0, py1 = pl.pallas_call(
        first_kernel,
        grid=(steps + 1,),
        in_specs=[whole(pltpu.SMEM), whole(pltpu.SMEM), whole(), block3(6), block3(6), block2, block2],
        out_specs=[whole()] * 7,
        out_shape=[
            pltpu.VMEM((NF, ROWS, NZ), f32), pltpu.VMEM((NF, ROWS, NZ), f32), pltpu.VMEM((4, CELLS, NZ), f32),
            sds(X_ROWS, NZ), sds(X_ROWS, NZ), sds(Y_ROWS, NZ), sds(Y_ROWS, NZ),
        ],
        scratch_shapes=[pltpu.VMEM((2, CELLS, NZ), f32)]
        + [pltpu.VMEM((X_ROWS, NZ), f32)] * 2 + [pltpu.VMEM((Y_ROWS, NZ), f32)] * 2,
        compiler_params=params(1),
        cost_estimate=cost(30 * NF * CELLS * NZ, 7 * 2**20),
        name="first",
    )(freq_index, links, floor, src, adj, cond_h, cond_v)

    ry1 = swap(py1, 1, 1)
    ry0 = swap(py0, 1, 0)
    rx0 = swap(px0, 0, 0)
    rx1 = swap(px1, 0, 1)

    w, keep, send = pl.pallas_call(
        second_kernel,
        grid=(steps,),
        in_specs=[whole(pltpu.SMEM), whole(), whole(), whole()],
        out_specs=[whole(), block2, block2],
        out_shape=[pltpu.VMEM((NF, CELLS, NZ), f32), sds(CELLS, NZ), sds(CELLS, NZ)],
        compiler_params=params(1),
        cost_estimate=cost(20 * NF * CELLS * NZ, 20 * 2**20),
        name="second",
    )(freq_index, u, v, ab)

    ty0, ty1 = pl.pallas_call(
        edge_kernel,
        in_specs=[whole(pltpu.SMEM)] + [whole()] * 3,
        out_specs=[whole()] * 2,
        out_shape=[sds(T_ROWS, NZ)] * 2,
        scratch_shapes=[pltpu.VMEM((T_ROWS, NZ), f32)] * 2,
        compiler_params=params(),
        cost_estimate=cost(10**5, 2**20),
        name="edges",
    )(links, ab, rx0, rx1)
    rt1 = swap(ty1, 1, 1)
    rt0 = swap(ty0, 1, 0)

    mine = keep + swap_freq(send, 1)
    mine = mine + swap_freq(mine, 2)
    other = swap_freq(mine, 1)

    planes, rows, keep_b, send_b = pl.pallas_call(
        boundary_kernel,
        in_specs=[whole(pltpu.SMEM)] * 2 + [whole()] * 9,
        out_specs=[whole()] * 4,
        out_shape=[pltpu.VMEM((NF, 4 * N, NZ), f32)] * 2 + [sds(8 * N, NZ)] * 2,
        compiler_params=params(),
        cost_estimate=cost(10**7, 4 * 2**20),
        name="boundary",
    )(freq_index, links, u, ab, w, rx0, rx1, ry0, ry1, rt0, rt1)

    mine_b = keep_b + swap_freq(send_b, 1)
    mine_b = mine_b + swap_freq(mine_b, 2)
    other_b = swap_freq(mine_b, 1)

    forward = pl.pallas_call(
        field_kernel,
        grid=(steps,),
        in_specs=[whole()] * 3,
        out_specs=block3(6),
        out_shape=sds(6, CELLS, NZ),
        compiler_params=params(1),
        cost_estimate=cost(10**6, 6 * 2**20),
        name="field",
    )(w, planes, rows)

    grad_h, grad_v = pl.pallas_call(
        gradient_kernel,
        grid=(steps,),
        in_specs=[block2, block2, whole(), whole(), whole(), block2, block2],
        out_specs=[block2, block2],
        out_shape=[sds(CELLS, NZ)] * 2,
        scratch_shapes=[pltpu.VMEM((BLOCK, NZ), f32)],
        compiler_params=params(1),
        cost_estimate=cost(10**6, 4 * 2**20),
        name="gradient",
    )(mine, other, mine_b, other_b, ab, cond_h, cond_v)

    return (
        forward.reshape(1, 1, 2, 3, N, N, NZ),
        grad_h.reshape(1, N, N, NZ),
        grad_v.reshape(1, N, N, NZ),
    )


def solution(mesh):
    return jax.shard_map(
        on_device,
        mesh=mesh,
        in_specs=(
            P("sub", None, None, None, None, None),
            P("freq", "sub", None, None, None, None, None),
            P("sub", None, None, None),
            P("sub", None, None, None),
            P("sub", None, None),
            P("sub", None),
            P("freq"),
        ),
        out_specs=(
            P("freq", "sub", None, None, None, None, None),
            P("sub", None, None, None),
            P("sub", None, None, None),
        ),
        check_vma=False,
    )
```

time: 212 us -> 91.6 us (0.43)
  waiting for transfers between devices: 73.5 us -> 24.8 us
  other arithmetic: 43.3 us -> 0.16 us
  starting transfers between devices: 62.5 us -> 25.5 us
  Pallas kernels: 0 us -> 29.9 us
  between operations: 15.5 us -> 1.4 us
  local copies, waits for them, and re-layouts: 15.2 us -> 8.58 us
    psum x1 -> x0, waiting for transfers between devices: 59.4 us -> none  [on_device(): total_h, total_v = lax.psum((term_h, term_v), 'freq')]
    ppermute x16 -> x12, starting transfers between devices: 62.4 us -> 25.5 us  [the longest x6 15.3 us: swap(): return lax.ppermute(value, 'sub', swap_pairs(axis, odd))]
    pallas_call x0 -> x6, Pallas kernels: none -> 29.9 us  [the longest x1 12.1 us: on_device(): pl.pallas_call(first_kernel, grid=(steps + 1,), in_specs=[whole(pltpu.SME...]
    add x5 -> x4, other arithmetic: 14.4 us -> 0.16 us  [the longest x1 0.08 us: on_device(): mine = keep + swap_freq(send, 1)]
    mul x13 -> x0, other arithmetic: 10.9 us -> none  [the longest x6 6.18 us: update(): jnp.stack([new_real, new_imag], axis=-5) * mask[..., None, None, :, :, :]]
    ppermute x16 -> x12, waiting for transfers between devices: 14 us -> 24.8 us  [the longest x6 17.5 us: swap(): return lax.ppermute(value, 'sub', swap_pairs(axis, odd))]
    div x6 -> x0, other arithmetic: 8.51 us -> none  [update(): new_real = (6.0 * real_part + shift3 * imag_part) / denom]
    broadcast_in_dim x11 -> x0, other arithmetic: 8.36 us -> none  [the longest x4 2.62 us: stencil_sum(): ghost_lo_y[..., :, None, :]]
  transfers between devices with their start and end apart: 17 -> 12, of which waited for: 5 -> 7; matrix products, arithmetic and copies ran while one was open for 7% -> 0% of each run, Pallas kernels for 0% -> 7%
where the time goes in v1:
time: 91.6 us; the launch traced here: 90.3 us
  Pallas kernels  29.9 us (33%)
  starting transfers between devices  25.5 us (28%)
  waiting for transfers between devices  24.8 us (27%)
  local copies, waits for them, and re-layouts  8.58 us (9%)
  between operations  1.4 us (2%)
    ppermute x6, waiting for transfers between devices, swap(): return lax.ppermute(value, 'sub', swap_pairs(axis, odd))  17.5 us
    ppermute x6, starting transfers between devices, swap(): return lax.ppermute(value, 'sub', swap_pairs(axis, odd))  15.3 us
    pallas_call x1, Pallas kernels, on_device(): pl.pallas_call(first_kernel, grid=(steps + 1,), in_specs=[whole(pltpu.SME...  12.1 us
    ppermute x6, starting transfers between devices, swap_freq(): return lax.ppermute(value, 'freq', [(i, i ^ flip) for i in range(4)])  10.1 us
    pallas_call x1, Pallas kernels, on_device(): pl.pallas_call(second_kernel, grid=(steps,), in_specs=[whole(pltpu.SMEM),...  9.78 us
    unnamed x16, local copies, waits for them, and re-layouts  8.58 us
    ppermute x6, waiting for transfers between devices, swap_freq(): return lax.ppermute(value, 'freq', [(i, i ^ flip) for i in range(4)])  7.24 us
    pallas_call x1, Pallas kernels, on_device(): pl.pallas_call(boundary_kernel, in_specs=[whole(pltpu.SMEM)] * 2 + [whole...  3.2 us
  transfers between devices with their start and end apart: 12, of which 7 were waited for; matrix products, arithmetic and copies ran while one was open for 0% of the time, Pallas kernels for 7%

profile of v1, /device:TPU:71, one launch (start us, length us, event | category | flops | bytes accessed | tf_op | source)
XLA Modules:
  0.0 90.3 jit_solution(5510365575088595414)
XLA Ops:
  1.3 0.0 copy-start.1
  1.3 1.9 %copy-done.1 = f32[1,2,3,32,32,128]{5,4,3,2,1,0:T(8,128)S(1)} copy-done((f32[1,2,3,32,32,128]{5,4,3,2,1,0:T(8,128)S(1)}, f32[1,2,3,32,32,128]{5,4,3,2,1,0:T(8,128)}, u32[]{:S(2)}) %copy-start.1) | copy-done | bytes 3145752
  3.2 0.0 copy-start.2
  3.2 1.0 %copy-done.2 = f32[1,32,32,128]{3,2,1,0:T(8,128)S(1)} copy-done((f32[1,32,32,128]{3,2,1,0:T(8,128)S(1)}, f32[1,32,32,128]{3,2,1,0:T(8,128)}, u32[]{:S(2)}) %copy-start.2) | copy-done | bytes 524312
  4.2 0.0 copy-start.4
  4.2 1.0 %copy-done.4 = f32[1,32,32,128]{3,2,1,0:T(8,128)S(1)} copy-done((f32[1,32,32,128]{3,2,1,0:T(8,128)S(1)}, f32[1,32,32,128]{3,2,1,0:T(8,128)}, u32[]{:S(2)}) %copy-start.4) | copy-done | bytes 524312
  5.3 0.0 copy-start.6
  5.3 0.7 copy-done.6
  6.0 0.0 copy-start.7
  6.0 0.7 copy-done.7
  6.6 12.1 %first.1 = (f32[12,1360,128]{2,1,0:T(8,128)S(1)}, f32[12,1360,128]{2,1,0:T(8,128)S(1)}, f32[4,1024,128]{2,1,0:T(8,128)S(1)}, f32[888,128]{1,0:T(8,128)S(1)}, f32...) custom-call(s32[1]{0:T(128)S(6)} %copy.10.freq_ref, s32[1,4]{1,0:T(1,128)S(1)} %copy-done.7, ...), custom_call_target="tpu_custom_call" | custom-call | flops 47185920 | bytes 7340032 | tf_op jit(solution)/shard_map/first/pallas_call | solution.py:447
  18.8 0.0 copy-start
  18.8 3.2 %copy-done = f32[12,1360,128]{2,1,0:T(8,128)} copy-done((f32[12,1360,128]{2,1,0:T(8,128)}, f32[12,1360,128]{2,1,0:T(8,128)S(1)}, u32[]{:S(2)}) %copy-start) | copy-done | bytes 8355864
  22.0 9.8 %second.1 = (f32[12,1024,128]{2,1,0:T(8,128)S(1)}, f32[1024,128]{1,0:T(8,128)S(1)}, f32[1024,128]{1,0:T(8,128)S(1)}) custom-call(s32[1]{0:T(128)S(6)} %copy.10.freq_ref, f32[12,1360,128]{2,1,0:T(8,128)S(1)} %get-tuple-element.21.u_ref, f32[12,1360,128]{2,1,0:T(8,128)} %copy-done, f32[4,1024,128]{2,1,0:T(8,128)S(1)} %get-tuple-element.23.ab_ref), custom_call_target="tpu_custom_call" | custom-call | flops 31457280 | bytes 20971520 | tf_op jit(solution)/shard_map/second/pallas_call | solution.py:468
  31.8 0.8 collective-permute-start.6
  32.6 1.5 %collective-permute-done.6 = f32[1024,128]{1,0:T(8,128)S(1)} collective-permute-done((f32[1024,128]{1,0:T(8,128)S(1)}, f32[1024,128]{1,0:T(8,128)S(1)}, u32[]{:S(2)}, u32[]{:S(2)}) %collective-permute-start.6) | collective-permute-done | bytes 524320 | tf_op jit(solution)/shard_map/ppermute | solution.py:428
  34.1 0.1 add.12
  34.2 1.7 %collective-permute-start.7 = (f32[1024,128]{1,0:T(8,128)S(1)}, f32[1024,128]{1,0:T(8,128)S(1)}, u32[]{:S(2)}, u32[]{:S(2)}) collective-permute-start(f32[1024,128]{1,0:T(8,128)S(1)} %add.12), channel_id=1, source_target_pairs={{0,2},{1,3},{2,0},{3,1},{4,6},{5,7},{6,4},{7,5},{8,10},{9,11},{10,... | collective-permute-start | bytes 1572872 | tf_op jit(solution)/shard_map/ppermute | solution.py:428
  35.9 1.3 %collective-permute-start = (f32[888,128]{1,0:T(8,128)S(1)}, f32[888,128]{1,0:T(8,128)S(1)}, u32[]{:S(2)}, u32[]{:S(2)}) collective-permute-start(f32[888,128]{1,0:T(8,128)S(1)} %get-tuple-element.25), channel_id=1, source_target_pairs={{0,4},{4,0},{8,12},{12,8},{16,20},{20,16},{24,28},{28,24},{32,36},... | collective-permute-start | bytes 1363976 | tf_op jit(solution)/shard_map/ppermute | solution.py:424
  37.2 4.1 %collective-permute-start.1 = (f32[888,128]{1,0:T(8,128)S(1)}, f32[888,128]{1,0:T(8,128)S(1)}, u32[]{:S(2)}, u32[]{:S(2)}) collective-permute-start(f32[888,128]{1,0:T(8,128)S(1)} %get-tuple-element.26), channel_id=1, source_target_pairs={{4,8},{8,4},{12,16},{16,12},{20,24},{24,20},{36,40},{40,36},{44,48... | collective-permute-start | bytes 1363976 | tf_op jit(solution)/shard_map/ppermute | solution.py:424
  41.3 0.9 %collective-permute-start.2 = (f32[832,128]{1,0:T(8,128)S(1)}, f32[832,128]{1,0:T(8,128)S(1)}, u32[]{:S(2)}, u32[]{:S(2)}) collective-permute-start(f32[832,128]{1,0:T(8,128)S(1)} %get-tuple-element.27), channel_id=1, source_target_pairs={{0,32},{4,36},{8,40},{12,44},{16,48},{20,52},{24,56},{28,60},{32,0... | collective-permute-start | bytes 1277960 | tf_op jit(solution)/shard_map/ppermute | solution.py:424
  42.2 7.1 %collective-permute-start.3 = (f32[832,128]{1,0:T(8,128)S(1)}, f32[832,128]{1,0:T(8,128)S(1)}, u32[]{:S(2)}, u32[]{:S(2)}) collective-permute-start(f32[832,128]{1,0:T(8,128)S(1)} %get-tuple-element.28), channel_id=1, source_target_pairs={{32,64},{36,68},{40,72},{44,76},{48,80},{52,84},{56,88},{60,92},{6... | collective-permute-start | bytes 1277960 | tf_op jit(solution)/shard_map/ppermute | solution.py:424
  49.3 0.0 collective-permute-done.7
  49.3 0.1 add.13.mine_ref
  49.3 1.9 %collective-permute-start.8 = (f32[1024,128]{1,0:T(8,128)S(1)}, f32[1024,128]{1,0:T(8,128)S(1)}, u32[]{:S(2)}, u32[]{:S(2)}) collective-permute-start(f32[1024,128]{1,0:T(8,128)S(1)} %add.13.mine_ref), channel_id=1, source_target_pairs={{0,1},{1,0},{2,3},{3,2},{4,5},{5,4},{6,7},{7,6},{8,9},{9,8},{10,11... | collective-permute-start | bytes 1572872 | tf_op jit(solution)/shard_map/ppermute | solution.py:428
  51.2 0.0 collective-permute-done.rx0_ref
  51.2 10.1 %collective-permute-done.1.rx1_ref = f32[888,128]{1,0:T(8,128)S(1)} collective-permute-done((f32[888,128]{1,0:T(8,128)S(1)}, f32[888,128]{1,0:T(8,128)S(1)}, u32[]{:S(2)}, u32[]{:S(2)}) %collective-permute-start.1) | collective-permute-done | bytes 454688 | tf_op jit(solution)/shard_map/ppermute | solution.py:424
  61.3 0.7 edges.1
  62.0 0.1 collective-permute-start.4
  62.1 1.9 %collective-permute-start.5 = (f32[72,128]{1,0:T(8,128)S(1)}, f32[72,128]{1,0:T(8,128)S(1)}, u32[]{:S(2)}, u32[]{:S(2)}) collective-permute-start(f32[72,128]{1,0:T(8,128)S(1)} %get-tuple-element.30), channel_id=1, source_target_pairs={{32,64},{36,68},{40,72},{44,76},{48,80},{52,84},{56,88},{60,92},{6... | collective-permute-start | bytes 110600 | tf_op jit(solution)/shard_map/ppermute | solution.py:424
  64.0 5.9 %collective-permute-done.2.ry0_ref = f32[832,128]{1,0:T(8,128)S(1)} collective-permute-done((f32[832,128]{1,0:T(8,128)S(1)}, f32[832,128]{1,0:T(8,128)S(1)}, u32[]{:S(2)}, u32[]{:S(2)}) %collective-permute-start.2) | collective-permute-done | bytes 426016 | tf_op jit(solution)/shard_map/ppermute | solution.py:424
  69.9 0.0 collective-permute-done.3.ry1_ref
  69.9 0.8 collective-permute-done.4.rt0_ref
  70.7 0.7 collective-permute-done.5.rt1_ref
  71.4 3.2 %boundary.1 = (f32[12,128,128]{2,1,0:T(8,128)S(1)}, f32[12,128,128]{2,1,0:T(8,128)S(1)}, f32[256,128]{1,0:T(8,128)S(1)}, f32[256,128]{1,0:T(8,128)S(1)}) custom-call(s32[1]{0:T(128)S(6)} %copy.10.freq_ref, s32[1,4]{1,0:T(1,128)S(1)} %copy-done.7, f32[12,1360,128]{2,1,0:T(8,128)S(1)} %get-tuple-element.21.u_ref, ...), custom_call_target="tpu_custom_call" | custom-call | flops 10000000 | bytes 4194304 | tf_op jit(solution)/shard_map/boundary/pallas_call | solution.py:496
  74.6 4.4 %collective-permute-start.9 = (f32[256,128]{1,0:T(8,128)S(1)}, f32[256,128]{1,0:T(8,128)S(1)}, u32[]{:S(2)}, u32[]{:S(2)}) collective-permute-start(f32[256,128]{1,0:T(8,128)S(1)} %get-tuple-element.36), channel_id=1, source_target_pairs={{0,1},{1,0},{2,3},{3,2},{4,5},{5,4},{6,7},{7,6},{8,9},{9,8},{10,11... | collective-permute-start | bytes 393224 | tf_op jit(solution)/shard_map/ppermute | solution.py:428
  79.0 1.0 %collective-permute-done.9 = f32[256,128]{1,0:T(8,128)S(1)} collective-permute-done((f32[256,128]{1,0:T(8,128)S(1)}, f32[256,128]{1,0:T(8,128)S(1)}, u32[]{:S(2)}, u32[]{:S(2)}) %collective-permute-start.9) | collective-permute-done | bytes 131104 | tf_op jit(solution)/shard_map/ppermute | solution.py:428
  80.1 0.1 collective-permute-start.10
  80.2 4.7 %collective-permute-done.10 = f32[256,128]{1,0:T(8,128)S(1)} collective-permute-done((f32[256,128]{1,0:T(8,128)S(1)}, f32[256,128]{1,0:T(8,128)S(1)}, u32[]{:S(2)}, u32[]{:S(2)}) %collective-permute-start.10) | collective-permute-done | bytes 131104 | tf_op jit(solution)/shard_map/ppermute | solution.py:428
  84.9 1.3 %collective-permute-start.11 = (f32[256,128]{1,0:T(8,128)S(1)}, f32[256,128]{1,0:T(8,128)S(1)}, u32[]{:S(2)}, u32[]{:S(2)}) collective-permute-start(f32[256,128]{1,0:T(8,128)S(1)} %add.15.mine_b_ref), channel_id=1, source_target_pairs={{0,1},{1,0},{2,3},{3,2},{4,5},{5,4},{6,7},{7,6},{8,9},{9,8},{10,11... | collective-permute-start | bytes 393224 | tf_op jit(solution)/shard_map/ppermute | solution.py:428
  86.2 0.0 copy-start.3
  86.2 0.0 copy-start.5
  86.2 2.3 %field.1 = f32[6,1024,128]{2,1,0:T(8,128)} custom-call(f32[12,1024,128]{2,1,0:T(8,128)S(1)} %get-tuple-element.24.w_ref, f32[12,128,128]{2,1,0:T(8,128)S(1)} %get-tuple-element.31.planes_ref, f32[12,128,128]{2,1,0:T(8,128)S(1)} %get-tuple-element.32.rows_ref), custom_call_target="tpu_custom_call" | custom-call | flops 1000000 | bytes 6291456 | tf_op jit(solution)/shard_map/field/pallas_call | solution.py:510
  88.5 0.0 collective-permute-done.11.other_b_ref
  88.5 0.0 collective-permute-done.8.other_ref
  88.5 0.0 copy-done.3
  88.5 0.0 copy-done.5
  88.5 1.8 %gradient.1 = (f32[1024,128]{1,0:T(8,128)}, f32[1024,128]{1,0:T(8,128)}) custom-call(f32[1024,128]{1,0:T(8,128)S(1)} %add.13.mine_ref, f32[1024,128]{1,0:T(8,128)S(1)} %collective-permute-done.8.other_ref, f32[256,128]{1,0:T(8,128)S(1)} %add.15.mine_b_ref, f32[256,128]{1,0:T(8,128)S(1)} %collective-permute-done.11.other_b_ref, ...), custom_call_target="tpu_custom_call" | custom-call | flops 1000000 | bytes 4194304 | tf_op jit(solution)/shard_map/gradient/pallas_call | solution.py:521
  (2 shorter events, 0.0 us)
Async XLA Ops:
  1.3 1.9 %copy-start.1 = (f32[1,2,3,32,32,128]{5,4,3,2,1,0:T(8,128)S(1)}, f32[1,2,3,32,32,128]{5,4,3,2,1,0:T(8,128)}, u32[]{:S(2)}) copy-start(f32[1,2,3,32,32,128]{5,4,3,2,1,0:T(8,128)} %param.7) | copy-start | bytes 9437188
  3.2 1.0 %copy-start.2 = (f32[1,32,32,128]{3,2,1,0:T(8,128)S(1)}, f32[1,32,32,128]{3,2,1,0:T(8,128)}, u32[]{:S(2)}) copy-start(f32[1,32,32,128]{3,2,1,0:T(8,128)} %param.9) | copy-start | bytes 1572868
  4.2 1.0 %copy-start.4 = (f32[1,32,32,128]{3,2,1,0:T(8,128)S(1)}, f32[1,32,32,128]{3,2,1,0:T(8,128)}, u32[]{:S(2)}) copy-start(f32[1,32,32,128]{3,2,1,0:T(8,128)} %param.10) | copy-start | bytes 1572868
  5.3 0.7 copy-start.6
  6.0 0.7 copy-start.7
  18.8 3.2 %copy-start = (f32[12,1360,128]{2,1,0:T(8,128)}, f32[12,1360,128]{2,1,0:T(8,128)S(1)}, u32[]{:S(2)}) copy-start(f32[12,1360,128]{2,1,0:T(8,128)S(1)} %get-tuple-element.22.v_ref) | copy-start | bytes 25067524
  31.8 2.3 %collective-permute-start.6 = (f32[1024,128]{1,0:T(8,128)S(1)}, f32[1024,128]{1,0:T(8,128)S(1)}, u32[]{:S(2)}, u32[]{:S(2)}) collective-permute-start(f32[1024,128]{1,0:T(8,128)S(1)} %get-tuple-element.34), channel_id=1, source_target_pairs={{0,1},{1,0},{2,3},{3,2},{4,5},{5,4},{6,7},{7,6},{8,9},{9,8},{10,11... | collective-permute-start | bytes 1572872 | tf_op jit(solution)/shard_map/ppermute | solution.py:428
  34.2 15.1 %collective-permute-start.7 = (f32[1024,128]{1,0:T(8,128)S(1)}, f32[1024,128]{1,0:T(8,128)S(1)}, u32[]{:S(2)}, u32[]{:S(2)}) collective-permute-start(f32[1024,128]{1,0:T(8,128)S(1)} %add.12), channel_id=1, source_target_pairs={{0,2},{1,3},{2,0},{3,1},{4,6},{5,7},{6,4},{7,5},{8,10},{9,11},{10,... | collective-permute-start | bytes 1572872 | tf_op jit(solution)/shard_map/ppermute | solution.py:428
  35.9 15.3 %collective-permute-start = (f32[888,128]{1,0:T(8,128)S(1)}, f32[888,128]{1,0:T(8,128)S(1)}, u32[]{:S(2)}, u32[]{:S(2)}) collective-permute-start(f32[888,128]{1,0:T(8,128)S(1)} %get-tuple-element.25), channel_id=1, source_target_pairs={{0,4},{4,0},{8,12},{12,8},{16,20},{20,16},{24,28},{28,24},{32,36},... | collective-permute-start | bytes 1363976 | tf_op jit(solution)/shard_map/ppermute | solution.py:424
  37.2 24.1 %collective-permute-start.1 = (f32[888,128]{1,0:T(8,128)S(1)}, f32[888,128]{1,0:T(8,128)S(1)}, u32[]{:S(2)}, u32[]{:S(2)}) collective-permute-start(f32[888,128]{1,0:T(8,128)S(1)} %get-tuple-element.26), channel_id=1, source_target_pairs={{4,8},{8,4},{12,16},{16,12},{20,24},{24,20},{36,40},{40,36},{44,48... | collective-permute-start | bytes 1363976 | tf_op jit(solution)/shard_map/ppermute | solution.py:424
  41.3 28.6 %collective-permute-start.2 = (f32[832,128]{1,0:T(8,128)S(1)}, f32[832,128]{1,0:T(8,128)S(1)}, u32[]{:S(2)}, u32[]{:S(2)}) collective-permute-start(f32[832,128]{1,0:T(8,128)S(1)} %get-tuple-element.27), channel_id=1, source_target_pairs={{0,32},{4,36},{8,40},{12,44},{16,48},{20,52},{24,56},{28,60},{32,0... | collective-permute-start | bytes 1277960 | tf_op jit(solution)/shard_map/ppermute | solution.py:424
  42.2 27.7 %collective-permute-start.3 = (f32[832,128]{1,0:T(8,128)S(1)}, f32[832,128]{1,0:T(8,128)S(1)}, u32[]{:S(2)}, u32[]{:S(2)}) collective-permute-start(f32[832,128]{1,0:T(8,128)S(1)} %get-tuple-element.28), channel_id=1, source_target_pairs={{32,64},{36,68},{40,72},{44,76},{48,80},{52,84},{56,88},{60,92},{6... | collective-permute-start | bytes 1277960 | tf_op jit(solution)/shard_map/ppermute | solution.py:424
  49.3 39.1 %collective-permute-start.8 = (f32[1024,128]{1,0:T(8,128)S(1)}, f32[1024,128]{1,0:T(8,128)S(1)}, u32[]{:S(2)}, u32[]{:S(2)}) collective-permute-start(f32[1024,128]{1,0:T(8,128)S(1)} %add.13.mine_ref), channel_id=1, source_target_pairs={{0,1},{1,0},{2,3},{3,2},{4,5},{5,4},{6,7},{7,6},{8,9},{9,8},{10,11... | collective-permute-start | bytes 1572872 | tf_op jit(solution)/shard_map/ppermute | solution.py:428
  62.0 8.7 %collective-permute-start.4 = (f32[72,128]{1,0:T(8,128)S(1)}, f32[72,128]{1,0:T(8,128)S(1)}, u32[]{:S(2)}, u32[]{:S(2)}) collective-permute-start(f32[72,128]{1,0:T(8,128)S(1)} %get-tuple-element.29), channel_id=1, source_target_pairs={{0,32},{4,36},{8,40},{12,44},{16,48},{20,52},{24,56},{28,60},{32,0... | collective-permute-start | bytes 110600 | tf_op jit(solution)/shard_map/ppermute | solution.py:424
  62.1 9.3 %collective-permute-start.5 = (f32[72,128]{1,0:T(8,128)S(1)}, f32[72,128]{1,0:T(8,128)S(1)}, u32[]{:S(2)}, u32[]{:S(2)}) collective-permute-start(f32[72,128]{1,0:T(8,128)S(1)} %get-tuple-element.30), channel_id=1, source_target_pairs={{32,64},{36,68},{40,72},{44,76},{48,80},{52,84},{56,88},{60,92},{6... | collective-permute-start | bytes 110600 | tf_op jit(solution)/shard_map/ppermute | solution.py:424
  74.6 5.4 %collective-permute-start.9 = (f32[256,128]{1,0:T(8,128)S(1)}, f32[256,128]{1,0:T(8,128)S(1)}, u32[]{:S(2)}, u32[]{:S(2)}) collective-permute-start(f32[256,128]{1,0:T(8,128)S(1)} %get-tuple-element.36), channel_id=1, source_target_pairs={{0,1},{1,0},{2,3},{3,2},{4,5},{5,4},{6,7},{7,6},{8,9},{9,8},{10,11... | collective-permute-start | bytes 393224 | tf_op jit(solution)/shard_map/ppermute | solution.py:428
  80.1 4.8 %collective-permute-start.10 = (f32[256,128]{1,0:T(8,128)S(1)}, f32[256,128]{1,0:T(8,128)S(1)}, u32[]{:S(2)}, u32[]{:S(2)}) collective-permute-start(f32[256,128]{1,0:T(8,128)S(1)} %add.14), channel_id=1, source_target_pairs={{0,2},{1,3},{2,0},{3,1},{4,6},{5,7},{6,4},{7,5},{8,10},{9,11},{10,... | collective-permute-start | bytes 393224 | tf_op jit(solution)/shard_map/ppermute | solution.py:428
  84.9 3.6 %collective-permute-start.11 = (f32[256,128]{1,0:T(8,128)S(1)}, f32[256,128]{1,0:T(8,128)S(1)}, u32[]{:S(2)}, u32[]{:S(2)}) collective-permute-start(f32[256,128]{1,0:T(8,128)S(1)} %add.15.mine_b_ref), channel_id=1, source_target_pairs={{0,1},{1,0},{2,3},{3,2},{4,5},{5,4},{6,7},{7,6},{8,9},{9,8},{10,11... | collective-permute-start | bytes 393224 | tf_op jit(solution)/shard_map/ppermute | solution.py:428
  86.2 2.3 %copy-start.3 = (f32[1,32,32,128]{3,2,1,0:T(8,128)S(1)}, f32[1,32,32,128]{3,2,1,0:T(8,128)}, u32[]{:S(2)}) copy-start(f32[1,32,32,128]{3,2,1,0:T(8,128)} %param.9) | copy-start | bytes 1572868
  86.2 2.3 %copy-start.5 = (f32[1,32,32,128]{3,2,1,0:T(8,128)S(1)}, f32[1,32,32,128]{3,2,1,0:T(8,128)}, u32[]{:S(2)}) copy-start(f32[1,32,32,128]{3,2,1,0:T(8,128)} %param.10) | copy-start | bytes 1572868

commit v2 on v1

--- a/solution.py
+++ b/solution.py
@@ -16,7 +16,7 @@
 CELLS = N * N
 NF = 12
 FACE = NF * N
-X_V, X_S, X_R, X_C, X_ROWS = FACE, 2 * FACE, 2 * FACE + 64, 2 * FACE + 112, 2 * FACE + 120
+X_S, X_R, X_C, X_ROWS = 2 * FACE, 2 * FACE + 64, 2 * FACE + 112, 2 * FACE + 120
 Y_ROWS = 2 * FACE + 64
 T_ROWS = 72
 
@@ -30,9 +30,12 @@
     return pl.BlockSpec(memory_space=space)
 
 
-def params(steps=0):
-    kind = {"dimension_semantics": ("arbitrary",)} if steps else {}
-    return pltpu.CompilerParams(vmem_limit_bytes=30 * 2**20, **kind)
+def params(mib):
+    return pltpu.CompilerParams(vmem_limit_bytes=mib * 2**20)
+
+
+def in_hbm(value):
+    return pltpu.with_memory_space_constraint(value, pltpu.HBM)
 
 
 def cost(flops, size):
@@ -45,6 +48,10 @@
 
 def scale_of(freq_ref):
     return OMEGA0 * jnp.left_shift(jnp.int32(1), freq_ref[0]).astype(f32)
+
+
+def link_of(links_ref, k):
+    return links_ref[0:1, k:k + 1].astype(f32)
 
 
 def lane_neighbours(u):
@@ -89,109 +96,93 @@
     return total + lane_neighbours(centre)
 
 
-def first_kernel(
-    freq_ref, links_ref, floor_ref, src_ref, adj_ref, sh_ref, sv_ref,
-    u_ref, v_ref, ab_ref, px0_ref, px1_ref, py0_ref, py1_ref,
-    shift_ref, xl_ref, xh_ref, yl_ref, yh_ref,
+def floor_column(floor_ref, x, first, size):
+    floor = floor_ref[pl.ds(x, 1), :].astype(f32)
+    row = lax.broadcasted_iota(jnp.int32, (size, N), 0) + first
+    col = lax.broadcasted_iota(jnp.int32, (size, N), 1)
+    return jnp.sum(jnp.where(row == col, floor, 0.0), axis=1, keepdims=True)
+
+
+def mask_of(column):
+    depth = lax.broadcasted_iota(jnp.int32, (column.shape[0], NZ), 1).astype(f32)
+    return (depth >= column).astype(f32)
+
+
+def parity():
+    sub = lax.axis_index("sub")
+    return lax.rem(sub, 2) == 1, lax.rem(lax.div(sub, SX), 2) == 1
+
+
+def face(out_ref, shift, field, keep=None):
+    ab = [[factors(value) for value in layer] for layer in shift]
+    for k in range(2):
+        out_ref[X_S + k * N:X_S + (k + 1) * N, :] = shift[0][k]
+    for fr, fi, k in pairs():
+        u = [times(ab[l][k], field(fr, l), field(fi, l)) for l in range(3)]
+        v = []
+        for l in range(2):
+            near = [u[l + 1][c] if l == 0 else u[0][c] + u[2][c] for c in range(2)]
+            total = [near[c] + row_neighbours(u[l][c]) + lane_neighbours(u[l][c]) for c in range(2)]
+            new = times(ab[l][k], *total)
+            v.append([u[l][c] + new[c] for c in range(2)])
+        for c, f in enumerate((fr, fi)):
+            out_ref[f * N:(f + 1) * N, :] = trace(u[0][c], u[1][c])
+            out_ref[FACE + f * N:FACE + (f + 1) * N, :] = trace(v[0][c], v[1][c])
+            if keep is not None:
+                keep(f, u[0][c], u[1][c])
+
+
+def strip_kernel(
+    freq_ref, links_ref, floor_ref,
+    srcx_ref, adjx_ref, shx_ref, svx_ref, srcy_ref, adjy_ref, shy_ref, svy_ref,
+    px0_ref, px1_ref, py0_ref, py1_ref, xl_ref, xh_ref, yl_ref, yh_ref,
 ):
     step = pl.program_id(0)
     scale = scale_of(freq_ref)
+    odd_x, odd_y = parity()
+    fields = [ref.reshape(6, N * 8, NZ) for ref in (srcy_ref, adjy_ref)]
+    sigmas = [ref.reshape(N * 8, NZ) for ref in (shy_ref, svy_ref)]
+
+    def side(s, x_ref, y_ref):
+        def plane(l):
+            return slice((3 - l) * N, (4 - l) * N) if s else slice(l * N, (l + 1) * N)
+
+        def line(l):
+            return pl.ds(7 - l if s else l, N, stride=8)
+
+        def field_x(f, l):
+            return srcx_ref[f, plane(l), :] if f < 6 else adjx_ref[f - 6, plane(l), :]
+
+        def field_y(f, l):
+            return fields[f // 6][f % 6, line(l), :]
+
+        def relay(f, outer, inner):
+            for e in range(2):
+                for l, value in enumerate((outer, inner)):
+                    at = X_R + e * 24 + f * 2 + l
+                    row = [value[y:y + 1, :] for y in ((N - 1, N - 2) if e else (0, 1))]
+                    x_ref[at:at + 1, :] = link_of(links_ref, 2 + e) * trace(*row)
+
+        layers = [N - 1 - l if s else l for l in range(3)]
+        masks = [mask_of(floor_column(floor_ref, x, 0, N)) for x in layers]
+        shift = [[scale * ref[plane(l), :] * masks[l] for ref in (shx_ref, svx_ref)] for l in range(3)]
+        face(x_ref, shift, field_x, relay)
+        for end in range(2):
+            for k in range(2):
+                for l in range(2):
+                    at = X_C + end * 4 + k * 2 + l
+                    x_ref[at:at + 1, :] = shift[l][k][end * (N - 1):end * (N - 1) + 1, :]
+        masks = [mask_of(floor_ref[:, y:y + 1].astype(f32)) for y in layers]
+        shift = [[scale * ref[line(l), :] * masks[l] for ref in sigmas] for l in range(3)]
+        face(y_ref, shift, field_y)
 
     @pl.when(step == 0)
     def _():
-        zeros = jnp.zeros((PLANE, NZ), f32)
-        for f in range(NF):
-            for ref in (u_ref, v_ref):
-                ref[f, 0:PLANE, :] = zeros
-                ref[f, ROWS - PLANE:ROWS, :] = zeros
-
-    @pl.when(step < N // STEP)
-    def _():
-        def plane(j, carry):
-            x = step * STEP + j
-            here = pl.ds(pl.multiple_of(j * N, N), N)
-            there = pl.ds(pl.multiple_of(x * N, N), N)
-            start = pl.multiple_of(base(x), 8)
-            floor = floor_ref[pl.ds(x, 1), :].astype(f32)
-            row = lax.broadcasted_iota(jnp.int32, (N, N), 0)
-            col = lax.broadcasted_iota(jnp.int32, (N, N), 1)
-            column = jnp.sum(jnp.where(row == col, floor, 0.0), axis=1, keepdims=True)
-            depth = lax.broadcasted_iota(jnp.int32, (N, NZ), 1).astype(f32)
-            mask = (depth >= column).astype(f32)
-            ab = []
-            for k, ref in enumerate((sh_ref, sv_ref)):
-                shift = scale * ref[here, :] * mask
-                shift_ref[k, there, :] = shift
-                ab.append(factors(shift))
-                ab_ref[2 * k, there, :] = ab[k][0]
-                ab_ref[2 * k + 1, there, :] = ab[k][1]
-            zeros = jnp.zeros((8, NZ), f32)
-            for fr, fi, k in pairs():
-                ref, g = (src_ref, 0) if fr < 6 else (adj_ref, 6)
-                re, im = times(ab[k], ref[fr - g, here, :], ref[fi - g, here, :])
-                for f, value in ((fr, re), (fi, im)):
-                    u_ref[f, pl.ds(start, N), :] = value
-                    u_ref[f, pl.ds(start + N, 8), :] = zeros
-                    v_ref[f, pl.ds(start + N, 8), :] = zeros
-            return carry
-
-        lax.fori_loop(0, STEP, plane, 0)
-
-    @pl.when(step > 0)
-    def _():
-        def plane(j, carry):
-            x = (step - 1) * STEP + j
-            there = pl.ds(pl.multiple_of(x * N, N), N)
-            start = pl.multiple_of(base(x), 8)
-            ab = [(ab_ref[2 * k, there, :], ab_ref[2 * k + 1, there, :]) for k in range(2)]
-            for fr, fi, k in pairs():
-                re, im = times(ab[k], stencil(u_ref, fr, x), stencil(u_ref, fi, x))
-                v_ref[fr, pl.ds(start, N), :] = u_ref[fr, pl.ds(start, N), :] + re
-                v_ref[fi, pl.ds(start, N), :] = u_ref[fi, pl.ds(start, N), :] + im
-            return carry
-
-        lax.fori_loop(0, STEP, plane, 0)
-
-    @pl.when(step == N // STEP)
-    def _():
-        link_y = [links_ref[0, 2].astype(f32), links_ref[0, 3].astype(f32)]
-
-        def field(f, carry):
-            for ref, at in ((u_ref, 0), (v_ref, FACE)):
-                out = pl.ds(pl.multiple_of(at + f * N, N), N)
-                layer = [ref[f, pl.ds(base(x), N), :] for x in (0, 1, N - 2, N - 1)]
-                xl_ref[out, :] = trace(layer[0], layer[1])
-                xh_ref[out, :] = trace(layer[3], layer[2])
-                for b in range(N // 8):
-                    out = pl.ds(pl.multiple_of(at + f * N + b * 8, 8), 8)
-                    layer = [ref[f, pl.ds(base(b * 8) + y, 8, stride=PLANE), :] for y in (0, 1, N - 2, N - 1)]
-                    yl_ref[out, :] = trace(layer[0], layer[1])
-                    yh_ref[out, :] = trace(layer[3], layer[2])
-            return carry
-
-        lax.fori_loop(0, NF, field, 0)
-        for k in range(2):
-            out = slice(X_S + k * N, X_S + (k + 1) * N)
-            xl_ref[out, :] = shift_ref[k, 0:N, :]
-            xh_ref[out, :] = shift_ref[k, CELLS - N:CELLS, :]
-            yl_ref[out, :] = shift_ref[k, pl.ds(0, N, stride=N), :]
-            yh_ref[out, :] = shift_ref[k, pl.ds(N - 1, N, stride=N), :]
-        for e, y_ref in enumerate((yl_ref, yh_ref)):
-            for f in range(NF):
-                at = X_R + e * 24 + f * 2
-                xl_ref[at:at + 2, :] = y_ref[f * N:f * N + 2, :] * link_y[e]
-                xh_ref[at:at + 2, :] = y_ref[f * N + 30:f * N + 32, :] * link_y[e]
-            for k in range(2):
-                for layer in range(2):
-                    at = X_C + e * 4 + k * 2 + layer
-                    y = e * (N - 1)
-                    low = layer * N + y
-                    high = (N - 1 - layer) * N + y
-                    xl_ref[at:at + 1, :] = shift_ref[k, low:low + 1, :]
-                    xh_ref[at:at + 1, :] = shift_ref[k, high:high + 1, :]
-        sub = lax.axis_index("sub")
-        odd_x = lax.rem(sub, 2) == 1
-        odd_y = lax.rem(lax.div(sub, SX), 2) == 1
+        side(0, xl_ref, yl_ref)
+
+    @pl.when(step == 1)
+    def _():
+        side(1, xh_ref, yh_ref)
         low, high = xl_ref[...], xh_ref[...]
         px0_ref[...] = jnp.where(odd_x, low, high)
         px1_ref[...] = jnp.where(odd_x, high, low)
@@ -200,43 +191,8 @@
         py1_ref[...] = jnp.where(odd_y, high, low)
 
 
-def second_kernel(freq_ref, u_ref, v_ref, ab_ref, w_ref, keep_ref, send_ref):
-    step = pl.program_id(0)
-    scale = scale_of(freq_ref)
-    odd_core = lax.rem(lax.axis_index("freq"), 2) == 1
-
-    def plane(j, carry):
-        x = step * STEP + j
-        here = pl.ds(pl.multiple_of(j * N, N), N)
-        there = pl.ds(pl.multiple_of(x * N, N), N)
-        start = pl.multiple_of(base(x), 8)
-        ab = [(ab_ref[2 * k, there, :], ab_ref[2 * k + 1, there, :]) for k in range(2)]
-        term = [None, None]
-        for comp in range(3):
-            k = comp // 2
-            new = []
-            for solve in range(2):
-                fr, fi = solve * 6 + comp, solve * 6 + 3 + comp
-                re, im = times(ab[k], stencil(v_ref, fr, x), stencil(v_ref, fi, x))
-                re = re + u_ref[fr, pl.ds(start, N), :]
-                im = im + u_ref[fi, pl.ds(start, N), :]
-                w_ref[fr, there, :] = re
-                w_ref[fi, there, :] = im
-                new.append((re, im))
-            product = new[1][0] * new[0][1] + new[1][1] * new[0][0]
-            term[k] = product if term[k] is None else term[k] + product
-        term_h, term_v = scale * term[0], scale * term[1]
-        keep_ref[here, :] = jnp.where(odd_core, term_v, term_h)
-        send_ref[here, :] = jnp.where(odd_core, term_h, term_v)
-        return carry
-
-    lax.fori_loop(0, STEP, plane, 0)
-
-
 def edge_kernel(links_ref, ab_ref, rx0_ref, rx1_ref, ty0_ref, ty1_ref, tl_ref, th_ref):
-    sub = lax.axis_index("sub")
-    odd_x = lax.rem(sub, 2) == 1
-    odd_y = lax.rem(lax.div(sub, SX), 2) == 1
+    odd_x, odd_y = parity()
 
     def from_x(side, rows):
         first, second = rx0_ref[rows, :], rx1_ref[rows, :]
@@ -245,7 +201,7 @@
     for e, t_ref in enumerate((tl_ref, th_ref)):
         outer, inner = (0, 1) if e == 0 else (N - 1, N - 2)
         for side in range(2):
-            link = links_ref[0, side].astype(f32)
+            link = link_of(links_ref, side)
             x = side * (N - 1)
             for fr, fi, k in pairs():
                 layers = []
@@ -264,16 +220,98 @@
     ty1_ref[...] = jnp.where(odd_y, high, low)
 
 
+def solve_kernel(
+    freq_ref, floor_ref, src_ref, adj_ref, sh_ref, sv_ref,
+    u_ref, ab_ref, w_ref, keep_ref, send_ref, v_ref,
+):
+    step = pl.program_id(0)
+    scale = scale_of(freq_ref)
+    odd_core = lax.rem(lax.axis_index("freq"), 2) == 1
+
+    @pl.when(step == 0)
+    def _():
+        zeros = jnp.zeros((PLANE, NZ), f32)
+        for f in range(NF):
+            for ref in (u_ref, v_ref):
+                ref[f, 0:PLANE, :] = zeros
+                ref[f, ROWS - PLANE:ROWS, :] = zeros
+
+    @pl.when(step < N // STEP)
+    def _():
+        def plane(j, carry):
+            x = step * STEP + j
+            here = pl.ds(pl.multiple_of(j * N, N), N)
+            there = pl.ds(pl.multiple_of(x * N, N), N)
+            start = pl.multiple_of(base(x), 8)
+            mask = mask_of(floor_column(floor_ref, x, 0, N))
+            ab = []
+            for k, ref in enumerate((sh_ref, sv_ref)):
+                ab.append(factors(scale * ref[here, :] * mask))
+                ab_ref[2 * k, there, :] = ab[k][0]
+                ab_ref[2 * k + 1, there, :] = ab[k][1]
+            zeros = jnp.zeros((8, NZ), f32)
+            for fr, fi, k in pairs():
+                ref, g = (src_ref, 0) if fr < 6 else (adj_ref, 6)
+                re, im = times(ab[k], ref[fr - g, here, :], ref[fi - g, here, :])
+                for f, value in ((fr, re), (fi, im)):
+                    u_ref[f, pl.ds(start, N), :] = value
+                    u_ref[f, pl.ds(start + N, 8), :] = zeros
+                    v_ref[f, pl.ds(start + N, 8), :] = zeros
+            return carry
+
+        lax.fori_loop(0, STEP, plane, 0, unroll=4)
+
+    @pl.when(step > 0)
+    def _():
+        def plane(j, carry):
+            x = (step - 1) * STEP + j
+            there = pl.ds(pl.multiple_of(x * N, N), N)
+            start = pl.multiple_of(base(x), 8)
+            ab = [(ab_ref[2 * k, there, :], ab_ref[2 * k + 1, there, :]) for k in range(2)]
+            for fr, fi, k in pairs():
+                re, im = times(ab[k], stencil(u_ref, fr, x), stencil(u_ref, fi, x))
+                v_ref[fr, pl.ds(start, N), :] = u_ref[fr, pl.ds(start, N), :] + re
+                v_ref[fi, pl.ds(start, N), :] = u_ref[fi, pl.ds(start, N), :] + im
+            return carry
+
+        lax.fori_loop(0, STEP, plane, 0, unroll=4)
+
+    @pl.when(step == N // STEP)
+    def _():
+        def plane(x, carry):
+            there = pl.ds(pl.multiple_of(x * N, N), N)
+            start = pl.multiple_of(base(x), 8)
+            ab = [(ab_ref[2 * k, there, :], ab_ref[2 * k + 1, there, :]) for k in range(2)]
+            term = [None, None]
+            for comp in range(3):
+                k = comp // 2
+                new = []
+                for solve in range(2):
+                    fr, fi = solve * 6 + comp, solve * 6 + 3 + comp
+                    re, im = times(ab[k], stencil(v_ref, fr, x), stencil(v_ref, fi, x))
+                    re = re + u_ref[fr, pl.ds(start, N), :]
+                    im = im + u_ref[fi, pl.ds(start, N), :]
+                    w_ref[fr, there, :] = re
+                    w_ref[fi, there, :] = im
+                    new.append((re, im))
+                product = new[1][0] * new[0][1] + new[1][1] * new[0][0]
+                term[k] = product if term[k] is None else term[k] + product
+            term_h, term_v = scale * term[0], scale * term[1]
+            keep_ref[there, :] = jnp.where(odd_core, term_v, term_h)
+            send_ref[there, :] = jnp.where(odd_core, term_h, term_v)
+            return carry
+
+        lax.fori_loop(0, N, plane, 0, unroll=4)
+
+
 def boundary_kernel(
     freq_ref, links_ref, u_ref, ab_ref, w_ref, rx0_ref, rx1_ref, ry0_ref, ry1_ref, rt0_ref, rt1_ref,
     planes_ref, rows_ref, keep_ref, send_ref,
 ):
     scale = scale_of(freq_ref)
-    sub = lax.axis_index("sub")
-    odd_x = lax.rem(sub, 2) == 1
-    odd_y = lax.rem(lax.div(sub, SX), 2) == 1
+    odd_x, odd_y = parity()
     odd_core = lax.rem(lax.axis_index("freq"), 2) == 1
-    link = [links_ref[0, k].astype(f32) for k in range(4)]
+    link = [link_of(links_ref, k) for k in range(4)]
     row = lax.broadcasted_iota(jnp.int32, (N, NZ), 0)
 
     def pick(odd, side, first_ref, second_ref, rows):
@@ -329,8 +367,7 @@
             for e in range(2):
                 layers = []
                 for layer in range(2):
-                    col = layer if s == 1 else 1 - layer
-                    relay = [from_t(e, 24 + s * 24 + f * 2 + col, 1) for f in both]
+                    relay = [from_t(e, 24 + s * 24 + f * 2 + layer, 1) for f in both]
                     layers.append(times(corner[s][e][k][layer], *relay))
                 corners.append([trace(layers[0][c], layers[1][c]) for c in range(2)])
             rhs0, rhs1 = [], []
@@ -434,78 +471,85 @@
 
 def on_device(source, adjoint_source, sigma_h, sigma_v, seafloor, links, freq_index):
     steps = N // STEP
-    src = source.reshape(6, CELLS, NZ)
-    adj = adjoint_source.reshape(6, CELLS, NZ)
+    src = in_hbm(source.reshape(6, N, N, NZ))
+    adj = in_hbm(adjoint_source.reshape(6, N, N, NZ))
     cond_h = sigma_h.reshape(CELLS, NZ)
     cond_v = sigma_v.reshape(CELLS, NZ)
-    floor = seafloor.reshape(N, N)
+    cond_h4 = in_hbm(sigma_h.reshape(N, N, NZ))
+    cond_v4 = in_hbm(sigma_v.reshape(N, N, NZ))
+    floor = in_hbm(seafloor.reshape(N, N))
+    links = in_hbm(links)
+    smem = whole(pltpu.SMEM)
 
     def block3(size):
         return pl.BlockSpec((size, BLOCK, NZ), lambda i: (0, jnp.minimum(i, steps - 1), 0))
 
     block2 = pl.BlockSpec((BLOCK, NZ), lambda i: (jnp.minimum(i, steps - 1), 0))
-    u, v, ab, px0, px1, py0, py1 = pl.pallas_call(
-        first_kernel,
-        grid=(steps + 1,),
-        in_specs=[whole(pltpu.SMEM), whole(pltpu.SMEM), whole(), block3(6), block3(6), block2, block2],
-        out_specs=[whole()] * 7,
-        out_shape=[
-            pltpu.VMEM((NF, ROWS, NZ), f32), pltpu.VMEM((NF, ROWS, NZ), f32), pltpu.VMEM((4, CELLS, NZ), f32),
-            sds(X_ROWS, NZ), sds(X_ROWS, NZ), sds(Y_ROWS, NZ), sds(Y_ROWS, NZ),
-        ],
-        scratch_shapes=[pltpu.VMEM((2, CELLS, NZ), f32)]
-        + [pltpu.VMEM((X_ROWS, NZ), f32)] * 2 + [pltpu.VMEM((Y_ROWS, NZ), f32)] * 2,
-        compiler_params=params(1),
-        cost_estimate=cost(30 * NF * CELLS * NZ, 7 * 2**20),
-        name="first",
-    )(freq_index, links, floor, src, adj, cond_h, cond_v)
-
+
+    flat_src, flat_adj = in_hbm(source.reshape(6, CELLS, NZ)), in_hbm(adjoint_source.reshape(6, CELLS, NZ))
+    flat_h, flat_v = in_hbm(cond_h), in_hbm(cond_v)
+    last = N // 4 - 1
+    field_x = pl.BlockSpec((6, 4 * N, NZ), lambda i: (0, i * last, 0))
+    sigma_x = pl.BlockSpec((4 * N, NZ), lambda i: (i * last, 0))
+    field_y = pl.BlockSpec((6, N, 8, NZ), lambda i: (0, 0, i * (N // 8 - 1), 0))
+    sigma_y = pl.BlockSpec((N, 8, NZ), lambda i: (0, i * (N // 8 - 1), 0))
+    px0, px1, py0, py1 = pl.pallas_call(
+        strip_kernel,
+        grid=(2,),
+        in_specs=[smem] + [whole()] * 2 + [field_x, field_x, sigma_x, sigma_x, field_y, field_y, sigma_y, sigma_y],
+        out_specs=[whole()] * 4,
+        out_shape=[sds(X_ROWS, NZ), sds(X_ROWS, NZ), sds(Y_ROWS, NZ), sds(Y_ROWS, NZ)],
+        scratch_shapes=[pltpu.VMEM((X_ROWS, NZ), f32)] * 2 + [pltpu.VMEM((Y_ROWS, NZ), f32)] * 2,
+        compiler_params=params(14),
+        cost_estimate=cost(10**6, 12 * 2**20),
+        name="strips",
+    )(freq_index, links, floor, flat_src, flat_adj, flat_h, flat_v, src, adj, cond_h4, cond_v4)
     ry1 = swap(py1, 1, 1)
     ry0 = swap(py0, 1, 0)
+    rx1 = swap(px1, 0, 1)
     rx0 = swap(px0, 0, 0)
-    rx1 = swap(px1, 0, 1)
-
-    w, keep, send = pl.pallas_call(
-        second_kernel,
-        grid=(steps,),
-        in_specs=[whole(pltpu.SMEM), whole(), whole(), whole()],
-        out_specs=[whole(), block2, block2],
-        out_shape=[pltpu.VMEM((NF, CELLS, NZ), f32), sds(CELLS, NZ), sds(CELLS, NZ)],
-        compiler_params=params(1),
-        cost_estimate=cost(20 * NF * CELLS * NZ, 20 * 2**20),
-        name="second",
-    )(freq_index, u, v, ab)
+
+    u, ab, w, keep, send = pl.pallas_call(
+        solve_kernel,
+        grid=(steps + 1,),
+        in_specs=[smem, whole(), block3(6), block3(6), block2, block2],
+        out_specs=[whole()] * 5,
+        out_shape=[
+            pltpu.VMEM((NF, ROWS, NZ), f32), pltpu.VMEM((4, CELLS, NZ), f32), pltpu.VMEM((NF, CELLS, NZ), f32),
+            sds(CELLS, NZ), sds(CELLS, NZ),
+        ],
+        scratch_shapes=[pltpu.VMEM((NF, ROWS, NZ), f32)],
+        compiler_params=params(16),
+        cost_estimate=cost(60 * NF * CELLS * NZ, 40 * 2**20),
+        name="solve",
+    )(freq_index, floor, flat_src, flat_adj, flat_h, flat_v)
 
     ty0, ty1 = pl.pallas_call(
         edge_kernel,
-        in_specs=[whole(pltpu.SMEM)] + [whole()] * 3,
+        in_specs=[whole()] * 4,
         out_specs=[whole()] * 2,
         out_shape=[sds(T_ROWS, NZ)] * 2,
         scratch_shapes=[pltpu.VMEM((T_ROWS, NZ), f32)] * 2,
-        compiler_params=params(),
-        cost_estimate=cost(10**5, 2**20),
+        compiler_params=params(4),
+        cost_estimate=cost(10**5, 10**6),
         name="edges",
     )(links, ab, rx0, rx1)
     rt1 = swap(ty1, 1, 1)
     rt0 = swap(ty0, 1, 0)
 
+    send, ry0, ry1, rt0, rt1 = lax.optimization_barrier((send, ry0, ry1, rt0, rt1))
     mine = keep + swap_freq(send, 1)
-    mine = mine + swap_freq(mine, 2)
-    other = swap_freq(mine, 1)
+    partner = swap_freq(mine, 2)
 
     planes, rows, keep_b, send_b = pl.pallas_call(
         boundary_kernel,
-        in_specs=[whole(pltpu.SMEM)] * 2 + [whole()] * 9,
+        in_specs=[smem] + [whole()] * 10,
         out_specs=[whole()] * 4,
         out_shape=[pltpu.VMEM((NF, 4 * N, NZ), f32)] * 2 + [sds(8 * N, NZ)] * 2,
-        compiler_params=params(),
-        cost_estimate=cost(10**7, 4 * 2**20),
+        compiler_params=params(8),
+        cost_estimate=cost(10**6, 11 * 2**20),
         name="boundary",
     )(freq_index, links, u, ab, w, rx0, rx1, ry0, ry1, rt0, rt1)
-
-    mine_b = keep_b + swap_freq(send_b, 1)
-    mine_b = mine_b + swap_freq(mine_b, 2)
-    other_b = swap_freq(mine_b, 1)
 
     forward = pl.pallas_call(
         field_kernel,
@@ -513,10 +557,17 @@
         in_specs=[whole()] * 3,
         out_specs=block3(6),
         out_shape=sds(6, CELLS, NZ),
-        compiler_params=params(1),
+        compiler_params=params(6),
         cost_estimate=cost(10**6, 6 * 2**20),
         name="field",
     )(w, planes, rows)
+
+    mine_b = keep_b + swap_freq(send_b, 1)
+    partner_b, partner, forward = lax.optimization_barrier((swap_freq(mine_b, 2), partner, forward))
+    mine = mine + partner
+    mine_b = mine_b + partner_b
+    other = swap_freq(mine, 1)
+    other_b = swap_freq(mine_b, 1)
 
     grad_h, grad_v = pl.pallas_call(
         gradient_kernel,
@@ -525,7 +576,7 @@
         out_specs=[block2, block2],
         out_shape=[sds(CELLS, NZ)] * 2,
         scratch_shapes=[pltpu.VMEM((BLOCK, NZ), f32)],
-        compiler_params=params(1),
+        compiler_params=params(6),
         cost_estimate=cost(10**6, 4 * 2**20),
         name="gradient",
     )(mine, other, mine_b, other_b, ab, cond_h, cond_v)

time: 91.6 us -> 69.3 us (0.76); the launches traced: 90.3 us -> 69.1 us
  waiting for transfers between devices: 24.8 us -> 15 us
  local copies, waits for them, and re-layouts: 8.58 us -> 0.01 us
  Pallas kernels: 29.9 us -> 23.8 us
  starting transfers between devices: 25.5 us -> 28.7 us
    ppermute x6, waiting for transfers between devices: 17.5 us -> 3.39 us  [swap(): return lax.ppermute(value, 'sub', swap_pairs(axis, odd))]
    unnamed x16 -> x4, local copies, waits for them, and re-layouts: 8.58 us -> 0.01 us
    pallas_call x4, Pallas kernels: 25.8 us -> 19.7 us  [the longest x1 12.1 us: on_device(): pl.pallas_call(solve_kernel, grid=(steps + 1,), in_specs=[smem, whole(),...]
    ppermute x6, starting transfers between devices: 15.3 us -> 20.2 us  [swap(): return lax.ppermute(value, 'sub', swap_pairs(axis, odd))]
    ppermute x6, waiting for transfers between devices: 7.24 us -> 11.6 us  [swap_freq(): return lax.ppermute(value, 'freq', [(i, i ^ flip) for i in range(4)])]
    ppermute x6, starting transfers between devices: 10.1 us -> 8.51 us  [swap_freq(): return lax.ppermute(value, 'freq', [(i, i ^ flip) for i in range(4)])]
  transfers between devices with their start and end apart: 12 -> 12, of which waited for: 7 -> 7; matrix products, arithmetic and copies ran while one was open for 0% -> 0% of each run, Pallas kernels for 7% -> 27%
where the time goes in v2:
time: 69.3 us; the launch traced here: 69.1 us
  starting transfers between devices  28.7 us (41%)
  Pallas kernels  23.8 us (34%)
  waiting for transfers between devices  15 us (22%)
  between operations  1.39 us (2%)
    ppermute x6, starting transfers between devices, swap(): return lax.ppermute(value, 'sub', swap_pairs(axis, odd))  20.2 us
    pallas_call x1, Pallas kernels, on_device(): pl.pallas_call(solve_kernel, grid=(steps + 1,), in_specs=[smem, whole(),...  12.1 us
    ppermute x6, waiting for transfers between devices, swap_freq(): return lax.ppermute(value, 'freq', [(i, i ^ flip) for i in range(4)])  11.6 us
    ppermute x6, starting transfers between devices, swap_freq(): return lax.ppermute(value, 'freq', [(i, i ^ flip) for i in range(4)])  8.51 us
    pallas_call x1, Pallas kernels, on_device(): pl.pallas_call(strip_kernel, grid=(2,), in_specs=[smem] + [whole()] * 2 +...  3.67 us
    ppermute x6, waiting for transfers between devices, swap(): return lax.ppermute(value, 'sub', swap_pairs(axis, odd))  3.39 us
    pallas_call x1, Pallas kernels, on_device(): pl.pallas_call(boundary_kernel, in_specs=[smem] + [whole()] * 10, out_spe...  3.11 us
    pallas_call x1, Pallas kernels, on_device(): pl.pallas_call(field_kernel, grid=(steps,), in_specs=[whole()] * 3, out_s...  2.34 us
  transfers between devices with their start and end apart: 12, of which 7 were waited for; matrix products, arithmetic and copies ran while one was open for 0% of the time, Pallas kernels for 27%

profile of v2, /device:TPU:71, one launch (start us, length us, event | category | flops | bytes accessed | tf_op | source)
XLA Modules:
  0.0 69.1 jit_solution(14882864179411539466)
XLA Ops:
  1.3 3.7 %strips.1 = (f32[888,128]{1,0:T(8,128)S(1)}, f32[888,128]{1,0:T(8,128)S(1)}, f32[832,128]{1,0:T(8,128)S(1)}, f32[832,128]{1,0:T(8,128)S(1)}) custom-call(s32[1]{0:T(128)S(6)} %copy.10.freq_ref, s32[1,4]{1,0:T(1,128)} %links_ref.5, s32[32,32]{1,0:T(8,128)} %bitcast.27, f32[6,1024,128]{2,1,0:T(8,128)} %bitcast.20, f32[6,1024,128]{2,1,0:T(8,128)} %bitcast.23, ...), custom_call_target="tpu_custom_call" | custom-call | flops 1000000 | bytes 12582912 | tf_op jit(solution)/shard_map/strips/pallas_call | solution.py:496
  4.9 1.4 %collective-permute-start = (f32[888,128]{1,0:T(8,128)S(1)}, f32[888,128]{1,0:T(8,128)S(1)}, u32[]{:S(2)}, u32[]{:S(2)}) collective-permute-start(f32[888,128]{1,0:T(8,128)S(1)} %get-tuple-element.31), channel_id=1, source_target_pairs={{0,4},{4,0},{8,12},{12,8},{16,20},{20,16},{24,28},{28,24},{32,36},... | collective-permute-start | bytes 1363976 | tf_op jit(solution)/shard_map/ppermute | solution.py:461
  6.3 4.1 %collective-permute-start.1 = (f32[888,128]{1,0:T(8,128)S(1)}, f32[888,128]{1,0:T(8,128)S(1)}, u32[]{:S(2)}, u32[]{:S(2)}) collective-permute-start(f32[888,128]{1,0:T(8,128)S(1)} %get-tuple-element.32), channel_id=1, source_target_pairs={{4,8},{8,4},{12,16},{16,12},{20,24},{24,20},{36,40},{40,36},{44,48... | collective-permute-start | bytes 1363976 | tf_op jit(solution)/shard_map/ppermute | solution.py:461
  10.4 0.9 %collective-permute-start.2 = (f32[832,128]{1,0:T(8,128)S(1)}, f32[832,128]{1,0:T(8,128)S(1)}, u32[]{:S(2)}, u32[]{:S(2)}) collective-permute-start(f32[832,128]{1,0:T(8,128)S(1)} %get-tuple-element.34), channel_id=1, source_target_pairs={{0,32},{4,36},{8,40},{12,44},{16,48},{20,52},{24,56},{28,60},{32,0... | collective-permute-start | bytes 1277960 | tf_op jit(solution)/shard_map/ppermute | solution.py:461
  11.3 8.0 %collective-permute-start.3 = (f32[832,128]{1,0:T(8,128)S(1)}, f32[832,128]{1,0:T(8,128)S(1)}, u32[]{:S(2)}, u32[]{:S(2)}) collective-permute-start(f32[832,128]{1,0:T(8,128)S(1)} %get-tuple-element.35), channel_id=1, source_target_pairs={{32,64},{36,68},{40,72},{44,76},{48,80},{52,84},{56,88},{60,92},{6... | collective-permute-start | bytes 1277960 | tf_op jit(solution)/shard_map/ppermute | solution.py:461
  19.3 12.1 %solve.1 = (f32[12,1360,128]{2,1,0:T(8,128)S(1)}, f32[4,1024,128]{2,1,0:T(8,128)S(1)}, f32[12,1024,128]{2,1,0:T(8,128)S(1)}, f32[1024,128]{1,0:T(8,128)S(1)}, f32[1024,128]{1,0:T(8,128)S(1)}) custom-call(s32[1]{0:T(128)S(6)} %copy.10.freq_ref, s32[32,32]{1,0:T(8,128)} %bitcast.28, f32[6,1024,128]{2,1,0:T(8,128)} %bitcast.22, f32[6,1024,128]{2,1,0:T(8,128)} %bitcast.25, ...), custom_call_target="tpu_custom_call" | custom-call | flops 94371840 | bytes 41943040 | tf_op jit(solution)/shard_map/solve/pallas_call | solution.py:512
  31.4 0.0 collective-permute-done.rx0_ref
  31.4 0.0 collective-permute-done.1.rx1_ref
  31.4 0.8 %edges.1 = (f32[72,128]{1,0:T(8,128)S(1)}, f32[72,128]{1,0:T(8,128)S(1)}) custom-call(s32[1,4]{1,0:T(1,128)} %links_ref.5, f32[4,1024,128]{2,1,0:T(8,128)S(1)} %get-tuple-element.29.ab_ref, f32[888,128]{1,0:T(8,128)S(1)} %collective-permute-done.rx0_ref, f32[888,128]{1,0:T(8,128)S(1)} %collective-permute-done.1.rx1_ref), custom_call_target="tpu_custom_call" | custom-call | flops 100000 | bytes 1000000 | tf_op jit(solution)/shard_map/edges/pallas_call | solution.py:527
  32.2 0.1 collective-permute-start.4
  32.3 5.8 %collective-permute-start.5 = (f32[72,128]{1,0:T(8,128)S(1)}, f32[72,128]{1,0:T(8,128)S(1)}, u32[]{:S(2)}, u32[]{:S(2)}) collective-permute-start(f32[72,128]{1,0:T(8,128)S(1)} %get-tuple-element.37), channel_id=1, source_target_pairs={{32,64},{36,68},{40,72},{44,76},{48,80},{52,84},{56,88},{60,92},{6... | collective-permute-start | bytes 110600 | tf_op jit(solution)/shard_map/ppermute | solution.py:461
  38.2 0.8 %collective-permute-done.2.ry0_ref = f32[832,128]{1,0:T(8,128)S(1)} collective-permute-done((f32[832,128]{1,0:T(8,128)S(1)}, f32[832,128]{1,0:T(8,128)S(1)}, u32[]{:S(2)}, u32[]{:S(2)}) %collective-permute-start.2) | collective-permute-done | bytes 426016 | tf_op jit(solution)/shard_map/ppermute | solution.py:461
  39.0 0.0 collective-permute-done.3.ry1_ref
  39.0 0.8 %collective-permute-done.4.rt0_ref = f32[72,128]{1,0:T(8,128)S(1)} collective-permute-done((f32[72,128]{1,0:T(8,128)S(1)}, f32[72,128]{1,0:T(8,128)S(1)}, u32[]{:S(2)}, u32[]{:S(2)}) %collective-permute-start.4) | collective-permute-done | bytes 36896 | tf_op jit(solution)/shard_map/ppermute | solution.py:461
  39.8 1.8 %collective-permute-done.5.rt1_ref = f32[72,128]{1,0:T(8,128)S(1)} collective-permute-done((f32[72,128]{1,0:T(8,128)S(1)}, f32[72,128]{1,0:T(8,128)S(1)}, u32[]{:S(2)}, u32[]{:S(2)}) %collective-permute-start.5) | collective-permute-done | bytes 36896 | tf_op jit(solution)/shard_map/ppermute | solution.py:461
  41.6 3.5 %collective-permute-start.8 = (f32[1024,128]{1,0:T(8,128)S(1)}, f32[1024,128]{1,0:T(8,128)S(1)}, u32[]{:S(2)}, u32[]{:S(2)}) collective-permute-start(f32[1024,128]{1,0:T(8,128)S(1)} %get-tuple-element.45), channel_id=1, source_target_pairs={{0,1},{1,0},{2,3},{3,2},{4,5},{5,4},{6,7},{7,6},{8,9},{9,8},{10,11... | collective-permute-start | bytes 1572872 | tf_op jit(solution)/shard_map/ppermute | solution.py:465
  45.1 1.5 %collective-permute-done.8 = f32[1024,128]{1,0:T(8,128)S(1)} collective-permute-done((f32[1024,128]{1,0:T(8,128)S(1)}, f32[1024,128]{1,0:T(8,128)S(1)}, u32[]{:S(2)}, u32[]{:S(2)}) %collective-permute-start.8) | collective-permute-done | bytes 524320 | tf_op jit(solution)/shard_map/ppermute | solution.py:465
  46.6 0.1 add.13
  46.7 3.1 %collective-permute-start.9 = (f32[1024,128]{1,0:T(8,128)S(1)}, f32[1024,128]{1,0:T(8,128)S(1)}, u32[]{:S(2)}, u32[]{:S(2)}) collective-permute-start(f32[1024,128]{1,0:T(8,128)S(1)} %add.13), channel_id=1, source_target_pairs={{0,2},{1,3},{2,0},{3,1},{4,6},{5,7},{6,4},{7,5},{8,10},{9,11},{10,... | collective-permute-start | bytes 1572872 | tf_op jit(solution)/shard_map/ppermute | solution.py:465
  49.8 3.1 %boundary.1 = (f32[12,128,128]{2,1,0:T(8,128)S(1)}, f32[12,128,128]{2,1,0:T(8,128)S(1)}, f32[256,128]{1,0:T(8,128)S(1)}, f32[256,128]{1,0:T(8,128)S(1)}) custom-call(s32[1]{0:T(128)S(6)} %copy.10.freq_ref, s32[1,4]{1,0:T(1,128)} %links_ref.5, f32[12,1360,128]{2,1,0:T(8,128)S(1)} %get-tuple-element.28.u_ref, f32[4,1024,128]{2,1,0:T(8,128)S(1)} %get-tuple-element.29.ab_ref, ...), custom_call_target="tpu_custom_call" | custom-call | flops 1000000 | bytes 11534336 | tf_op jit(solution)/shard_map/boundary/pallas_call | solution.py:544
  52.9 0.7 %collective-permute-start.6 = (f32[256,128]{1,0:T(8,128)S(1)}, f32[256,128]{1,0:T(8,128)S(1)}, u32[]{:S(2)}, u32[]{:S(2)}) collective-permute-start(f32[256,128]{1,0:T(8,128)S(1)} %get-tuple-element.43), channel_id=1, source_target_pairs={{0,1},{1,0},{2,3},{3,2},{4,5},{5,4},{6,7},{7,6},{8,9},{9,8},{10,11... | collective-permute-start | bytes 393224 | tf_op jit(solution)/shard_map/ppermute | solution.py:465
  53.6 1.0 %collective-permute-done.6 = f32[256,128]{1,0:T(8,128)S(1)} collective-permute-done((f32[256,128]{1,0:T(8,128)S(1)}, f32[256,128]{1,0:T(8,128)S(1)}, u32[]{:S(2)}, u32[]{:S(2)}) %collective-permute-start.6) | collective-permute-done | bytes 131104 | tf_op jit(solution)/shard_map/ppermute | solution.py:465
  54.6 0.1 collective-permute-start.7
  54.7 0.0 copy-start
  54.7 0.0 copy-start.1
  54.7 2.3 %field.1 = f32[6,1024,128]{2,1,0:T(8,128)} custom-call(f32[12,1024,128]{2,1,0:T(8,128)S(1)} %get-tuple-element.30.w_ref, f32[12,128,128]{2,1,0:T(8,128)S(1)} %get-tuple-element.46.planes_ref, f32[12,128,128]{2,1,0:T(8,128)S(1)} %get-tuple-element.47.rows_ref), custom_call_target="tpu_custom_call" | custom-call | flops 1000000 | bytes 6291456 | tf_op jit(solution)/shard_map/field/pallas_call | solution.py:554
  57.1 7.5 %collective-permute-done.7 = f32[256,128]{1,0:T(8,128)S(1)} collective-permute-done((f32[256,128]{1,0:T(8,128)S(1)}, f32[256,128]{1,0:T(8,128)S(1)}, u32[]{:S(2)}, u32[]{:S(2)}) %collective-permute-start.7) | collective-permute-done | bytes 131104 | tf_op jit(solution)/shard_map/ppermute | solution.py:465
  64.6 0.0 collective-permute-done.9
  64.6 0.1 add.14.mine_ref
  64.6 1.0 %collective-permute-start.10 = (f32[1024,128]{1,0:T(8,128)S(1)}, f32[1024,128]{1,0:T(8,128)S(1)}, u32[]{:S(2)}, u32[]{:S(2)}) collective-permute-start(f32[1024,128]{1,0:T(8,128)S(1)} %add.14.mine_ref), channel_id=1, source_target_pairs={{0,1},{1,0},{2,3},{3,2},{4,5},{5,4},{6,7},{7,6},{8,9},{9,8},{10,11... | collective-permute-start | bytes 1572872 | tf_op jit(solution)/shard_map/ppermute | solution.py:465
  65.6 0.1 collective-permute-start.11
  65.7 1.6 %collective-permute-done.11.other_b_ref = f32[256,128]{1,0:T(8,128)S(1)} collective-permute-done((f32[256,128]{1,0:T(8,128)S(1)}, f32[256,128]{1,0:T(8,128)S(1)}, u32[]{:S(2)}, u32[]{:S(2)}) %collective-permute-start.11) | collective-permute-done | bytes 131104 | tf_op jit(solution)/shard_map/ppermute | solution.py:465
  67.3 0.0 collective-permute-done.10.other_ref
  67.3 0.0 copy-done
  67.3 0.0 copy-done.1
  67.3 1.8 %gradient.1 = (f32[1024,128]{1,0:T(8,128)}, f32[1024,128]{1,0:T(8,128)}) custom-call(f32[1024,128]{1,0:T(8,128)S(1)} %add.14.mine_ref, f32[1024,128]{1,0:T(8,128)S(1)} %collective-permute-done.10.other_ref, f32[256,128]{1,0:T(8,128)S(1)} %add.15.mine_b_ref, f32[256,128]{1,0:T(8,128)S(1)} %collective-permute-done.11.other_b_ref, ...), custom_call_target="tpu_custom_call" | custom-call | flops 1000000 | bytes 4194304 | tf_op jit(solution)/shard_map/gradient/pallas_call | solution.py:572
  (2 shorter events, 0.0 us)
Async XLA Ops:
  4.9 26.4 %collective-permute-start = (f32[888,128]{1,0:T(8,128)S(1)}, f32[888,128]{1,0:T(8,128)S(1)}, u32[]{:S(2)}, u32[]{:S(2)}) collective-permute-start(f32[888,128]{1,0:T(8,128)S(1)} %get-tuple-element.31), channel_id=1, source_target_pairs={{0,4},{4,0},{8,12},{12,8},{16,20},{20,16},{24,28},{28,24},{32,36},... | collective-permute-start | bytes 1363976 | tf_op jit(solution)/shard_map/ppermute | solution.py:461
  6.3 25.1 %collective-permute-start.1 = (f32[888,128]{1,0:T(8,128)S(1)}, f32[888,128]{1,0:T(8,128)S(1)}, u32[]{:S(2)}, u32[]{:S(2)}) collective-permute-start(f32[888,128]{1,0:T(8,128)S(1)} %get-tuple-element.32), channel_id=1, source_target_pairs={{4,8},{8,4},{12,16},{16,12},{20,24},{24,20},{36,40},{40,36},{44,48... | collective-permute-start | bytes 1363976 | tf_op jit(solution)/shard_map/ppermute | solution.py:461
  10.4 28.6 %collective-permute-start.2 = (f32[832,128]{1,0:T(8,128)S(1)}, f32[832,128]{1,0:T(8,128)S(1)}, u32[]{:S(2)}, u32[]{:S(2)}) collective-permute-start(f32[832,128]{1,0:T(8,128)S(1)} %get-tuple-element.34), channel_id=1, source_target_pairs={{0,32},{4,36},{8,40},{12,44},{16,48},{20,52},{24,56},{28,60},{32,0... | collective-permute-start | bytes 1277960 | tf_op jit(solution)/shard_map/ppermute | solution.py:461
  11.3 27.7 %collective-permute-start.3 = (f32[832,128]{1,0:T(8,128)S(1)}, f32[832,128]{1,0:T(8,128)S(1)}, u32[]{:S(2)}, u32[]{:S(2)}) collective-permute-start(f32[832,128]{1,0:T(8,128)S(1)} %get-tuple-element.35), channel_id=1, source_target_pairs={{32,64},{36,68},{40,72},{44,76},{48,80},{52,84},{56,88},{60,92},{6... | collective-permute-start | bytes 1277960 | tf_op jit(solution)/shard_map/ppermute | solution.py:461
  32.2 7.5 %collective-permute-start.4 = (f32[72,128]{1,0:T(8,128)S(1)}, f32[72,128]{1,0:T(8,128)S(1)}, u32[]{:S(2)}, u32[]{:S(2)}) collective-permute-start(f32[72,128]{1,0:T(8,128)S(1)} %get-tuple-element.36), channel_id=1, source_target_pairs={{0,32},{4,36},{8,40},{12,44},{16,48},{20,52},{24,56},{28,60},{32,0... | collective-permute-start | bytes 110600 | tf_op jit(solution)/shard_map/ppermute | solution.py:461
  32.3 9.2 %collective-permute-start.5 = (f32[72,128]{1,0:T(8,128)S(1)}, f32[72,128]{1,0:T(8,128)S(1)}, u32[]{:S(2)}, u32[]{:S(2)}) collective-permute-start(f32[72,128]{1,0:T(8,128)S(1)} %get-tuple-element.37), channel_id=1, source_target_pairs={{32,64},{36,68},{40,72},{44,76},{48,80},{52,84},{56,88},{60,92},{6... | collective-permute-start | bytes 110600 | tf_op jit(solution)/shard_map/ppermute | solution.py:461
  41.6 5.0 %collective-permute-start.8 = (f32[1024,128]{1,0:T(8,128)S(1)}, f32[1024,128]{1,0:T(8,128)S(1)}, u32[]{:S(2)}, u32[]{:S(2)}) collective-permute-start(f32[1024,128]{1,0:T(8,128)S(1)} %get-tuple-element.45), channel_id=1, source_target_pairs={{0,1},{1,0},{2,3},{3,2},{4,5},{5,4},{6,7},{7,6},{8,9},{9,8},{10,11... | collective-permute-start | bytes 1572872 | tf_op jit(solution)/shard_map/ppermute | solution.py:465
  46.7 17.9 %collective-permute-start.9 = (f32[1024,128]{1,0:T(8,128)S(1)}, f32[1024,128]{1,0:T(8,128)S(1)}, u32[]{:S(2)}, u32[]{:S(2)}) collective-permute-start(f32[1024,128]{1,0:T(8,128)S(1)} %add.13), channel_id=1, source_target_pairs={{0,2},{1,3},{2,0},{3,1},{4,6},{5,7},{6,4},{7,5},{8,10},{9,11},{10,... | collective-permute-start | bytes 1572872 | tf_op jit(solution)/shard_map/ppermute | solution.py:465
  52.9 1.7 %collective-permute-start.6 = (f32[256,128]{1,0:T(8,128)S(1)}, f32[256,128]{1,0:T(8,128)S(1)}, u32[]{:S(2)}, u32[]{:S(2)}) collective-permute-start(f32[256,128]{1,0:T(8,128)S(1)} %get-tuple-element.43), channel_id=1, source_target_pairs={{0,1},{1,0},{2,3},{3,2},{4,5},{5,4},{6,7},{7,6},{8,9},{9,8},{10,11... | collective-permute-start | bytes 393224 | tf_op jit(solution)/shard_map/ppermute | solution.py:465
  54.6 9.9 %collective-permute-start.7 = (f32[256,128]{1,0:T(8,128)S(1)}, f32[256,128]{1,0:T(8,128)S(1)}, u32[]{:S(2)}, u32[]{:S(2)}) collective-permute-start(f32[256,128]{1,0:T(8,128)S(1)} %add.12), channel_id=1, source_target_pairs={{0,2},{1,3},{2,0},{3,1},{4,6},{5,7},{6,4},{7,5},{8,10},{9,11},{10,... | collective-permute-start | bytes 393224 | tf_op jit(solution)/shard_map/ppermute | solution.py:465
  54.7 12.6 %copy-start = (f32[1,32,32,128]{3,2,1,0:T(8,128)S(1)}, f32[1,32,32,128]{3,2,1,0:T(8,128)}, u32[]{:S(2)}) copy-start(f32[1,32,32,128]{3,2,1,0:T(8,128)} %param.9) | copy-start | bytes 1572868
  54.7 12.6 %copy-start.1 = (f32[1,32,32,128]{3,2,1,0:T(8,128)S(1)}, f32[1,32,32,128]{3,2,1,0:T(8,128)}, u32[]{:S(2)}) copy-start(f32[1,32,32,128]{3,2,1,0:T(8,128)} %param.10) | copy-start | bytes 1572868
  64.6 2.7 %collective-permute-start.10 = (f32[1024,128]{1,0:T(8,128)S(1)}, f32[1024,128]{1,0:T(8,128)S(1)}, u32[]{:S(2)}, u32[]{:S(2)}) collective-permute-start(f32[1024,128]{1,0:T(8,128)S(1)} %add.14.mine_ref), channel_id=1, source_target_pairs={{0,1},{1,0},{2,3},{3,2},{4,5},{5,4},{6,7},{7,6},{8,9},{9,8},{10,11... | collective-permute-start | bytes 1572872 | tf_op jit(solution)/shard_map/ppermute | solution.py:465
  65.6 1.7 %collective-permute-start.11 = (f32[256,128]{1,0:T(8,128)S(1)}, f32[256,128]{1,0:T(8,128)S(1)}, u32[]{:S(2)}, u32[]{:S(2)}) collective-permute-start(f32[256,128]{1,0:T(8,128)S(1)} %add.15.mine_b_ref), channel_id=1, source_target_pairs={{0,1},{1,0},{2,3},{3,2},{4,5},{5,4},{6,7},{7,6},{8,9},{9,8},{10,11... | collective-permute-start | bytes 393224 | tf_op jit(solution)/shard_map/ppermute | solution.py:465

commit v3 on v2

--- a/solution.py
+++ b/solution.py
@@ -9,6 +9,8 @@
 SUBS = 64
 N = 32
 NZ = 128
+PIECES = (20, 8)
+INNER = N - 4
 PLANE = 40
 ROWS = 34 * PLANE
 STEP = 8
@@ -222,11 +224,13 @@
 
 def solve_kernel(
     freq_ref, floor_ref, src_ref, adj_ref, sh_ref, sv_ref,
-    u_ref, ab_ref, w_ref, keep_ref, send_ref, v_ref,
+    u_ref, ab_ref, w_ref, *refs,
 ):
     step = pl.program_id(0)
     scale = scale_of(freq_ref)
     odd_core = lax.rem(lax.axis_index("freq"), 2) == 1
+    count = len(PIECES)
+    keep_refs, send_refs, v_ref = refs[:count], refs[count:2 * count], refs[2 * count]
 
     @pl.when(step == 0)
     def _():
@@ -278,7 +282,7 @@
 
     @pl.when(step == N // STEP)
     def _():
-        def plane(x, carry):
+        def last_update(x):
             there = pl.ds(pl.multiple_of(x * N, N), N)
             start = pl.multiple_of(base(x), 8)
             ab = [(ab_ref[2 * k, there, :], ab_ref[2 * k + 1, there, :]) for k in range(2)]
@@ -296,12 +300,22 @@
                     new.append((re, im))
                 product = new[1][0] * new[0][1] + new[1][1] * new[0][0]
                 term[k] = product if term[k] is None else term[k] + product
-            term_h, term_v = scale * term[0], scale * term[1]
-            keep_ref[there, :] = jnp.where(odd_core, term_v, term_h)
-            send_ref[there, :] = jnp.where(odd_core, term_h, term_v)
-            return carry
-
-        lax.fori_loop(0, N, plane, 0, unroll=4)
+            return term
+
+        for x in (0, 1, N - 2, N - 1):
+            last_update(x)
+        first = 2
+        for size, keep_ref, send_ref in zip(PIECES, keep_refs, send_refs):
+            def plane(j, carry, first=first, keep_ref=keep_ref, send_ref=send_ref):
+                here = pl.ds(j * INNER, INNER)
+                term = last_update(first + j)
+                term_h, term_v = scale * term[0], scale * term[1]
+                keep_ref[here, :] = jnp.where(odd_core, term_v, term_h)[2:N - 2, :]
+                send_ref[here, :] = jnp.where(odd_core, term_h, term_v)[2:N - 2, :]
+                return carry
+
+            lax.fori_loop(0, size, plane, 0, unroll=2)
+            first += size
 
 
 def boundary_kernel(
@@ -434,7 +448,10 @@
     mask = (ab_ref[0, pl.ds(pl.multiple_of(step * BLOCK, BLOCK), BLOCK), :] > 0.0).astype(f32)
     for k, (sigma_ref, out_ref) in enumerate(((sh_ref, gh_ref), (sv_ref, gv_ref))):
         first = odd_core if k == 1 else jnp.logical_not(odd_core)
-        total_ref[...] = jnp.where(first, mine_ref[...], other_ref[...])
+        for j in range(STEP):
+            inner = jnp.clip(step * STEP + j - 2, 0, INNER - 1)
+            rows = pl.ds(inner * INNER, INNER)
+            total_ref[j * N + 2:(j + 1) * N - 2, :] = jnp.where(first, mine_ref[rows, :], other_ref[rows, :])
 
         def boundary(rows):
             return jnp.where(first, mine_b_ref[rows, :], other_b_ref[rows, :])
@@ -509,15 +526,14 @@
     rx1 = swap(px1, 0, 1)
     rx0 = swap(px0, 0, 0)
 
-    u, ab, w, keep, send = pl.pallas_call(
+    u, ab, w, *terms = pl.pallas_call(
         solve_kernel,
         grid=(steps + 1,),
         in_specs=[smem, whole(), block3(6), block3(6), block2, block2],
-        out_specs=[whole()] * 5,
+        out_specs=[whole()] * (3 + 2 * len(PIECES)),
         out_shape=[
             pltpu.VMEM((NF, ROWS, NZ), f32), pltpu.VMEM((4, CELLS, NZ), f32), pltpu.VMEM((NF, CELLS, NZ), f32),
-            sds(CELLS, NZ), sds(CELLS, NZ),
-        ],
+        ] + [sds(size * INNER, NZ) for size in PIECES] * 2,
         scratch_shapes=[pltpu.VMEM((NF, ROWS, NZ), f32)],
         compiler_params=params(16),
         cost_estimate=cost(60 * NF * CELLS * NZ, 40 * 2**20),
@@ -531,15 +547,14 @@
         out_shape=[sds(T_ROWS, NZ)] * 2,
         scratch_shapes=[pltpu.VMEM((T_ROWS, NZ), f32)] * 2,
         compiler_params=params(4),
-        cost_estimate=cost(10**5, 10**6),
+        cost_estimate=cost(1000, 1000),
         name="edges",
     )(links, ab, rx0, rx1)
     rt1 = swap(ty1, 1, 1)
     rt0 = swap(ty0, 1, 0)
 
-    send, ry0, ry1, rt0, rt1 = lax.optimization_barrier((send, ry0, ry1, rt0, rt1))
-    mine = keep + swap_freq(send, 1)
-    partner = swap_freq(mine, 2)
+    part = [keep + swap_freq(send, 1) for keep, send in zip(terms[:len(PIECES)], terms[len(PIECES):])]
+    partner = [swap_freq(value, 2) for value in part]
 
     planes, rows, keep_b, send_b = pl.pallas_call(
         boundary_kernel,
@@ -547,7 +562,7 @@
         out_specs=[whole()] * 4,
         out_shape=[pltpu.VMEM((NF, 4 * N, NZ), f32)] * 2 + [sds(8 * N, NZ)] * 2,
         compiler_params=params(8),
-        cost_estimate=cost(10**6, 11 * 2**20),
+        cost_estimate=cost(1000, 1000),
         name="boundary",
     )(freq_index, links, u, ab, w, rx0, rx1, ry0, ry1, rt0, rt1)
 
@@ -558,13 +573,13 @@
         out_specs=block3(6),
         out_shape=sds(6, CELLS, NZ),
         compiler_params=params(6),
-        cost_estimate=cost(10**6, 6 * 2**20),
+        cost_estimate=cost(1000, 1000),
         name="field",
     )(w, planes, rows)
 
     mine_b = keep_b + swap_freq(send_b, 1)
     partner_b, partner, forward = lax.optimization_barrier((swap_freq(mine_b, 2), partner, forward))
-    mine = mine + partner
+    mine = jnp.concatenate([value + other for value, other in zip(part, partner)], axis=0)
     mine_b = mine_b + partner_b
     other = swap_freq(mine, 1)
     other_b = swap_freq(mine_b, 1)
@@ -572,12 +587,12 @@
     grad_h, grad_v = pl.pallas_call(
         gradient_kernel,
         grid=(steps,),
-        in_specs=[block2, block2, whole(), whole(), whole(), block2, block2],
+        in_specs=[whole()] * 5 + [block2, block2],
         out_specs=[block2, block2],
         out_shape=[sds(CELLS, NZ)] * 2,
         scratch_shapes=[pltpu.VMEM((BLOCK, NZ), f32)],
         compiler_params=params(6),
-        cost_estimate=cost(10**6, 4 * 2**20),
+        cost_estimate=cost(1000, 1000),
         name="gradient",
     )(mine, other, mine_b, other_b, ab, cond_h, cond_v)
 

time: 69.3 us -> 63.5 us (0.916)
  waiting for transfers between devices: 15 us -> 8.4 us
    ppermute x6 -> x8, waiting for transfers between devices: 11.6 us -> 5.71 us  [swap_freq(): return lax.ppermute(value, 'freq', [(i, i ^ flip) for i in range(4)])]
    ppermute x6, waiting for transfers between devices: 3.39 us -> 2.68 us  [swap(): return lax.ppermute(value, 'sub', swap_pairs(axis, odd))]
    ppermute x6 -> x8, starting transfers between devices: 8.51 us -> 8.95 us  [swap_freq(): return lax.ppermute(value, 'freq', [(i, i ^ flip) for i in range(4)])]
  transfers between devices with their start and end apart: 12 -> 14, of which waited for: 7 -> 4; matrix products, arithmetic and copies ran while one was open for 0% -> 0% of each run, Pallas kernels for 27% -> 30%
where the time goes in v3:
time: 63.5 us; the launch traced here: 63.3 us
  starting transfers between devices  29.1 us (46%)
  Pallas kernels  24.2 us (38%)
  waiting for transfers between devices  8.4 us (13%)
  between operations  1.38 us (2%)
    ppermute x6, starting transfers between devices, swap(): return lax.ppermute(value, 'sub', swap_pairs(axis, odd))  20.2 us
    pallas_call x1, Pallas kernels, on_device(): pl.pallas_call(solve_kernel, grid=(steps + 1,), in_specs=[smem, whole(),...  12.5 us
    ppermute x8, starting transfers between devices, swap_freq(): return lax.ppermute(value, 'freq', [(i, i ^ flip) for i in range(4)])  8.95 us
    ppermute x8, waiting for transfers between devices, swap_freq(): return lax.ppermute(value, 'freq', [(i, i ^ flip) for i in range(4)])  5.71 us
    pallas_call x1, Pallas kernels, on_device(): pl.pallas_call(strip_kernel, grid=(2,), in_specs=[smem] + [whole()] * 2 +...  3.67 us
    pallas_call x1, Pallas kernels, on_device(): pl.pallas_call(boundary_kernel, in_specs=[smem] + [whole()] * 10, out_spe...  3.11 us
    ppermute x6, waiting for transfers between devices, swap(): return lax.ppermute(value, 'sub', swap_pairs(axis, odd))  2.68 us
    pallas_call x1, Pallas kernels, on_device(): pl.pallas_call(field_kernel, grid=(steps,), in_specs=[whole()] * 3, out_s...  2.31 us
  transfers between devices with their start and end apart: 14, of which 4 were waited for; matrix products, arithmetic and copies ran while one was open for 0% of the time, Pallas kernels for 30%

profile of v3, /device:TPU:71, one launch (start us, length us, event | category | flops | bytes accessed | tf_op | source)
XLA Modules:
  0.0 63.3 jit_solution(11001323094194803687)
XLA Ops:
  1.3 3.7 %strips.1 = (f32[888,128]{1,0:T(8,128)S(1)}, f32[888,128]{1,0:T(8,128)S(1)}, f32[832,128]{1,0:T(8,128)S(1)}, f32[832,128]{1,0:T(8,128)S(1)}) custom-call(s32[1]{0:T(128)S(6)} %copy.10.freq_ref, s32[1,4]{1,0:T(1,128)} %links_ref.5, s32[32,32]{1,0:T(8,128)} %bitcast.27, f32[6,1024,128]{2,1,0:T(8,128)} %bitcast.20, f32[6,1024,128]{2,1,0:T(8,128)} %bitcast.23, ...), custom_call_target="tpu_custom_call" | custom-call | flops 1000000 | bytes 12582912 | tf_op jit(solution)/shard_map/strips/pallas_call | solution.py:513
  4.9 1.4 %collective-permute-start = (f32[888,128]{1,0:T(8,128)S(1)}, f32[888,128]{1,0:T(8,128)S(1)}, u32[]{:S(2)}, u32[]{:S(2)}) collective-permute-start(f32[888,128]{1,0:T(8,128)S(1)} %get-tuple-element.29), channel_id=1, source_target_pairs={{0,4},{4,0},{8,12},{12,8},{16,20},{20,16},{24,28},{28,24},{32,36},... | collective-permute-start | bytes 1363976 | tf_op jit(solution)/shard_map/ppermute | solution.py:478
  6.3 4.1 %collective-permute-start.1 = (f32[888,128]{1,0:T(8,128)S(1)}, f32[888,128]{1,0:T(8,128)S(1)}, u32[]{:S(2)}, u32[]{:S(2)}) collective-permute-start(f32[888,128]{1,0:T(8,128)S(1)} %get-tuple-element.30), channel_id=1, source_target_pairs={{4,8},{8,4},{12,16},{16,12},{20,24},{24,20},{36,40},{40,36},{44,48... | collective-permute-start | bytes 1363976 | tf_op jit(solution)/shard_map/ppermute | solution.py:478
  10.4 0.9 %collective-permute-start.2 = (f32[832,128]{1,0:T(8,128)S(1)}, f32[832,128]{1,0:T(8,128)S(1)}, u32[]{:S(2)}, u32[]{:S(2)}) collective-permute-start(f32[832,128]{1,0:T(8,128)S(1)} %get-tuple-element.31), channel_id=1, source_target_pairs={{0,32},{4,36},{8,40},{12,44},{16,48},{20,52},{24,56},{28,60},{32,0... | collective-permute-start | bytes 1277960 | tf_op jit(solution)/shard_map/ppermute | solution.py:478
  11.3 8.0 %collective-permute-start.3 = (f32[832,128]{1,0:T(8,128)S(1)}, f32[832,128]{1,0:T(8,128)S(1)}, u32[]{:S(2)}, u32[]{:S(2)}) collective-permute-start(f32[832,128]{1,0:T(8,128)S(1)} %get-tuple-element.32), channel_id=1, source_target_pairs={{32,64},{36,68},{40,72},{44,76},{48,80},{52,84},{56,88},{60,92},{6... | collective-permute-start | bytes 1277960 | tf_op jit(solution)/shard_map/ppermute | solution.py:478
  19.3 12.5 %solve.1 = (f32[12,1360,128]{2,1,0:T(8,128)S(1)}, f32[4,1024,128]{2,1,0:T(8,128)S(1)}, f32[12,1024,128]{2,1,0:T(8,128)S(1)}, f32[560,128]{1,0:T(8,128)S(1)}, f32...) custom-call(s32[1]{0:T(128)S(6)} %copy.10.freq_ref, s32[32,32]{1,0:T(8,128)} %bitcast.28, ...), custom_call_target="tpu_custom_call" | custom-call | flops 94371840 | bytes 41943040 | tf_op jit(solution)/shard_map/solve/pallas_call | solution.py:529
  31.8 1.9 %collective-permute-start.8 = (f32[560,128]{1,0:T(8,128)S(1)}, f32[560,128]{1,0:T(8,128)S(1)}, u32[]{:S(2)}, u32[]{:S(2)}) collective-permute-start(f32[560,128]{1,0:T(8,128)S(1)} %get-tuple-element.38), channel_id=1, source_target_pairs={{0,1},{1,0},{2,3},{3,2},{4,5},{5,4},{6,7},{7,6},{8,9},{9,8},{10,11... | collective-permute-start | bytes 860168 | tf_op jit(solution)/shard_map/ppermute | solution.py:482
  33.7 0.0 collective-permute-done.rx0_ref
  33.7 0.0 collective-permute-done.1.rx1_ref
  33.7 0.8 %edges.1 = (f32[72,128]{1,0:T(8,128)S(1)}, f32[72,128]{1,0:T(8,128)S(1)}) custom-call(s32[1,4]{1,0:T(1,128)} %links_ref.5, f32[4,1024,128]{2,1,0:T(8,128)S(1)} %get-tuple-element.27.ab_ref, f32[888,128]{1,0:T(8,128)S(1)} %collective-permute-done.rx0_ref, f32[888,128]{1,0:T(8,128)S(1)} %collective-permute-done.1.rx1_ref), custom_call_target="tpu_custom_call" | custom-call | flops 1000 | bytes 1000 | tf_op jit(solution)/shard_map/edges/pallas_call | solution.py:543
  34.5 0.1 collective-permute-start.4
  34.6 5.8 %collective-permute-start.5 = (f32[72,128]{1,0:T(8,128)S(1)}, f32[72,128]{1,0:T(8,128)S(1)}, u32[]{:S(2)}, u32[]{:S(2)}) collective-permute-start(f32[72,128]{1,0:T(8,128)S(1)} %get-tuple-element.34), channel_id=1, source_target_pairs={{32,64},{36,68},{40,72},{44,76},{48,80},{52,84},{56,88},{60,92},{6... | collective-permute-start | bytes 110600 | tf_op jit(solution)/shard_map/ppermute | solution.py:478
  40.4 0.0 collective-permute-done.8
  40.4 0.8 %collective-permute-start.9 = (f32[560,128]{1,0:T(8,128)S(1)}, f32[560,128]{1,0:T(8,128)S(1)}, u32[]{:S(2)}, u32[]{:S(2)}) collective-permute-start(f32[560,128]{1,0:T(8,128)S(1)} %add.19), channel_id=1, source_target_pairs={{0,2},{1,3},{2,0},{3,1},{4,6},{5,7},{6,4},{7,5},{8,10},{9,11},{10,... | collective-permute-start | bytes 860168 | tf_op jit(solution)/shard_map/ppermute | solution.py:482
  41.2 0.0 collective-permute-done.2.ry0_ref
  41.3 0.0 collective-permute-done.3.ry1_ref
  41.3 0.0 collective-permute-done.4.rt0_ref
  41.3 2.7 %collective-permute-done.5.rt1_ref = f32[72,128]{1,0:T(8,128)S(1)} collective-permute-done((f32[72,128]{1,0:T(8,128)S(1)}, f32[72,128]{1,0:T(8,128)S(1)}, u32[]{:S(2)}, u32[]{:S(2)}) %collective-permute-start.5) | collective-permute-done | bytes 36896 | tf_op jit(solution)/shard_map/ppermute | solution.py:478
  43.9 3.1 %boundary.1 = (f32[12,128,128]{2,1,0:T(8,128)S(1)}, f32[12,128,128]{2,1,0:T(8,128)S(1)}, f32[256,128]{1,0:T(8,128)S(1)}, f32[256,128]{1,0:T(8,128)S(1)}) custom-call(s32[1]{0:T(128)S(6)} %copy.10.freq_ref, s32[1,4]{1,0:T(1,128)} %links_ref.5, f32[12,1360,128]{2,1,0:T(8,128)S(1)} %get-tuple-element.26.u_ref, f32[4,1024,128]{2,1,0:T(8,128)S(1)} %get-tuple-element.27.ab_ref, ...), custom_call_target="tpu_custom_call" | custom-call | flops 1000 | bytes 1000 | tf_op jit(solution)/shard_map/boundary/pallas_call | solution.py:559
  47.1 1.6 %collective-permute-start.6 = (f32[256,128]{1,0:T(8,128)S(1)}, f32[256,128]{1,0:T(8,128)S(1)}, u32[]{:S(2)}, u32[]{:S(2)}) collective-permute-start(f32[256,128]{1,0:T(8,128)S(1)} %get-tuple-element.36), channel_id=1, source_target_pairs={{0,1},{1,0},{2,3},{3,2},{4,5},{5,4},{6,7},{7,6},{8,9},{9,8},{10,11... | collective-permute-start | bytes 393224 | tf_op jit(solution)/shard_map/ppermute | solution.py:482
  48.6 0.1 collective-permute-start.10
  48.7 0.9 %collective-permute-done.6 = f32[256,128]{1,0:T(8,128)S(1)} collective-permute-done((f32[256,128]{1,0:T(8,128)S(1)}, f32[256,128]{1,0:T(8,128)S(1)}, u32[]{:S(2)}, u32[]{:S(2)}) %collective-permute-start.6) | collective-permute-done | bytes 131104 | tf_op jit(solution)/shard_map/ppermute | solution.py:482
  49.6 3.2 %collective-permute-start.7 = (f32[256,128]{1,0:T(8,128)S(1)}, f32[256,128]{1,0:T(8,128)S(1)}, u32[]{:S(2)}, u32[]{:S(2)}) collective-permute-start(f32[256,128]{1,0:T(8,128)S(1)} %add.18), channel_id=1, source_target_pairs={{0,2},{1,3},{2,0},{3,1},{4,6},{5,7},{6,4},{7,5},{8,10},{9,11},{10,... | collective-permute-start | bytes 393224 | tf_op jit(solution)/shard_map/ppermute | solution.py:482
  52.8 0.0 collective-permute-done.10
  52.8 0.3 collective-permute-start.11
  53.2 0.0 copy-start
  53.2 0.0 copy-start.1
  53.2 2.3 %field.1 = f32[6,1024,128]{2,1,0:T(8,128)} custom-call(f32[12,1024,128]{2,1,0:T(8,128)S(1)} %get-tuple-element.28.w_ref, f32[12,128,128]{2,1,0:T(8,128)S(1)} %get-tuple-element.41.planes_ref, f32[12,128,128]{2,1,0:T(8,128)S(1)} %get-tuple-element.42.rows_ref), custom_call_target="tpu_custom_call" | custom-call | flops 1000 | bytes 1000 | tf_op jit(solution)/shard_map/field/pallas_call | solution.py:569
  55.5 3.4 %collective-permute-done.11 = f32[224,128]{1,0:T(8,128)S(1)} collective-permute-done((f32[224,128]{1,0:T(8,128)S(1)}, f32[224,128]{1,0:T(8,128)S(1)}, u32[]{:S(2)}, u32[]{:S(2)}) %collective-permute-start.11) | collective-permute-done | bytes 114720 | tf_op jit(solution)/shard_map/ppermute | solution.py:482
  58.9 0.0 collective-permute-done.9
  58.9 0.0 collective-permute-done.7
  59.0 1.0 %collective-permute-start.12 = (f32[784,128]{1,0:T(8,128)S(1)}, f32[784,128]{1,0:T(8,128)S(1)}, u32[]{:S(2)}, u32[]{:S(2)}) collective-permute-start(f32[784,128]{1,0:T(8,128)S(1)} %pad_maximum_fusion.mine_ref), channel_id=1, source_target_pairs={{0,1},{1,0},{2,3},{3,2},{4,5},{5,4},{6,7},{7,6},{8,9},{9,8},{10,11... | collective-permute-start | bytes 1204232 | tf_op jit(solution)/shard_map/ppermute | solution.py:482
  59.9 0.1 collective-permute-start.13
  60.0 1.4 %collective-permute-done.13.other_b_ref = f32[256,128]{1,0:T(8,128)S(1)} collective-permute-done((f32[256,128]{1,0:T(8,128)S(1)}, f32[256,128]{1,0:T(8,128)S(1)}, u32[]{:S(2)}, u32[]{:S(2)}) %collective-permute-start.13) | collective-permute-done | bytes 131104 | tf_op jit(solution)/shard_map/ppermute | solution.py:482
  61.5 0.0 collective-permute-done.12.other_ref
  61.5 0.0 copy-done
  61.5 0.0 copy-done.1
  61.5 1.8 %gradient.1 = (f32[1024,128]{1,0:T(8,128)}, f32[1024,128]{1,0:T(8,128)}) custom-call(f32[784,128]{1,0:T(8,128)S(1)} %pad_maximum_fusion.mine_ref, f32[784,128]{1,0:T(8,128)S(1)} %collective-permute-done.12.other_ref, f32[256,128]{1,0:T(8,128)S(1)} %add.23.mine_b_ref, f32[256,128]{1,0:T(8,128)S(1)} %collective-permute-done.13.other_b_ref, ...), custom_call_target="tpu_custom_call" | custom-call | flops 1000 | bytes 1000 | tf_op jit(solution)/shard_map/gradient/pallas_call | solution.py:587
  (7 shorter events, 0.2 us)
Async XLA Ops:
  4.9 28.7 %collective-permute-start = (f32[888,128]{1,0:T(8,128)S(1)}, f32[888,128]{1,0:T(8,128)S(1)}, u32[]{:S(2)}, u32[]{:S(2)}) collective-permute-start(f32[888,128]{1,0:T(8,128)S(1)} %get-tuple-element.29), channel_id=1, source_target_pairs={{0,4},{4,0},{8,12},{12,8},{16,20},{20,16},{24,28},{28,24},{32,36},... | collective-permute-start | bytes 1363976 | tf_op jit(solution)/shard_map/ppermute | solution.py:478
  6.3 27.3 %collective-permute-start.1 = (f32[888,128]{1,0:T(8,128)S(1)}, f32[888,128]{1,0:T(8,128)S(1)}, u32[]{:S(2)}, u32[]{:S(2)}) collective-permute-start(f32[888,128]{1,0:T(8,128)S(1)} %get-tuple-element.30), channel_id=1, source_target_pairs={{4,8},{8,4},{12,16},{16,12},{20,24},{24,20},{36,40},{40,36},{44,48... | collective-permute-start | bytes 1363976 | tf_op jit(solution)/shard_map/ppermute | solution.py:478
  10.4 30.8 %collective-permute-start.2 = (f32[832,128]{1,0:T(8,128)S(1)}, f32[832,128]{1,0:T(8,128)S(1)}, u32[]{:S(2)}, u32[]{:S(2)}) collective-permute-start(f32[832,128]{1,0:T(8,128)S(1)} %get-tuple-element.31), channel_id=1, source_target_pairs={{0,32},{4,36},{8,40},{12,44},{16,48},{20,52},{24,56},{28,60},{32,0... | collective-permute-start | bytes 1277960 | tf_op jit(solution)/shard_map/ppermute | solution.py:478
  11.3 29.9 %collective-permute-start.3 = (f32[832,128]{1,0:T(8,128)S(1)}, f32[832,128]{1,0:T(8,128)S(1)}, u32[]{:S(2)}, u32[]{:S(2)}) collective-permute-start(f32[832,128]{1,0:T(8,128)S(1)} %get-tuple-element.32), channel_id=1, source_target_pairs={{32,64},{36,68},{40,72},{44,76},{48,80},{52,84},{56,88},{60,92},{6... | collective-permute-start | bytes 1277960 | tf_op jit(solution)/shard_map/ppermute | solution.py:478
  31.8 8.6 %collective-permute-start.8 = (f32[560,128]{1,0:T(8,128)S(1)}, f32[560,128]{1,0:T(8,128)S(1)}, u32[]{:S(2)}, u32[]{:S(2)}) collective-permute-start(f32[560,128]{1,0:T(8,128)S(1)} %get-tuple-element.38), channel_id=1, source_target_pairs={{0,1},{1,0},{2,3},{3,2},{4,5},{5,4},{6,7},{7,6},{8,9},{9,8},{10,11... | collective-permute-start | bytes 860168 | tf_op jit(solution)/shard_map/ppermute | solution.py:482
  34.5 6.8 %collective-permute-start.4 = (f32[72,128]{1,0:T(8,128)S(1)}, f32[72,128]{1,0:T(8,128)S(1)}, u32[]{:S(2)}, u32[]{:S(2)}) collective-permute-start(f32[72,128]{1,0:T(8,128)S(1)} %get-tuple-element.33), channel_id=1, source_target_pairs={{0,32},{4,36},{8,40},{12,44},{16,48},{20,52},{24,56},{28,60},{32,0... | collective-permute-start | bytes 110600 | tf_op jit(solution)/shard_map/ppermute | solution.py:478
  34.6 9.3 %collective-permute-start.5 = (f32[72,128]{1,0:T(8,128)S(1)}, f32[72,128]{1,0:T(8,128)S(1)}, u32[]{:S(2)}, u32[]{:S(2)}) collective-permute-start(f32[72,128]{1,0:T(8,128)S(1)} %get-tuple-element.34), channel_id=1, source_target_pairs={{32,64},{36,68},{40,72},{44,76},{48,80},{52,84},{56,88},{60,92},{6... | collective-permute-start | bytes 110600 | tf_op jit(solution)/shard_map/ppermute | solution.py:478
  40.4 18.4 %collective-permute-start.9 = (f32[560,128]{1,0:T(8,128)S(1)}, f32[560,128]{1,0:T(8,128)S(1)}, u32[]{:S(2)}, u32[]{:S(2)}) collective-permute-start(f32[560,128]{1,0:T(8,128)S(1)} %add.19), channel_id=1, source_target_pairs={{0,2},{1,3},{2,0},{3,1},{4,6},{5,7},{6,4},{7,5},{8,10},{9,11},{10,... | collective-permute-start | bytes 860168 | tf_op jit(solution)/shard_map/ppermute | solution.py:482
  47.1 2.5 %collective-permute-start.6 = (f32[256,128]{1,0:T(8,128)S(1)}, f32[256,128]{1,0:T(8,128)S(1)}, u32[]{:S(2)}, u32[]{:S(2)}) collective-permute-start(f32[256,128]{1,0:T(8,128)S(1)} %get-tuple-element.36), channel_id=1, source_target_pairs={{0,1},{1,0},{2,3},{3,2},{4,5},{5,4},{6,7},{7,6},{8,9},{9,8},{10,11... | collective-permute-start | bytes 393224 | tf_op jit(solution)/shard_map/ppermute | solution.py:482
  48.6 4.2 %collective-permute-start.10 = (f32[224,128]{1,0:T(8,128)S(1)}, f32[224,128]{1,0:T(8,128)S(1)}, u32[]{:S(2)}, u32[]{:S(2)}) collective-permute-start(f32[224,128]{1,0:T(8,128)S(1)} %get-tuple-element.40), channel_id=1, source_target_pairs={{0,1},{1,0},{2,3},{3,2},{4,5},{5,4},{6,7},{7,6},{8,9},{9,8},{10,11... | collective-permute-start | bytes 344072 | tf_op jit(solution)/shard_map/ppermute | solution.py:482
  49.6 9.3 %collective-permute-start.7 = (f32[256,128]{1,0:T(8,128)S(1)}, f32[256,128]{1,0:T(8,128)S(1)}, u32[]{:S(2)}, u32[]{:S(2)}) collective-permute-start(f32[256,128]{1,0:T(8,128)S(1)} %add.18), channel_id=1, source_target_pairs={{0,2},{1,3},{2,0},{3,1},{4,6},{5,7},{6,4},{7,5},{8,10},{9,11},{10,... | collective-permute-start | bytes 393224 | tf_op jit(solution)/shard_map/ppermute | solution.py:482
  52.8 6.0 %collective-permute-start.11 = (f32[224,128]{1,0:T(8,128)S(1)}, f32[224,128]{1,0:T(8,128)S(1)}, u32[]{:S(2)}, u32[]{:S(2)}) collective-permute-start(f32[224,128]{1,0:T(8,128)S(1)} %add.20), channel_id=1, source_target_pairs={{0,2},{1,3},{2,0},{3,1},{4,6},{5,7},{6,4},{7,5},{8,10},{9,11},{10,... | collective-permute-start | bytes 344072 | tf_op jit(solution)/shard_map/ppermute | solution.py:482
  53.2 8.3 %copy-start = (f32[1,32,32,128]{3,2,1,0:T(8,128)S(1)}, f32[1,32,32,128]{3,2,1,0:T(8,128)}, u32[]{:S(2)}) copy-start(f32[1,32,32,128]{3,2,1,0:T(8,128)} %param.9) | copy-start | bytes 1572868
  53.2 8.3 %copy-start.1 = (f32[1,32,32,128]{3,2,1,0:T(8,128)S(1)}, f32[1,32,32,128]{3,2,1,0:T(8,128)}, u32[]{:S(2)}) copy-start(f32[1,32,32,128]{3,2,1,0:T(8,128)} %param.10) | copy-start | bytes 1572868
  59.0 2.5 %collective-permute-start.12 = (f32[784,128]{1,0:T(8,128)S(1)}, f32[784,128]{1,0:T(8,128)S(1)}, u32[]{:S(2)}, u32[]{:S(2)}) collective-permute-start(f32[784,128]{1,0:T(8,128)S(1)} %pad_maximum_fusion.mine_ref), channel_id=1, source_target_pairs={{0,1},{1,0},{2,3},{3,2},{4,5},{5,4},{6,7},{7,6},{8,9},{9,8},{10,11... | collective-permute-start | bytes 1204232 | tf_op jit(solution)/shard_map/ppermute | solution.py:482
  59.9 1.5 %collective-permute-start.13 = (f32[256,128]{1,0:T(8,128)S(1)}, f32[256,128]{1,0:T(8,128)S(1)}, u32[]{:S(2)}, u32[]{:S(2)}) collective-permute-start(f32[256,128]{1,0:T(8,128)S(1)} %add.23.mine_b_ref), channel_id=1, source_target_pairs={{0,1},{1,0},{2,3},{3,2},{4,5},{5,4},{6,7},{7,6},{8,9},{9,8},{10,11... | collective-permute-start | bytes 393224 | tf_op jit(solution)/shard_map/ppermute | solution.py:482

commit v4 on v3

--- a/solution.py
+++ b/solution.py
@@ -9,7 +9,7 @@
 SUBS = 64
 N = 32
 NZ = 128
-PIECES = (20, 8)
+PIECES = (25, 3)
 INNER = N - 4
 PLANE = 40
 ROWS = 34 * PLANE
@@ -226,100 +226,88 @@
     freq_ref, floor_ref, src_ref, adj_ref, sh_ref, sv_ref,
     u_ref, ab_ref, w_ref, *refs,
 ):
-    step = pl.program_id(0)
     scale = scale_of(freq_ref)
     odd_core = lax.rem(lax.axis_index("freq"), 2) == 1
     count = len(PIECES)
     keep_refs, send_refs, v_ref = refs[:count], refs[count:2 * count], refs[2 * count]
-
-    @pl.when(step == 0)
-    def _():
-        zeros = jnp.zeros((PLANE, NZ), f32)
-        for f in range(NF):
-            for ref in (u_ref, v_ref):
-                ref[f, 0:PLANE, :] = zeros
-                ref[f, ROWS - PLANE:ROWS, :] = zeros
-
-    @pl.when(step < N // STEP)
-    def _():
-        def plane(j, carry):
-            x = step * STEP + j
-            here = pl.ds(pl.multiple_of(j * N, N), N)
-            there = pl.ds(pl.multiple_of(x * N, N), N)
-            start = pl.multiple_of(base(x), 8)
-            mask = mask_of(floor_column(floor_ref, x, 0, N))
-            ab = []
-            for k, ref in enumerate((sh_ref, sv_ref)):
-                ab.append(factors(scale * ref[here, :] * mask))
-                ab_ref[2 * k, there, :] = ab[k][0]
-                ab_ref[2 * k + 1, there, :] = ab[k][1]
-            zeros = jnp.zeros((8, NZ), f32)
-            for fr, fi, k in pairs():
-                ref, g = (src_ref, 0) if fr < 6 else (adj_ref, 6)
-                re, im = times(ab[k], ref[fr - g, here, :], ref[fi - g, here, :])
-                for f, value in ((fr, re), (fi, im)):
-                    u_ref[f, pl.ds(start, N), :] = value
-                    u_ref[f, pl.ds(start + N, 8), :] = zeros
-                    v_ref[f, pl.ds(start + N, 8), :] = zeros
+    zeros = jnp.zeros((PLANE, NZ), f32)
+    for f in range(NF):
+        for ref in (u_ref, v_ref):
+            ref[f, 0:PLANE, :] = zeros
+            ref[f, ROWS - PLANE:ROWS, :] = zeros
+
+    def first_update(x, carry):
+        there = pl.ds(pl.multiple_of(x * N, N), N)
+        start = pl.multiple_of(base(x), 8)
+        mask = mask_of(floor_column(floor_ref, x, 0, N))
+        ab = []
+        for k, ref in enumerate((sh_ref, sv_ref)):
+            ab.append(factors(scale * ref[there, :] * mask))
+            ab_ref[2 * k, there, :] = ab[k][0]
+            ab_ref[2 * k + 1, there, :] = ab[k][1]
+        zeros = jnp.zeros((8, NZ), f32)
+        for fr, fi, k in pairs():
+            ref, g = (src_ref, 0) if fr < 6 else (adj_ref, 6)
+            re, im = times(ab[k], ref[fr - g, there, :], ref[fi - g, there, :])
+            for f, value in ((fr, re), (fi, im)):
+                u_ref[f, pl.ds(start, N), :] = value
+                u_ref[f, pl.ds(start + N, 8), :] = zeros
+                v_ref[f, pl.ds(start + N, 8), :] = zeros
+        return carry
+
+    lax.fori_loop(0, N, first_update, 0, unroll=4)
+
+    def second_update(x, carry):
+        there = pl.ds(pl.multiple_of(x * N, N), N)
+        start = pl.multiple_of(base(x), 8)
+        ab = [(ab_ref[2 * k, there, :], ab_ref[2 * k + 1, there, :]) for k in range(2)]
+        for fr, fi, k in pairs():
+            re, im = times(ab[k], stencil(u_ref, fr, x), stencil(u_ref, fi, x))
+            v_ref[fr, pl.ds(start, N), :] = u_ref[fr, pl.ds(start, N), :] + re
+            v_ref[fi, pl.ds(start, N), :] = u_ref[fi, pl.ds(start, N), :] + im
+        return carry
+
+    lax.fori_loop(0, N, second_update, 0, unroll=4)
+
+    def last_update(x):
+        there = pl.ds(pl.multiple_of(x * N, N), N)
+        start = pl.multiple_of(base(x), 8)
+        ab = [(ab_ref[2 * k, there, :], ab_ref[2 * k + 1, there, :]) for k in range(2)]
+        term = [None, None]
+        for comp in range(3):
+            k = comp // 2
+            new = []
+            for solve in range(2):
+                fr, fi = solve * 6 + comp, solve * 6 + 3 + comp
+                re, im = times(ab[k], stencil(v_ref, fr, x), stencil(v_ref, fi, x))
+                re = re + u_ref[fr, pl.ds(start, N), :]
+                im = im + u_ref[fi, pl.ds(start, N), :]
+                w_ref[fr, there, :] = re
+                w_ref[fi, there, :] = im
+                new.append((re, im))
+            product = new[1][0] * new[0][1] + new[1][1] * new[0][0]
+            term[k] = product if term[k] is None else term[k] + product
+        return term
+
+    for x in (0, 1, N - 2, N - 1):
+        last_update(x)
+    first = 2
+    for size, keep_ref, send_ref in zip(PIECES, keep_refs, send_refs):
+        def plane(j, carry, first=first, keep_ref=keep_ref, send_ref=send_ref):
+            here = pl.ds(j * INNER, INNER)
+            term = last_update(first + j)
+            term_h, term_v = scale * term[0], scale * term[1]
+            keep_ref[here, :] = jnp.where(odd_core, term_v, term_h)[2:N - 2, :]
+            send_ref[here, :] = jnp.where(odd_core, term_h, term_v)[2:N - 2, :]
             return carry
 
-        lax.fori_loop(0, STEP, plane, 0, unroll=4)
-
-    @pl.when(step > 0)
-    def _():
-        def plane(j, carry):
-            x = (step - 1) * STEP + j
-            there = pl.ds(pl.multiple_of(x * N, N), N)
-            start = pl.multiple_of(base(x), 8)
-            ab = [(ab_ref[2 * k, there, :], ab_ref[2 * k + 1, there, :]) for k in range(2)]
-            for fr, fi, k in pairs():
-                re, im = times(ab[k], stencil(u_ref, fr, x), stencil(u_ref, fi, x))
-                v_ref[fr, pl.ds(start, N), :] = u_ref[fr, pl.ds(start, N), :] + re
-                v_ref[fi, pl.ds(start, N), :] = u_ref[fi, pl.ds(start, N), :] + im
-            return carry
-
-        lax.fori_loop(0, STEP, plane, 0, unroll=4)
-
-    @pl.when(step == N // STEP)
-    def _():
-        def last_update(x):
-            there = pl.ds(pl.multiple_of(x * N, N), N)
-            start = pl.multiple_of(base(x), 8)
-            ab = [(ab_ref[2 * k, there, :], ab_ref[2 * k + 1, there, :]) for k in range(2)]
-            term = [None, None]
-            for comp in range(3):
-                k = comp // 2
-                new = []
-                for solve in range(2):
-                    fr, fi = solve * 6 + comp, solve * 6 + 3 + comp
-                    re, im = times(ab[k], stencil(v_ref, fr, x), stencil(v_ref, fi, x))
-                    re = re + u_ref[fr, pl.ds(start, N), :]
-                    im = im + u_ref[fi, pl.ds(start, N), :]
-                    w_ref[fr, there, :] = re
-                    w_ref[fi, there, :] = im
-                    new.append((re, im))
-                product = new[1][0] * new[0][1] + new[1][1] * new[0][0]
-                term[k] = product if term[k] is None else term[k] + product
-            return term
-
-        for x in (0, 1, N - 2, N - 1):
-            last_update(x)
-        first = 2
-        for size, keep_ref, send_ref in zip(PIECES, keep_refs, send_refs):
-            def plane(j, carry, first=first, keep_ref=keep_ref, send_ref=send_ref):
-                here = pl.ds(j * INNER, INNER)
-                term = last_update(first + j)
-                term_h, term_v = scale * term[0], scale * term[1]
-                keep_ref[here, :] = jnp.where(odd_core, term_v, term_h)[2:N - 2, :]
-                send_ref[here, :] = jnp.where(odd_core, term_h, term_v)[2:N - 2, :]
-                return carry
-
-            lax.fori_loop(0, size, plane, 0, unroll=2)
-            first += size
+        lax.fori_loop(0, size, plane, 0, unroll=4)
+        first += size
 
 
 def boundary_kernel(
-    freq_ref, links_ref, u_ref, ab_ref, w_ref, rx0_ref, rx1_ref, ry0_ref, ry1_ref, rt0_ref, rt1_ref,
+    freq_ref, links_ref, u_ref, ab_ref, w_ref, py0_ref, py1_ref,
+    rx0_ref, rx1_ref, ry0_ref, ry1_ref, rt0_ref, rt1_ref, keep_in_ref, send_in_ref,
     planes_ref, rows_ref, keep_ref, send_ref,
 ):
     scale = scale_of(freq_ref)
@@ -355,15 +343,15 @@
     corner = [[[[factors(from_x(s, X_C + e * 4 + k * 2 + layer, 1)) for layer in range(2)]
                 for k in range(2)] for e in range(2)] for s in range(2)]
 
+    row_factors = [[[ab_row(k, y) for y in ys] for ys in ((0, 1), (N - 1, N - 2))] for k in range(2)]
+
     for fr, fi, k in pairs():
         both = (fr, fi)
         edge, ghost_y = [], []
         for e in range(2):
-            outer, inner = (0, 1) if e == 0 else (N - 1, N - 2)
             g1 = [link[2 + e] * from_y(e, f * N, N) for f in both]
-            edge.append((g1, times(ab_row(k, outer), *g1)))
-            own = [trace(u_ref[f, pl.ds(base(0) + outer, N, stride=PLANE), :],
-                         u_ref[f, pl.ds(base(0) + inner, N, stride=PLANE), :]) for f in both]
+            edge.append((g1, times(row_factors[k][e][0], *g1)))
+            own = [pick(odd_y, e, py0_ref, py1_ref, slice(f * N, (f + 1) * N)) for f in both]
             back = times(near_y[e][k], *own)
             ghost_y.append([
                 link[2 + e] * (from_y(e, FACE + f * N, N) + KEEP * back[c] + ends(from_t(e, f, 1), from_t(e, NF + f, 1)))
@@ -402,12 +390,14 @@
             outer, inner = (0, 1) if e == 0 else (N - 1, N - 2)
             w0 = edge[e][1]
             rhs = [row_neighbours(w0[c]) + lane_neighbours(w0[c]) + ghost_y[e][c] for c in range(2)]
-            fix0 = times(ab_row(k, outer), *rhs)
-            fix1 = times(ab_row(k, inner), *w0)
+            fix0 = times(row_factors[k][e][0], *rhs)
+            fix1 = times(row_factors[k][e][1], *w0)
             at0, at1 = (0, 1) if e == 0 else (3, 2)
             for c, f in enumerate(both):
                 rows_ref[f, at0 * N:(at0 + 1) * N, :] = w_ref[f, pl.ds(outer, N, stride=N), :] + fix0[c]
                 rows_ref[f, at1 * N:(at1 + 1) * N, :] = w_ref[f, pl.ds(inner, N, stride=N), :] + fix1[c]
+    keep_ref[8 * N:, :] = keep_in_ref[...]
+    send_ref[8 * N:, :] = send_in_ref[...]
     for ref, at in ((planes_ref, 0), (rows_ref, 4 * N)):
         term = [None, None]
         for comp in range(3):
@@ -445,23 +435,30 @@
 def gradient_kernel(mine_ref, other_ref, mine_b_ref, other_b_ref, ab_ref, sh_ref, sv_ref, gh_ref, gv_ref, total_ref):
     step = pl.program_id(0)
     odd_core = lax.rem(lax.axis_index("freq"), 2) == 1
-    mask = (ab_ref[0, pl.ds(pl.multiple_of(step * BLOCK, BLOCK), BLOCK), :] > 0.0).astype(f32)
+    block = pl.ds(pl.multiple_of(step * BLOCK, BLOCK), BLOCK)
+    mask = (ab_ref[0, block, :] > 0.0).astype(f32)
     for k, (sigma_ref, out_ref) in enumerate(((sh_ref, gh_ref), (sv_ref, gv_ref))):
         first = odd_core if k == 1 else jnp.logical_not(odd_core)
         for j in range(STEP):
-            inner = jnp.clip(step * STEP + j - 2, 0, INNER - 1)
+            inner = jnp.clip(step * STEP + j - 2, 0, PIECES[0] - 1)
             rows = pl.ds(inner * INNER, INNER)
             total_ref[j * N + 2:(j + 1) * N - 2, :] = jnp.where(first, mine_ref[rows, :], other_ref[rows, :])
 
         def boundary(rows):
             return jnp.where(first, mine_b_ref[rows, :], other_b_ref[rows, :])
+
+        @pl.when(step == N // STEP - 1)
+        def _():
+            for p in range(PIECES[1]):
+                at, rows = (STEP - 2 - PIECES[1] + p) * N + 2, 8 * N + p * INNER
+                total_ref[at:at + INNER, :] = boundary(slice(rows, rows + INNER))
 
         put_boundary(
             step, total_ref, (),
             lambda at: boundary(slice(at, at + 2 * N)),
             lambda at: boundary(pl.ds(pl.multiple_of((4 + at) * N + step * STEP, 8), STEP)),
         )
-        out_ref[...] = sigma_ref[...] * mask * total_ref[...]
+        out_ref[...] = sigma_ref[block, :] * mask * total_ref[...]
 
 
 def swap_pairs(axis, odd):
@@ -528,17 +525,18 @@
 
     u, ab, w, *terms = pl.pallas_call(
         solve_kernel,
-        grid=(steps + 1,),
-        in_specs=[smem, whole(), block3(6), block3(6), block2, block2],
+        in_specs=[smem] + [whole()] * 5,
         out_specs=[whole()] * (3 + 2 * len(PIECES)),
         out_shape=[
             pltpu.VMEM((NF, ROWS, NZ), f32), pltpu.VMEM((4, CELLS, NZ), f32), pltpu.VMEM((NF, CELLS, NZ), f32),
         ] + [sds(size * INNER, NZ) for size in PIECES] * 2,
         scratch_shapes=[pltpu.VMEM((NF, ROWS, NZ), f32)],
-        compiler_params=params(16),
+        compiler_params=params(24),
         cost_estimate=cost(60 * NF * CELLS * NZ, 40 * 2**20),
         name="solve",
-    )(freq_index, floor, flat_src, flat_adj, flat_h, flat_v)
+    )(
+        freq_index, floor, source.reshape(6, CELLS, NZ), adjoint_source.reshape(6, CELLS, NZ), cond_h, cond_v
+    )
 
     ty0, ty1 = pl.pallas_call(
         edge_kernel,
@@ -553,18 +551,18 @@
     rt1 = swap(ty1, 1, 1)
     rt0 = swap(ty0, 1, 0)
 
-    part = [keep + swap_freq(send, 1) for keep, send in zip(terms[:len(PIECES)], terms[len(PIECES):])]
-    partner = [swap_freq(value, 2) for value in part]
+    mine = terms[0] + swap_freq(terms[2], 1)
+    partner = swap_freq(mine, 2)
 
     planes, rows, keep_b, send_b = pl.pallas_call(
         boundary_kernel,
-        in_specs=[smem] + [whole()] * 10,
+        in_specs=[smem] + [whole()] * 14,
         out_specs=[whole()] * 4,
-        out_shape=[pltpu.VMEM((NF, 4 * N, NZ), f32)] * 2 + [sds(8 * N, NZ)] * 2,
+        out_shape=[pltpu.VMEM((NF, 4 * N, NZ), f32)] * 2 + [sds(8 * N + PIECES[1] * INNER, NZ)] * 2,
         compiler_params=params(8),
         cost_estimate=cost(1000, 1000),
         name="boundary",
-    )(freq_index, links, u, ab, w, rx0, rx1, ry0, ry1, rt0, rt1)
+    )(freq_index, links, u, ab, w, py0, py1, rx0, rx1, ry0, ry1, rt0, rt1, terms[1], terms[3])
 
     forward = pl.pallas_call(
         field_kernel,
@@ -579,7 +577,7 @@
 
     mine_b = keep_b + swap_freq(send_b, 1)
     partner_b, partner, forward = lax.optimization_barrier((swap_freq(mine_b, 2), partner, forward))
-    mine = jnp.concatenate([value + other for value, other in zip(part, partner)], axis=0)
+    mine = mine + partner
     mine_b = mine_b + partner_b
     other = swap_freq(mine, 1)
     other_b = swap_freq(mine_b, 1)
@@ -587,7 +585,7 @@
     grad_h, grad_v = pl.pallas_call(
         gradient_kernel,
         grid=(steps,),
-        in_specs=[whole()] * 5 + [block2, block2],
+        in_specs=[whole()] * 7,
         out_specs=[block2, block2],
         out_shape=[sds(CELLS, NZ)] * 2,
         scratch_shapes=[pltpu.VMEM((BLOCK, NZ), f32)],

time: 63.5 us -> 61.8 us (0.973)
  Pallas kernels: 24.2 us -> 22.6 us
  waiting for transfers between devices: 8.4 us -> 7.37 us
  starting transfers between devices: 29.1 us -> 29.9 us
    pallas_call x3, Pallas kernels: 17.4 us -> 15.7 us  [the longest x1 11.3 us: on_device(): pl.pallas_call(solve_kernel, in_specs=[smem] + [whole()] * 5, out_specs=[...]
    ppermute x8 -> x6, waiting for transfers between devices: 5.71 us -> 4.71 us  [swap_freq(): return lax.ppermute(value, 'freq', [(i, i ^ flip) for i in range(4)])]
    ppermute x8 -> x6, starting transfers between devices: 8.95 us -> 9.73 us  [swap_freq(): return lax.ppermute(value, 'freq', [(i, i ^ flip) for i in range(4)])]
  transfers between devices with their start and end apart: 14 -> 12, of which waited for: 4 -> 4; matrix products, arithmetic and copies ran while one was open for 0% -> 0% of each run, Pallas kernels for 30% -> 28%
where the time goes in v4:
time: 61.8 us; the launch traced here: 61.5 us
  starting transfers between devices  29.9 us (48%)
  Pallas kernels  22.6 us (37%)
  waiting for transfers between devices  7.37 us (12%)
  between operations  1.42 us (2%)
    ppermute x6, starting transfers between devices, swap(): return lax.ppermute(value, 'sub', swap_pairs(axis, odd))  20.2 us
    pallas_call x1, Pallas kernels, on_device(): pl.pallas_call(solve_kernel, in_specs=[smem] + [whole()] * 5, out_specs=[...  11.3 us
    ppermute x6, starting transfers between devices, swap_freq(): return lax.ppermute(value, 'freq', [(i, i ^ flip) for i in range(4)])  9.73 us
    ppermute x6, waiting for transfers between devices, swap_freq(): return lax.ppermute(value, 'freq', [(i, i ^ flip) for i in range(4)])  4.71 us
    pallas_call x1, Pallas kernels, on_device(): pl.pallas_call(strip_kernel, grid=(2,), in_specs=[smem] + [whole()] * 2 +...  3.81 us
    ppermute x6, waiting for transfers between devices, swap(): return lax.ppermute(value, 'sub', swap_pairs(axis, odd))  2.66 us
    pallas_call x1, Pallas kernels, on_device(): pl.pallas_call(boundary_kernel, in_specs=[smem] + [whole()] * 14, out_spe...  2.63 us
    pallas_call x1, Pallas kernels, on_device(): pl.pallas_call(field_kernel, grid=(steps,), in_specs=[whole()] * 3, out_s...  2.31 us
  transfers between devices with their start and end apart: 12, of which 4 were waited for; matrix products, arithmetic and copies ran while one was open for 0% of the time, Pallas kernels for 28%

profile of v4, /device:TPU:71, one launch (start us, length us, event | category | flops | bytes accessed | tf_op | source)
XLA Modules:
  0.0 61.5 jit_solution(6912502669325196564)
XLA Ops:
  1.3 0.0 copy-start
  1.3 0.0 copy-start.1
  1.3 0.0 copy-start.2
  1.3 0.0 copy-start.3
  1.3 3.8 %strips.1 = (f32[888,128]{1,0:T(8,128)S(1)}, f32[888,128]{1,0:T(8,128)S(1)}, f32[832,128]{1,0:T(8,128)S(1)}, f32[832,128]{1,0:T(8,128)S(1)}) custom-call(s32[1]{0:T(128)S(6)} %copy.10.freq_ref, s32[1,4]{1,0:T(1,128)} %links_ref.5, s32[32,32]{1,0:T(8,128)} %bitcast.27, f32[6,1024,128]{2,1,0:T(8,128)} %bitcast.12, f32[6,1024,128]{2,1,0:T(8,128)} %bitcast.15, ...), custom_call_target="tpu_custom_call" | custom-call | flops 1000000 | bytes 12582912 | tf_op jit(solution)/shard_map/strips/pallas_call | solution.py:510
  5.1 1.4 %collective-permute-start = (f32[888,128]{1,0:T(8,128)S(1)}, f32[888,128]{1,0:T(8,128)S(1)}, u32[]{:S(2)}, u32[]{:S(2)}) collective-permute-start(f32[888,128]{1,0:T(8,128)S(1)} %get-tuple-element.30), channel_id=1, source_target_pairs={{0,4},{4,0},{8,12},{12,8},{16,20},{20,16},{24,28},{28,24},{32,36},... | collective-permute-start | bytes 1363976 | tf_op jit(solution)/shard_map/ppermute | solution.py:475
  6.5 4.1 %collective-permute-start.1 = (f32[888,128]{1,0:T(8,128)S(1)}, f32[888,128]{1,0:T(8,128)S(1)}, u32[]{:S(2)}, u32[]{:S(2)}) collective-permute-start(f32[888,128]{1,0:T(8,128)S(1)} %get-tuple-element.31), channel_id=1, source_target_pairs={{4,8},{8,4},{12,16},{16,12},{20,24},{24,20},{36,40},{40,36},{44,48... | collective-permute-start | bytes 1363976 | tf_op jit(solution)/shard_map/ppermute | solution.py:475
  10.6 0.9 %collective-permute-start.2 = (f32[832,128]{1,0:T(8,128)S(1)}, f32[832,128]{1,0:T(8,128)S(1)}, u32[]{:S(2)}, u32[]{:S(2)}) collective-permute-start(f32[832,128]{1,0:T(8,128)S(1)} %get-tuple-element.28.py0_ref), channel_id=1, source_target_pairs={{0,32},{4,36},{8,40},{12,44},{16,48},{20,52},{24,56},{28,60},{32,0... | collective-permute-start | bytes 1277960 | tf_op jit(solution)/shard_map/ppermute | solution.py:475
  11.5 8.0 %collective-permute-start.3 = (f32[832,128]{1,0:T(8,128)S(1)}, f32[832,128]{1,0:T(8,128)S(1)}, u32[]{:S(2)}, u32[]{:S(2)}) collective-permute-start(f32[832,128]{1,0:T(8,128)S(1)} %get-tuple-element.29.py1_ref), channel_id=1, source_target_pairs={{32,64},{36,68},{40,72},{44,76},{48,80},{52,84},{56,88},{60,92},{6... | collective-permute-start | bytes 1277960 | tf_op jit(solution)/shard_map/ppermute | solution.py:475
  19.5 0.0 copy-done
  19.5 0.0 copy-done.1
  19.5 0.0 copy-done.2
  19.5 0.0 copy-done.3
  19.5 11.3 %solve.1 = (f32[12,1360,128]{2,1,0:T(8,128)S(1)}, f32[4,1024,128]{2,1,0:T(8,128)S(1)}, f32[12,1024,128]{2,1,0:T(8,128)S(1)}, f32[700,128]{1,0:T(8,128)S(1)}, f32...) custom-call(s32[1]{0:T(128)S(6)} %copy.10.freq_ref, s32[32,32]{1,0:T(8,128)} %bitcast.28, ...), custom_call_target="tpu_custom_call" | custom-call | flops 94371840 | bytes 41943040 | tf_op jit(solution)/shard_map/solve/pallas_call | solution.py:526
  30.8 1.9 %collective-permute-start.8 = (f32[700,128]{1,0:T(8,128)S(1)}, f32[700,128]{1,0:T(8,128)S(1)}, u32[]{:S(2)}, u32[]{:S(2)}) collective-permute-start(f32[700,128]{1,0:T(8,128)S(1)} %get-tuple-element.39), channel_id=1, source_target_pairs={{0,1},{1,0},{2,3},{3,2},{4,5},{5,4},{6,7},{7,6},{8,9},{9,8},{10,11... | collective-permute-start | bytes 1075208 | tf_op jit(solution)/shard_map/ppermute | solution.py:479
  32.7 0.0 collective-permute-done.rx0_ref
  32.7 0.0 collective-permute-done.1.rx1_ref
  32.7 0.8 %edges.1 = (f32[72,128]{1,0:T(8,128)S(1)}, f32[72,128]{1,0:T(8,128)S(1)}) custom-call(s32[1,4]{1,0:T(1,128)} %links_ref.5, f32[4,1024,128]{2,1,0:T(8,128)S(1)} %get-tuple-element.26.ab_ref, f32[888,128]{1,0:T(8,128)S(1)} %collective-permute-done.rx0_ref, f32[888,128]{1,0:T(8,128)S(1)} %collective-permute-done.1.rx1_ref), custom_call_target="tpu_custom_call" | custom-call | flops 1000 | bytes 1000 | tf_op jit(solution)/shard_map/edges/pallas_call | solution.py:541
  33.5 0.1 collective-permute-start.4
  33.6 5.8 %collective-permute-start.5 = (f32[72,128]{1,0:T(8,128)S(1)}, f32[72,128]{1,0:T(8,128)S(1)}, u32[]{:S(2)}, u32[]{:S(2)}) collective-permute-start(f32[72,128]{1,0:T(8,128)S(1)} %get-tuple-element.33), channel_id=1, source_target_pairs={{32,64},{36,68},{40,72},{44,76},{48,80},{52,84},{56,88},{60,92},{6... | collective-permute-start | bytes 110600 | tf_op jit(solution)/shard_map/ppermute | solution.py:475
  39.4 0.0 collective-permute-done.8
  39.4 0.1 add.13
  39.4 0.8 %collective-permute-start.9 = (f32[700,128]{1,0:T(8,128)S(1)}, f32[700,128]{1,0:T(8,128)S(1)}, u32[]{:S(2)}, u32[]{:S(2)}) collective-permute-start(f32[700,128]{1,0:T(8,128)S(1)} %add.13), channel_id=1, source_target_pairs={{0,2},{1,3},{2,0},{3,1},{4,6},{5,7},{6,4},{7,5},{8,10},{9,11},{10,... | collective-permute-start | bytes 1075208 | tf_op jit(solution)/shard_map/ppermute | solution.py:479
  40.3 0.0 collective-permute-done.2.ry0_ref
  40.3 0.0 collective-permute-done.3.ry1_ref
  40.3 0.0 collective-permute-done.4.rt0_ref
  40.3 2.7 %collective-permute-done.5.rt1_ref = f32[72,128]{1,0:T(8,128)S(1)} collective-permute-done((f32[72,128]{1,0:T(8,128)S(1)}, f32[72,128]{1,0:T(8,128)S(1)}, u32[]{:S(2)}, u32[]{:S(2)}) %collective-permute-start.5) | collective-permute-done | bytes 36896 | tf_op jit(solution)/shard_map/ppermute | solution.py:475
  42.9 2.6 %boundary.1 = (f32[12,128,128]{2,1,0:T(8,128)S(1)}, f32[12,128,128]{2,1,0:T(8,128)S(1)}, f32[340,128]{1,0:T(8,128)S(1)}, f32[340,128]{1,0:T(8,128)S(1)}) custom-call(s32[1]{0:T(128)S(6)} %copy.10.freq_ref, s32[1,4]{1,0:T(1,128)} %links_ref.5, f32[12,1360,128]{2,1,0:T(8,128)S(1)} %get-tuple-element.25.u_ref, f32[4,1024,128]{2,1,0:T(8,128)S(1)} %get-tuple-element.26.ab_ref, ...), custom_call_target="tpu_custom_call" | custom-call | flops 1000 | bytes 1000 | tf_op jit(solution)/shard_map/boundary/pallas_call | solution.py:557
  45.6 2.5 %collective-permute-start.6 = (f32[340,128]{1,0:T(8,128)S(1)}, f32[340,128]{1,0:T(8,128)S(1)}, u32[]{:S(2)}, u32[]{:S(2)}) collective-permute-start(f32[340,128]{1,0:T(8,128)S(1)} %get-tuple-element.37), channel_id=1, source_target_pairs={{0,1},{1,0},{2,3},{3,2},{4,5},{5,4},{6,7},{7,6},{8,9},{9,8},{10,11... | collective-permute-start | bytes 522248 | tf_op jit(solution)/shard_map/ppermute | solution.py:479
  48.1 1.0 %collective-permute-done.6 = f32[340,128]{1,0:T(8,128)S(1)} collective-permute-done((f32[340,128]{1,0:T(8,128)S(1)}, f32[340,128]{1,0:T(8,128)S(1)}, u32[]{:S(2)}, u32[]{:S(2)}) %collective-permute-start.6) | collective-permute-done | bytes 174112 | tf_op jit(solution)/shard_map/ppermute | solution.py:479
  49.1 3.5 %collective-permute-start.7 = (f32[340,128]{1,0:T(8,128)S(1)}, f32[340,128]{1,0:T(8,128)S(1)}, u32[]{:S(2)}, u32[]{:S(2)}) collective-permute-start(f32[340,128]{1,0:T(8,128)S(1)} %add.12), channel_id=1, source_target_pairs={{0,2},{1,3},{2,0},{3,1},{4,6},{5,7},{6,4},{7,5},{8,10},{9,11},{10,... | collective-permute-start | bytes 522248 | tf_op jit(solution)/shard_map/ppermute | solution.py:479
  52.6 2.3 %field.1 = f32[6,1024,128]{2,1,0:T(8,128)} custom-call(f32[12,1024,128]{2,1,0:T(8,128)S(1)} %get-tuple-element.27.w_ref, f32[12,128,128]{2,1,0:T(8,128)S(1)} %get-tuple-element.40.planes_ref, f32[12,128,128]{2,1,0:T(8,128)S(1)} %get-tuple-element.41.rows_ref), custom_call_target="tpu_custom_call" | custom-call | flops 1000 | bytes 1000 | tf_op jit(solution)/shard_map/field/pallas_call | solution.py:567
  54.9 0.0 collective-permute-done.9
  54.9 2.2 %collective-permute-done.7 = f32[340,128]{1,0:T(8,128)S(1)} collective-permute-done((f32[340,128]{1,0:T(8,128)S(1)}, f32[340,128]{1,0:T(8,128)S(1)}, u32[]{:S(2)}, u32[]{:S(2)}) %collective-permute-start.7) | collective-permute-done | bytes 174112 | tf_op jit(solution)/shard_map/ppermute | solution.py:479
  57.2 1.0 %collective-permute-start.10 = (f32[700,128]{1,0:T(8,128)S(1)}, f32[700,128]{1,0:T(8,128)S(1)}, u32[]{:S(2)}, u32[]{:S(2)}) collective-permute-start(f32[700,128]{1,0:T(8,128)S(1)} %add.14.mine_ref), channel_id=1, source_target_pairs={{0,1},{1,0},{2,3},{3,2},{4,5},{5,4},{6,7},{7,6},{8,9},{9,8},{10,11... | collective-permute-start | bytes 1075208 | tf_op jit(solution)/shard_map/ppermute | solution.py:479
  58.2 0.1 collective-permute-start.11
  58.3 1.4 %collective-permute-done.11.other_b_ref = f32[340,128]{1,0:T(8,128)S(1)} collective-permute-done((f32[340,128]{1,0:T(8,128)S(1)}, f32[340,128]{1,0:T(8,128)S(1)}, u32[]{:S(2)}, u32[]{:S(2)}) %collective-permute-start.11) | collective-permute-done | bytes 174112 | tf_op jit(solution)/shard_map/ppermute | solution.py:479
  59.7 0.0 collective-permute-done.10.other_ref
  59.7 1.8 %gradient.1 = (f32[1024,128]{1,0:T(8,128)}, f32[1024,128]{1,0:T(8,128)}) custom-call(f32[700,128]{1,0:T(8,128)S(1)} %add.14.mine_ref, f32[700,128]{1,0:T(8,128)S(1)} %collective-permute-done.10.other_ref, f32[340,128]{1,0:T(8,128)S(1)} %add.15.mine_b_ref, f32[340,128]{1,0:T(8,128)S(1)} %collective-permute-done.11.other_b_ref, ...), custom_call_target="tpu_custom_call" | custom-call | flops 1000 | bytes 1000 | tf_op jit(solution)/shard_map/gradient/pallas_call | solution.py:585
  (3 shorter events, 0.1 us)
Async XLA Ops:
  1.3 18.2 %copy-start = (f32[1,2,3,32,32,128]{5,4,3,2,1,0:T(8,128)S(1)}, f32[1,2,3,32,32,128]{5,4,3,2,1,0:T(8,128)}, u32[]{:S(2)}) copy-start(f32[1,2,3,32,32,128]{5,4,3,2,1,0:T(8,128)} %param.7) | copy-start | bytes 9437188
  1.3 18.2 %copy-start.1 = (f32[1,1,2,3,32,32,128]{6,5,4,3,2,1,0:T(8,128)S(1)}, f32[1,1,2,3,32,32,128]{6,5,4,3,2,1,0:T(8,128)}, u32[]{:S(2)}) copy-start(f32[1,1,2,3,32,32,128]{6,5,4,3,2,1,0:T(8,128)} %param.8) | copy-start | bytes 9437188
  1.3 18.2 %copy-start.2 = (f32[1,32,32,128]{3,2,1,0:T(8,128)S(1)}, f32[1,32,32,128]{3,2,1,0:T(8,128)}, u32[]{:S(2)}) copy-start(f32[1,32,32,128]{3,2,1,0:T(8,128)} %param.9) | copy-start | bytes 1572868
  1.3 18.2 %copy-start.3 = (f32[1,32,32,128]{3,2,1,0:T(8,128)S(1)}, f32[1,32,32,128]{3,2,1,0:T(8,128)}, u32[]{:S(2)}) copy-start(f32[1,32,32,128]{3,2,1,0:T(8,128)} %param.10) | copy-start | bytes 1572868
  5.1 27.5 %collective-permute-start = (f32[888,128]{1,0:T(8,128)S(1)}, f32[888,128]{1,0:T(8,128)S(1)}, u32[]{:S(2)}, u32[]{:S(2)}) collective-permute-start(f32[888,128]{1,0:T(8,128)S(1)} %get-tuple-element.30), channel_id=1, source_target_pairs={{0,4},{4,0},{8,12},{12,8},{16,20},{20,16},{24,28},{28,24},{32,36},... | collective-permute-start | bytes 1363976 | tf_op jit(solution)/shard_map/ppermute | solution.py:475
  6.5 26.2 %collective-permute-start.1 = (f32[888,128]{1,0:T(8,128)S(1)}, f32[888,128]{1,0:T(8,128)S(1)}, u32[]{:S(2)}, u32[]{:S(2)}) collective-permute-start(f32[888,128]{1,0:T(8,128)S(1)} %get-tuple-element.31), channel_id=1, source_target_pairs={{4,8},{8,4},{12,16},{16,12},{20,24},{24,20},{36,40},{40,36},{44,48... | collective-permute-start | bytes 1363976 | tf_op jit(solution)/shard_map/ppermute | solution.py:475
  10.6 29.7 %collective-permute-start.2 = (f32[832,128]{1,0:T(8,128)S(1)}, f32[832,128]{1,0:T(8,128)S(1)}, u32[]{:S(2)}, u32[]{:S(2)}) collective-permute-start(f32[832,128]{1,0:T(8,128)S(1)} %get-tuple-element.28.py0_ref), channel_id=1, source_target_pairs={{0,32},{4,36},{8,40},{12,44},{16,48},{20,52},{24,56},{28,60},{32,0... | collective-permute-start | bytes 1277960 | tf_op jit(solution)/shard_map/ppermute | solution.py:475
  11.5 28.8 %collective-permute-start.3 = (f32[832,128]{1,0:T(8,128)S(1)}, f32[832,128]{1,0:T(8,128)S(1)}, u32[]{:S(2)}, u32[]{:S(2)}) collective-permute-start(f32[832,128]{1,0:T(8,128)S(1)} %get-tuple-element.29.py1_ref), channel_id=1, source_target_pairs={{32,64},{36,68},{40,72},{44,76},{48,80},{52,84},{56,88},{60,92},{6... | collective-permute-start | bytes 1277960 | tf_op jit(solution)/shard_map/ppermute | solution.py:475
  30.8 8.6 %collective-permute-start.8 = (f32[700,128]{1,0:T(8,128)S(1)}, f32[700,128]{1,0:T(8,128)S(1)}, u32[]{:S(2)}, u32[]{:S(2)}) collective-permute-start(f32[700,128]{1,0:T(8,128)S(1)} %get-tuple-element.39), channel_id=1, source_target_pairs={{0,1},{1,0},{2,3},{3,2},{4,5},{5,4},{6,7},{7,6},{8,9},{9,8},{10,11... | collective-permute-start | bytes 1075208 | tf_op jit(solution)/shard_map/ppermute | solution.py:479
  33.5 6.8 %collective-permute-start.4 = (f32[72,128]{1,0:T(8,128)S(1)}, f32[72,128]{1,0:T(8,128)S(1)}, u32[]{:S(2)}, u32[]{:S(2)}) collective-permute-start(f32[72,128]{1,0:T(8,128)S(1)} %get-tuple-element.32), channel_id=1, source_target_pairs={{0,32},{4,36},{8,40},{12,44},{16,48},{20,52},{24,56},{28,60},{32,0... | collective-permute-start | bytes 110600 | tf_op jit(solution)/shard_map/ppermute | solution.py:475
  33.6 9.3 %collective-permute-start.5 = (f32[72,128]{1,0:T(8,128)S(1)}, f32[72,128]{1,0:T(8,128)S(1)}, u32[]{:S(2)}, u32[]{:S(2)}) collective-permute-start(f32[72,128]{1,0:T(8,128)S(1)} %get-tuple-element.33), channel_id=1, source_target_pairs={{32,64},{36,68},{40,72},{44,76},{48,80},{52,84},{56,88},{60,92},{6... | collective-permute-start | bytes 110600 | tf_op jit(solution)/shard_map/ppermute | solution.py:475
  39.4 15.5 %collective-permute-start.9 = (f32[700,128]{1,0:T(8,128)S(1)}, f32[700,128]{1,0:T(8,128)S(1)}, u32[]{:S(2)}, u32[]{:S(2)}) collective-permute-start(f32[700,128]{1,0:T(8,128)S(1)} %add.13), channel_id=1, source_target_pairs={{0,2},{1,3},{2,0},{3,1},{4,6},{5,7},{6,4},{7,5},{8,10},{9,11},{10,... | collective-permute-start | bytes 1075208 | tf_op jit(solution)/shard_map/ppermute | solution.py:479
  45.6 3.5 %collective-permute-start.6 = (f32[340,128]{1,0:T(8,128)S(1)}, f32[340,128]{1,0:T(8,128)S(1)}, u32[]{:S(2)}, u32[]{:S(2)}) collective-permute-start(f32[340,128]{1,0:T(8,128)S(1)} %get-tuple-element.37), channel_id=1, source_target_pairs={{0,1},{1,0},{2,3},{3,2},{4,5},{5,4},{6,7},{7,6},{8,9},{9,8},{10,11... | collective-permute-start | bytes 522248 | tf_op jit(solution)/shard_map/ppermute | solution.py:479
  49.1 8.0 %collective-permute-start.7 = (f32[340,128]{1,0:T(8,128)S(1)}, f32[340,128]{1,0:T(8,128)S(1)}, u32[]{:S(2)}, u32[]{:S(2)}) collective-permute-start(f32[340,128]{1,0:T(8,128)S(1)} %add.12), channel_id=1, source_target_pairs={{0,2},{1,3},{2,0},{3,1},{4,6},{5,7},{6,4},{7,5},{8,10},{9,11},{10,... | collective-permute-start | bytes 522248 | tf_op jit(solution)/shard_map/ppermute | solution.py:479
  57.2 2.5 %collective-permute-start.10 = (f32[700,128]{1,0:T(8,128)S(1)}, f32[700,128]{1,0:T(8,128)S(1)}, u32[]{:S(2)}, u32[]{:S(2)}) collective-permute-start(f32[700,128]{1,0:T(8,128)S(1)} %add.14.mine_ref), channel_id=1, source_target_pairs={{0,1},{1,0},{2,3},{3,2},{4,5},{5,4},{6,7},{7,6},{8,9},{9,8},{10,11... | collective-permute-start | bytes 1075208 | tf_op jit(solution)/shard_map/ppermute | solution.py:479
  58.2 1.5 %collective-permute-start.11 = (f32[340,128]{1,0:T(8,128)S(1)}, f32[340,128]{1,0:T(8,128)S(1)}, u32[]{:S(2)}, u32[]{:S(2)}) collective-permute-start(f32[340,128]{1,0:T(8,128)S(1)} %add.15.mine_b_ref), channel_id=1, source_target_pairs={{0,1},{1,0},{2,3},{3,2},{4,5},{5,4},{6,7},{7,6},{8,9},{9,8},{10,11... | collective-permute-start | bytes 522248 | tf_op jit(solution)/shard_map/ppermute | solution.py:479

commit v5 on v4

--- a/solution.py
+++ b/solution.py
@@ -14,6 +14,7 @@
 PLANE = 40
 ROWS = 34 * PLANE
 STEP = 8
+LAST = 16
 BLOCK = STEP * N
 CELLS = N * N
 NF = 12
@@ -305,8 +306,17 @@
         first += size
 
 
+def gather_kernel(ab_ref, w_ref, abr_ref, wr_ref):
+    for at, y in enumerate((0, 1, N - 2, N - 1)):
+        out = slice(at * N, (at + 1) * N)
+        for k in range(4):
+            abr_ref[k, out, :] = ab_ref[k, pl.ds(y, N, stride=N), :]
+        for f in range(NF):
+            wr_ref[f, out, :] = w_ref[f, pl.ds(y, N, stride=N), :]
+
+
 def boundary_kernel(
-    freq_ref, links_ref, u_ref, ab_ref, w_ref, py0_ref, py1_ref,
+    freq_ref, links_ref, u_ref, ab_ref, w_ref, abr_ref, wr_ref, py0_ref, py1_ref,
     rx0_ref, rx1_ref, ry0_ref, ry1_ref, rt0_ref, rt1_ref, keep_in_ref, send_in_ref,
     planes_ref, rows_ref, keep_ref, send_ref,
 ):
@@ -335,15 +345,15 @@
     def ab_plane(k, x):
         return ab_ref[2 * k, x * N:(x + 1) * N, :], ab_ref[2 * k + 1, x * N:(x + 1) * N, :]
 
-    def ab_row(k, y):
-        return ab_ref[2 * k, pl.ds(y, N, stride=N), :], ab_ref[2 * k + 1, pl.ds(y, N, stride=N), :]
+    def ab_row(k, at):
+        return abr_ref[2 * k, at * N:(at + 1) * N, :], abr_ref[2 * k + 1, at * N:(at + 1) * N, :]
 
     near_x = [[factors(from_x(s, X_S + k * N, N)) for k in range(2)] for s in range(2)]
     near_y = [[factors(from_y(s, X_S + k * N, N)) for k in range(2)] for s in range(2)]
     corner = [[[[factors(from_x(s, X_C + e * 4 + k * 2 + layer, 1)) for layer in range(2)]
                 for k in range(2)] for e in range(2)] for s in range(2)]
 
-    row_factors = [[[ab_row(k, y) for y in ys] for ys in ((0, 1), (N - 1, N - 2))] for k in range(2)]
+    row_factors = [[[ab_row(k, at) for at in ats] for ats in ((0, 1), (3, 2))] for k in range(2)]
 
     for fr, fi, k in pairs():
         both = (fr, fi)
@@ -387,15 +397,14 @@
                 planes_ref[f, at0 * N:(at0 + 1) * N, :] = w_ref[f, x0 * N:(x0 + 1) * N, :] + fix0[c]
                 planes_ref[f, at1 * N:(at1 + 1) * N, :] = w_ref[f, x1 * N:(x1 + 1) * N, :] + fix1[c]
         for e in range(2):
-            outer, inner = (0, 1) if e == 0 else (N - 1, N - 2)
             w0 = edge[e][1]
             rhs = [row_neighbours(w0[c]) + lane_neighbours(w0[c]) + ghost_y[e][c] for c in range(2)]
             fix0 = times(row_factors[k][e][0], *rhs)
             fix1 = times(row_factors[k][e][1], *w0)
             at0, at1 = (0, 1) if e == 0 else (3, 2)
             for c, f in enumerate(both):
-                rows_ref[f, at0 * N:(at0 + 1) * N, :] = w_ref[f, pl.ds(outer, N, stride=N), :] + fix0[c]
-                rows_ref[f, at1 * N:(at1 + 1) * N, :] = w_ref[f, pl.ds(inner, N, stride=N), :] + fix1[c]
+                rows_ref[f, at0 * N:(at0 + 1) * N, :] = wr_ref[f, at0 * N:(at0 + 1) * N, :] + fix0[c]
+                rows_ref[f, at1 * N:(at1 + 1) * N, :] = wr_ref[f, at1 * N:(at1 + 1) * N, :] + fix1[c]
     keep_ref[8 * N:, :] = keep_in_ref[...]
     send_ref[8 * N:, :] = send_in_ref[...]
     for ref, at in ((planes_ref, 0), (rows_ref, 4 * N)):
@@ -408,17 +417,17 @@
         send_ref[at:at + 4 * N, :] = jnp.where(odd_core, term_h, term_v)
 
 
-def put_boundary(step, block_ref, index, planes, rows):
+def put_boundary(step, block_ref, index, planes, rows, size=STEP):
     for at, y in enumerate((0, 1, N - 2, N - 1)):
-        block_ref[(*index, pl.ds(y, STEP, stride=N), slice(None))] = rows(at)
+        block_ref[(*index, pl.ds(y, size, stride=N), slice(None))] = rows(at)
 
     @pl.when(step == 0)
     def _():
         block_ref[(*index, slice(0, 2 * N), slice(None))] = planes(0)
 
-    @pl.when(step == N // STEP - 1)
+    @pl.when(step == N // size - 1)
     def _():
-        block_ref[(*index, slice(BLOCK - 2 * N, BLOCK), slice(None))] = planes(2 * N)
+        block_ref[(*index, slice((size - 2) * N, size * N), slice(None))] = planes(2 * N)
 
 
 def field_kernel(w_ref, planes_ref, rows_ref, out_ref):
@@ -435,28 +444,29 @@
 def gradient_kernel(mine_ref, other_ref, mine_b_ref, other_b_ref, ab_ref, sh_ref, sv_ref, gh_ref, gv_ref, total_ref):
     step = pl.program_id(0)
     odd_core = lax.rem(lax.axis_index("freq"), 2) == 1
-    block = pl.ds(pl.multiple_of(step * BLOCK, BLOCK), BLOCK)
+    block = pl.ds(pl.multiple_of(step * LAST * N, LAST * N), LAST * N)
     mask = (ab_ref[0, block, :] > 0.0).astype(f32)
     for k, (sigma_ref, out_ref) in enumerate(((sh_ref, gh_ref), (sv_ref, gv_ref))):
         first = odd_core if k == 1 else jnp.logical_not(odd_core)
-        for j in range(STEP):
-            inner = jnp.clip(step * STEP + j - 2, 0, PIECES[0] - 1)
+        for j in range(LAST):
+            inner = jnp.clip(step * LAST + j - 2, 0, PIECES[0] - 1)
             rows = pl.ds(inner * INNER, INNER)
             total_ref[j * N + 2:(j + 1) * N - 2, :] = jnp.where(first, mine_ref[rows, :], other_ref[rows, :])
 
         def boundary(rows):
             return jnp.where(first, mine_b_ref[rows, :], other_b_ref[rows, :])
 
-        @pl.when(step == N // STEP - 1)
+        @pl.when(step == N // LAST - 1)
         def _():
             for p in range(PIECES[1]):
-                at, rows = (STEP - 2 - PIECES[1] + p) * N + 2, 8 * N + p * INNER
+                at, rows = (LAST - 2 - PIECES[1] + p) * N + 2, 8 * N + p * INNER
                 total_ref[at:at + INNER, :] = boundary(slice(rows, rows + INNER))
 
         put_boundary(
             step, total_ref, (),
             lambda at: boundary(slice(at, at + 2 * N)),
-            lambda at: boundary(pl.ds(pl.multiple_of((4 + at) * N + step * STEP, 8), STEP)),
+            lambda at: boundary(pl.ds(pl.multiple_of((4 + at) * N + step * LAST, 8), LAST)),
+            LAST,
         )
         out_ref[...] = sigma_ref[block, :] * mask * total_ref[...]
 
@@ -554,15 +564,24 @@
     mine = terms[0] + swap_freq(terms[2], 1)
     partner = swap_freq(mine, 2)
 
+    abr, wr = pl.pallas_call(
+        gather_kernel,
+        in_specs=[whole()] * 2,
+        out_specs=[whole()] * 2,
+        out_shape=[pltpu.VMEM((4, 4 * N, NZ), f32), pltpu.VMEM((NF, 4 * N, NZ), f32)],
+        compiler_params=params(4),
+        cost_estimate=cost(1000, 1000),
+        name="gather",
+    )(ab, w)
     planes, rows, keep_b, send_b = pl.pallas_call(
         boundary_kernel,
-        in_specs=[smem] + [whole()] * 14,
+        in_specs=[smem] + [whole()] * 16,
         out_specs=[whole()] * 4,
         out_shape=[pltpu.VMEM((NF, 4 * N, NZ), f32)] * 2 + [sds(8 * N + PIECES[1] * INNER, NZ)] * 2,
         compiler_params=params(8),
         cost_estimate=cost(1000, 1000),
         name="boundary",
-    )(freq_index, links, u, ab, w, py0, py1, rx0, rx1, ry0, ry1, rt0, rt1, terms[1], terms[3])
+    )(freq_index, links, u, ab, w, abr, wr, py0, py1, rx0, rx1, ry0, ry1, rt0, rt1, terms[1], terms[3])
 
     forward = pl.pallas_call(
         field_kernel,
@@ -584,11 +603,11 @@
 
     grad_h, grad_v = pl.pallas_call(
         gradient_kernel,
-        grid=(steps,),
+        grid=(N // LAST,),
         in_specs=[whole()] * 7,
-        out_specs=[block2, block2],
+        out_specs=[pl.BlockSpec((LAST * N, NZ), lambda i: (i, 0))] * 2,
         out_shape=[sds(CELLS, NZ)] * 2,
-        scratch_shapes=[pltpu.VMEM((BLOCK, NZ), f32)],
+        scratch_shapes=[pltpu.VMEM((LAST * N, NZ), f32)],
         compiler_params=params(6),
         cost_estimate=cost(1000, 1000),
         name="gradient",

time: 61.8 us -> 60.9 us (0.985)
  waiting for transfers between devices: 7.37 us -> 6.31 us
    ppermute x6, waiting for transfers between devices: 2.66 us -> 1.6 us  [swap(): return lax.ppermute(value, 'sub', swap_pairs(axis, odd))]
    pallas_call x2 -> x3, Pallas kernels: 4.41 us -> 4.58 us  [the longest x1 2.27 us: on_device(): pl.pallas_call(boundary_kernel, in_specs=[smem] + [whole()] * 16, out_spe...]
  transfers between devices with their start and end apart: 12 -> 12, of which waited for: 4 -> 4; matrix products, arithmetic and copies ran while one was open for 0% -> 0% of each run, Pallas kernels for 28% -> 29%
where the time goes in v5:
time: 60.9 us; the launch traced here: 60.6 us
  starting transfers between devices  29.9 us (49%)
  Pallas kernels  22.8 us (37%)
  waiting for transfers between devices  6.31 us (10%)
  between operations  1.45 us (2%)
    ppermute x6, starting transfers between devices, swap(): return lax.ppermute(value, 'sub', swap_pairs(axis, odd))  20.2 us
    pallas_call x1, Pallas kernels, on_device(): pl.pallas_call(solve_kernel, in_specs=[smem] + [whole()] * 5, out_specs=[...  11.3 us
    ppermute x6, starting transfers between devices, swap_freq(): return lax.ppermute(value, 'freq', [(i, i ^ flip) for i in range(4)])  9.73 us
    ppermute x6, waiting for transfers between devices, swap_freq(): return lax.ppermute(value, 'freq', [(i, i ^ flip) for i in range(4)])  4.71 us
    pallas_call x1, Pallas kernels, on_device(): pl.pallas_call(strip_kernel, grid=(2,), in_specs=[smem] + [whole()] * 2 +...  3.81 us
    pallas_call x1, Pallas kernels, on_device(): pl.pallas_call(field_kernel, grid=(steps,), in_specs=[whole()] * 3, out_s...  2.31 us
    pallas_call x1, Pallas kernels, on_device(): pl.pallas_call(boundary_kernel, in_specs=[smem] + [whole()] * 16, out_spe...  2.27 us
    ppermute x6, waiting for transfers between devices, swap(): return lax.ppermute(value, 'sub', swap_pairs(axis, odd))  1.6 us
  transfers between devices with their start and end apart: 12, of which 4 were waited for; matrix products, arithmetic and copies ran while one was open for 0% of the time, Pallas kernels for 29%

profile of v5, /device:TPU:71, one launch (start us, length us, event | category | flops | bytes accessed | tf_op | source)
XLA Modules:
  0.0 60.6 jit_solution(7149888840729538802)
XLA Ops:
  1.3 0.0 copy-start
  1.3 0.0 copy-start.1
  1.3 0.0 copy-start.2
  1.3 0.0 copy-start.3
  1.3 3.8 %strips.1 = (f32[888,128]{1,0:T(8,128)S(1)}, f32[888,128]{1,0:T(8,128)S(1)}, f32[832,128]{1,0:T(8,128)S(1)}, f32[832,128]{1,0:T(8,128)S(1)}) custom-call(s32[1]{0:T(128)S(6)} %copy.10.freq_ref, s32[1,4]{1,0:T(1,128)} %links_ref.5, s32[32,32]{1,0:T(8,128)} %bitcast.27, f32[6,1024,128]{2,1,0:T(8,128)} %bitcast.12, f32[6,1024,128]{2,1,0:T(8,128)} %bitcast.15, ...), custom_call_target="tpu_custom_call" | custom-call | flops 1000000 | bytes 12582912 | tf_op jit(solution)/shard_map/strips/pallas_call | solution.py:520
  5.1 1.4 %collective-permute-start = (f32[888,128]{1,0:T(8,128)S(1)}, f32[888,128]{1,0:T(8,128)S(1)}, u32[]{:S(2)}, u32[]{:S(2)}) collective-permute-start(f32[888,128]{1,0:T(8,128)S(1)} %get-tuple-element.34), channel_id=1, source_target_pairs={{0,4},{4,0},{8,12},{12,8},{16,20},{20,16},{24,28},{28,24},{32,36},... | collective-permute-start | bytes 1363976 | tf_op jit(solution)/shard_map/ppermute | solution.py:485
  6.5 4.1 %collective-permute-start.1 = (f32[888,128]{1,0:T(8,128)S(1)}, f32[888,128]{1,0:T(8,128)S(1)}, u32[]{:S(2)}, u32[]{:S(2)}) collective-permute-start(f32[888,128]{1,0:T(8,128)S(1)} %get-tuple-element.35), channel_id=1, source_target_pairs={{4,8},{8,4},{12,16},{16,12},{20,24},{24,20},{36,40},{40,36},{44,48... | collective-permute-start | bytes 1363976 | tf_op jit(solution)/shard_map/ppermute | solution.py:485
  10.6 0.9 %collective-permute-start.2 = (f32[832,128]{1,0:T(8,128)S(1)}, f32[832,128]{1,0:T(8,128)S(1)}, u32[]{:S(2)}, u32[]{:S(2)}) collective-permute-start(f32[832,128]{1,0:T(8,128)S(1)} %get-tuple-element.32.py0_ref), channel_id=1, source_target_pairs={{0,32},{4,36},{8,40},{12,44},{16,48},{20,52},{24,56},{28,60},{32,0... | collective-permute-start | bytes 1277960 | tf_op jit(solution)/shard_map/ppermute | solution.py:485
  11.5 8.0 %collective-permute-start.3 = (f32[832,128]{1,0:T(8,128)S(1)}, f32[832,128]{1,0:T(8,128)S(1)}, u32[]{:S(2)}, u32[]{:S(2)}) collective-permute-start(f32[832,128]{1,0:T(8,128)S(1)} %get-tuple-element.33.py1_ref), channel_id=1, source_target_pairs={{32,64},{36,68},{40,72},{44,76},{48,80},{52,84},{56,88},{60,92},{6... | collective-permute-start | bytes 1277960 | tf_op jit(solution)/shard_map/ppermute | solution.py:485
  19.5 0.0 copy-done
  19.5 0.0 copy-done.1
  19.5 0.0 copy-done.2
  19.5 0.0 copy-done.3
  19.5 11.3 %solve.1 = (f32[12,1360,128]{2,1,0:T(8,128)S(1)}, f32[4,1024,128]{2,1,0:T(8,128)S(1)}, f32[12,1024,128]{2,1,0:T(8,128)S(1)}, f32[700,128]{1,0:T(8,128)S(1)}, f32...) custom-call(s32[1]{0:T(128)S(6)} %copy.10.freq_ref, s32[32,32]{1,0:T(8,128)} %bitcast.28, ...), custom_call_target="tpu_custom_call" | custom-call | flops 94371840 | bytes 41943040 | tf_op jit(solution)/shard_map/solve/pallas_call | solution.py:536
  30.8 1.9 %collective-permute-start.8 = (f32[700,128]{1,0:T(8,128)S(1)}, f32[700,128]{1,0:T(8,128)S(1)}, u32[]{:S(2)}, u32[]{:S(2)}) collective-permute-start(f32[700,128]{1,0:T(8,128)S(1)} %get-tuple-element.43), channel_id=1, source_target_pairs={{0,1},{1,0},{2,3},{3,2},{4,5},{5,4},{6,7},{7,6},{8,9},{9,8},{10,11... | collective-permute-start | bytes 1075208 | tf_op jit(solution)/shard_map/ppermute | solution.py:489
  32.7 0.0 collective-permute-done.rx0_ref
  32.7 0.0 collective-permute-done.1.rx1_ref
  32.7 0.8 %edges.1 = (f32[72,128]{1,0:T(8,128)S(1)}, f32[72,128]{1,0:T(8,128)S(1)}) custom-call(s32[1,4]{1,0:T(1,128)} %links_ref.5, f32[4,1024,128]{2,1,0:T(8,128)S(1)} %get-tuple-element.28.ab_ref, f32[888,128]{1,0:T(8,128)S(1)} %collective-permute-done.rx0_ref, f32[888,128]{1,0:T(8,128)S(1)} %collective-permute-done.1.rx1_ref), custom_call_target="tpu_custom_call" | custom-call | flops 1000 | bytes 1000 | tf_op jit(solution)/shard_map/edges/pallas_call | solution.py:551
  33.5 0.1 collective-permute-start.4
  33.6 5.8 %collective-permute-start.5 = (f32[72,128]{1,0:T(8,128)S(1)}, f32[72,128]{1,0:T(8,128)S(1)}, u32[]{:S(2)}, u32[]{:S(2)}) collective-permute-start(f32[72,128]{1,0:T(8,128)S(1)} %get-tuple-element.37), channel_id=1, source_target_pairs={{32,64},{36,68},{40,72},{44,76},{48,80},{52,84},{56,88},{60,92},{6... | collective-permute-start | bytes 110600 | tf_op jit(solution)/shard_map/ppermute | solution.py:485
  39.4 0.0 collective-permute-done.8
  39.4 0.1 add.13
  39.4 0.8 %collective-permute-start.9 = (f32[700,128]{1,0:T(8,128)S(1)}, f32[700,128]{1,0:T(8,128)S(1)}, u32[]{:S(2)}, u32[]{:S(2)}) collective-permute-start(f32[700,128]{1,0:T(8,128)S(1)} %add.13), channel_id=1, source_target_pairs={{0,2},{1,3},{2,0},{3,1},{4,6},{5,7},{6,4},{7,5},{8,10},{9,11},{10,... | collective-permute-start | bytes 1075208 | tf_op jit(solution)/shard_map/ppermute | solution.py:489
  40.3 1.0 %gather.1 = (f32[4,128,128]{2,1,0:T(8,128)S(1)}, f32[12,128,128]{2,1,0:T(8,128)S(1)}) custom-call(f32[4,1024,128]{2,1,0:T(8,128)S(1)} %get-tuple-element.28.ab_ref, f32[12,1024,128]{2,1,0:T(8,128)S(1)} %get-tuple-element.29.w_ref), custom_call_target="tpu_custom_call" | custom-call | flops 1000 | bytes 1000 | tf_op jit(solution)/shard_map/gather/pallas_call | solution.py:567
  41.3 0.0 collective-permute-done.2.ry0_ref
  41.3 0.0 collective-permute-done.3.ry1_ref
  41.3 0.0 collective-permute-done.4.rt0_ref
  41.3 1.6 %collective-permute-done.5.rt1_ref = f32[72,128]{1,0:T(8,128)S(1)} collective-permute-done((f32[72,128]{1,0:T(8,128)S(1)}, f32[72,128]{1,0:T(8,128)S(1)}, u32[]{:S(2)}, u32[]{:S(2)}) %collective-permute-start.5) | collective-permute-done | bytes 36896 | tf_op jit(solution)/shard_map/ppermute | solution.py:485
  42.9 2.3 %boundary.1 = (f32[12,128,128]{2,1,0:T(8,128)S(1)}, f32[12,128,128]{2,1,0:T(8,128)S(1)}, f32[340,128]{1,0:T(8,128)S(1)}, f32[340,128]{1,0:T(8,128)S(1)}) custom-call(s32[1]{0:T(128)S(6)} %copy.10.freq_ref, s32[1,4]{1,0:T(1,128)} %links_ref.5, f32[12,1360,128]{2,1,0:T(8,128)S(1)} %get-tuple-element.27.u_ref, f32[4,1024,128]{2,1,0:T(8,128)S(1)} %get-tuple-element.28.ab_ref, ...), custom_call_target="tpu_custom_call" | custom-call | flops 1000 | bytes 1000 | tf_op jit(solution)/shard_map/boundary/pallas_call | solution.py:576
  45.2 2.5 %collective-permute-start.6 = (f32[340,128]{1,0:T(8,128)S(1)}, f32[340,128]{1,0:T(8,128)S(1)}, u32[]{:S(2)}, u32[]{:S(2)}) collective-permute-start(f32[340,128]{1,0:T(8,128)S(1)} %get-tuple-element.41), channel_id=1, source_target_pairs={{0,1},{1,0},{2,3},{3,2},{4,5},{5,4},{6,7},{7,6},{8,9},{9,8},{10,11... | collective-permute-start | bytes 522248 | tf_op jit(solution)/shard_map/ppermute | solution.py:489
  47.7 1.0 %collective-permute-done.6 = f32[340,128]{1,0:T(8,128)S(1)} collective-permute-done((f32[340,128]{1,0:T(8,128)S(1)}, f32[340,128]{1,0:T(8,128)S(1)}, u32[]{:S(2)}, u32[]{:S(2)}) %collective-permute-start.6) | collective-permute-done | bytes 174112 | tf_op jit(solution)/shard_map/ppermute | solution.py:489
  48.8 3.5 %collective-permute-start.7 = (f32[340,128]{1,0:T(8,128)S(1)}, f32[340,128]{1,0:T(8,128)S(1)}, u32[]{:S(2)}, u32[]{:S(2)}) collective-permute-start(f32[340,128]{1,0:T(8,128)S(1)} %add.12), channel_id=1, source_target_pairs={{0,2},{1,3},{2,0},{3,1},{4,6},{5,7},{6,4},{7,5},{8,10},{9,11},{10,... | collective-permute-start | bytes 522248 | tf_op jit(solution)/shard_map/ppermute | solution.py:489
  52.2 2.3 %field.1 = f32[6,1024,128]{2,1,0:T(8,128)} custom-call(f32[12,1024,128]{2,1,0:T(8,128)S(1)} %get-tuple-element.29.w_ref, f32[12,128,128]{2,1,0:T(8,128)S(1)} %get-tuple-element.44.planes_ref, f32[12,128,128]{2,1,0:T(8,128)S(1)} %get-tuple-element.45.rows_ref), custom_call_target="tpu_custom_call" | custom-call | flops 1000 | bytes 1000 | tf_op jit(solution)/shard_map/field/pallas_call | solution.py:586
  54.5 0.0 collective-permute-done.9
  54.5 2.2 %collective-permute-done.7 = f32[340,128]{1,0:T(8,128)S(1)} collective-permute-done((f32[340,128]{1,0:T(8,128)S(1)}, f32[340,128]{1,0:T(8,128)S(1)}, u32[]{:S(2)}, u32[]{:S(2)}) %collective-permute-start.7) | collective-permute-done | bytes 174112 | tf_op jit(solution)/shard_map/ppermute | solution.py:489
  56.8 1.0 %collective-permute-start.10 = (f32[700,128]{1,0:T(8,128)S(1)}, f32[700,128]{1,0:T(8,128)S(1)}, u32[]{:S(2)}, u32[]{:S(2)}) collective-permute-start(f32[700,128]{1,0:T(8,128)S(1)} %add.14.mine_ref), channel_id=1, source_target_pairs={{0,1},{1,0},{2,3},{3,2},{4,5},{5,4},{6,7},{7,6},{8,9},{9,8},{10,11... | collective-permute-start | bytes 1075208 | tf_op jit(solution)/shard_map/ppermute | solution.py:489
  57.8 0.1 collective-permute-start.11
  57.9 1.4 %collective-permute-done.11.other_b_ref = f32[340,128]{1,0:T(8,128)S(1)} collective-permute-done((f32[340,128]{1,0:T(8,128)S(1)}, f32[340,128]{1,0:T(8,128)S(1)}, u32[]{:S(2)}, u32[]{:S(2)}) %collective-permute-start.11) | collective-permute-done | bytes 174112 | tf_op jit(solution)/shard_map/ppermute | solution.py:489
  59.3 0.0 collective-permute-done.10.other_ref
  59.3 1.3 %gradient.1 = (f32[1024,128]{1,0:T(8,128)}, f32[1024,128]{1,0:T(8,128)}) custom-call(f32[700,128]{1,0:T(8,128)S(1)} %add.14.mine_ref, f32[700,128]{1,0:T(8,128)S(1)} %collective-permute-done.10.other_ref, f32[340,128]{1,0:T(8,128)S(1)} %add.15.mine_b_ref, f32[340,128]{1,0:T(8,128)S(1)} %collective-permute-done.11.other_b_ref, ...), custom_call_target="tpu_custom_call" | custom-call | flops 1000 | bytes 1000 | tf_op jit(solution)/shard_map/gradient/pallas_call | solution.py:604
  (3 shorter events, 0.1 us)
Async XLA Ops:
  1.3 18.2 %copy-start = (f32[1,2,3,32,32,128]{5,4,3,2,1,0:T(8,128)S(1)}, f32[1,2,3,32,32,128]{5,4,3,2,1,0:T(8,128)}, u32[]{:S(2)}) copy-start(f32[1,2,3,32,32,128]{5,4,3,2,1,0:T(8,128)} %param.7) | copy-start | bytes 9437188
  1.3 18.2 %copy-start.1 = (f32[1,1,2,3,32,32,128]{6,5,4,3,2,1,0:T(8,128)S(1)}, f32[1,1,2,3,32,32,128]{6,5,4,3,2,1,0:T(8,128)}, u32[]{:S(2)}) copy-start(f32[1,1,2,3,32,32,128]{6,5,4,3,2,1,0:T(8,128)} %param.8) | copy-start | bytes 9437188
  1.3 18.2 %copy-start.2 = (f32[1,32,32,128]{3,2,1,0:T(8,128)S(1)}, f32[1,32,32,128]{3,2,1,0:T(8,128)}, u32[]{:S(2)}) copy-start(f32[1,32,32,128]{3,2,1,0:T(8,128)} %param.9) | copy-start | bytes 1572868
  1.3 18.2 %copy-start.3 = (f32[1,32,32,128]{3,2,1,0:T(8,128)S(1)}, f32[1,32,32,128]{3,2,1,0:T(8,128)}, u32[]{:S(2)}) copy-start(f32[1,32,32,128]{3,2,1,0:T(8,128)} %param.10) | copy-start | bytes 1572868
  5.1 27.5 %collective-permute-start = (f32[888,128]{1,0:T(8,128)S(1)}, f32[888,128]{1,0:T(8,128)S(1)}, u32[]{:S(2)}, u32[]{:S(2)}) collective-permute-start(f32[888,128]{1,0:T(8,128)S(1)} %get-tuple-element.34), channel_id=1, source_target_pairs={{0,4},{4,0},{8,12},{12,8},{16,20},{20,16},{24,28},{28,24},{32,36},... | collective-permute-start | bytes 1363976 | tf_op jit(solution)/shard_map/ppermute | solution.py:485
  6.5 26.2 %collective-permute-start.1 = (f32[888,128]{1,0:T(8,128)S(1)}, f32[888,128]{1,0:T(8,128)S(1)}, u32[]{:S(2)}, u32[]{:S(2)}) collective-permute-start(f32[888,128]{1,0:T(8,128)S(1)} %get-tuple-element.35), channel_id=1, source_target_pairs={{4,8},{8,4},{12,16},{16,12},{20,24},{24,20},{36,40},{40,36},{44,48... | collective-permute-start | bytes 1363976 | tf_op jit(solution)/shard_map/ppermute | solution.py:485
  10.6 30.7 %collective-permute-start.2 = (f32[832,128]{1,0:T(8,128)S(1)}, f32[832,128]{1,0:T(8,128)S(1)}, u32[]{:S(2)}, u32[]{:S(2)}) collective-permute-start(f32[832,128]{1,0:T(8,128)S(1)} %get-tuple-element.32.py0_ref), channel_id=1, source_target_pairs={{0,32},{4,36},{8,40},{12,44},{16,48},{20,52},{24,56},{28,60},{32,0... | collective-permute-start | bytes 1277960 | tf_op jit(solution)/shard_map/ppermute | solution.py:485
  11.5 29.8 %collective-permute-start.3 = (f32[832,128]{1,0:T(8,128)S(1)}, f32[832,128]{1,0:T(8,128)S(1)}, u32[]{:S(2)}, u32[]{:S(2)}) collective-permute-start(f32[832,128]{1,0:T(8,128)S(1)} %get-tuple-element.33.py1_ref), channel_id=1, source_target_pairs={{32,64},{36,68},{40,72},{44,76},{48,80},{52,84},{56,88},{60,92},{6... | collective-permute-start | bytes 1277960 | tf_op jit(solution)/shard_map/ppermute | solution.py:485
  30.8 8.6 %collective-permute-start.8 = (f32[700,128]{1,0:T(8,128)S(1)}, f32[700,128]{1,0:T(8,128)S(1)}, u32[]{:S(2)}, u32[]{:S(2)}) collective-permute-start(f32[700,128]{1,0:T(8,128)S(1)} %get-tuple-element.43), channel_id=1, source_target_pairs={{0,1},{1,0},{2,3},{3,2},{4,5},{5,4},{6,7},{7,6},{8,9},{9,8},{10,11... | collective-permute-start | bytes 1075208 | tf_op jit(solution)/shard_map/ppermute | solution.py:489
  33.5 7.8 %collective-permute-start.4 = (f32[72,128]{1,0:T(8,128)S(1)}, f32[72,128]{1,0:T(8,128)S(1)}, u32[]{:S(2)}, u32[]{:S(2)}) collective-permute-start(f32[72,128]{1,0:T(8,128)S(1)} %get-tuple-element.36), channel_id=1, source_target_pairs={{0,32},{4,36},{8,40},{12,44},{16,48},{20,52},{24,56},{28,60},{32,0... | collective-permute-start | bytes 110600 | tf_op jit(solution)/shard_map/ppermute | solution.py:485
  33.6 9.3 %collective-permute-start.5 = (f32[72,128]{1,0:T(8,128)S(1)}, f32[72,128]{1,0:T(8,128)S(1)}, u32[]{:S(2)}, u32[]{:S(2)}) collective-permute-start(f32[72,128]{1,0:T(8,128)S(1)} %get-tuple-element.37), channel_id=1, source_target_pairs={{32,64},{36,68},{40,72},{44,76},{48,80},{52,84},{56,88},{60,92},{6... | collective-permute-start | bytes 110600 | tf_op jit(solution)/shard_map/ppermute | solution.py:485
  39.4 15.1 %collective-permute-start.9 = (f32[700,128]{1,0:T(8,128)S(1)}, f32[700,128]{1,0:T(8,128)S(1)}, u32[]{:S(2)}, u32[]{:S(2)}) collective-permute-start(f32[700,128]{1,0:T(8,128)S(1)} %add.13), channel_id=1, source_target_pairs={{0,2},{1,3},{2,0},{3,1},{4,6},{5,7},{6,4},{7,5},{8,10},{9,11},{10,... | collective-permute-start | bytes 1075208 | tf_op jit(solution)/shard_map/ppermute | solution.py:489
  45.2 3.5 %collective-permute-start.6 = (f32[340,128]{1,0:T(8,128)S(1)}, f32[340,128]{1,0:T(8,128)S(1)}, u32[]{:S(2)}, u32[]{:S(2)}) collective-permute-start(f32[340,128]{1,0:T(8,128)S(1)} %get-tuple-element.41), channel_id=1, source_target_pairs={{0,1},{1,0},{2,3},{3,2},{4,5},{5,4},{6,7},{7,6},{8,9},{9,8},{10,11... | collective-permute-start | bytes 522248 | tf_op jit(solution)/shard_map/ppermute | solution.py:489
  48.8 8.0 %collective-permute-start.7 = (f32[340,128]{1,0:T(8,128)S(1)}, f32[340,128]{1,0:T(8,128)S(1)}, u32[]{:S(2)}, u32[]{:S(2)}) collective-permute-start(f32[340,128]{1,0:T(8,128)S(1)} %add.12), channel_id=1, source_target_pairs={{0,2},{1,3},{2,0},{3,1},{4,6},{5,7},{6,4},{7,5},{8,10},{9,11},{10,... | collective-permute-start | bytes 522248 | tf_op jit(solution)/shard_map/ppermute | solution.py:489
  56.8 2.5 %collective-permute-start.10 = (f32[700,128]{1,0:T(8,128)S(1)}, f32[700,128]{1,0:T(8,128)S(1)}, u32[]{:S(2)}, u32[]{:S(2)}) collective-permute-start(f32[700,128]{1,0:T(8,128)S(1)} %add.14.mine_ref), channel_id=1, source_target_pairs={{0,1},{1,0},{2,3},{3,2},{4,5},{5,4},{6,7},{7,6},{8,9},{9,8},{10,11... | collective-permute-start | bytes 1075208 | tf_op jit(solution)/shard_map/ppermute | solution.py:489
  57.8 1.5 %collective-permute-start.11 = (f32[340,128]{1,0:T(8,128)S(1)}, f32[340,128]{1,0:T(8,128)S(1)}, u32[]{:S(2)}, u32[]{:S(2)}) collective-permute-start(f32[340,128]{1,0:T(8,128)S(1)} %add.15.mine_b_ref), channel_id=1, source_target_pairs={{0,1},{1,0},{2,3},{3,2},{4,5},{5,4},{6,7},{7,6},{8,9},{9,8},{10,11... | collective-permute-start | bytes 522248 | tf_op jit(solution)/shard_map/ppermute | solution.py:489

commit v6 on v5

--- a/solution.py
+++ b/solution.py
@@ -10,6 +10,7 @@
 N = 32
 NZ = 128
 PIECES = (25, 3)
+PIECE_ROWS = (25 * 28 + 4, 3 * 28 + 4)
 INNER = N - 4
 PLANE = 40
 ROWS = 34 * PLANE
@@ -186,7 +187,7 @@
     @pl.when(step == 1)
     def _():
         side(1, xh_ref, yh_ref)
-        low, high = xl_ref[...], xh_ref[...]
+        low, high = xl_ref[0:X_ROWS, :], xh_ref[0:X_ROWS, :]
         px0_ref[...] = jnp.where(odd_x, low, high)
         px1_ref[...] = jnp.where(odd_x, high, low)
         low, high = yl_ref[...], yh_ref[...]
@@ -298,8 +299,8 @@
             here = pl.ds(j * INNER, INNER)
             term = last_update(first + j)
             term_h, term_v = scale * term[0], scale * term[1]
-            keep_ref[here, :] = jnp.where(odd_core, term_v, term_h)[2:N - 2, :]
-            send_ref[here, :] = jnp.where(odd_core, term_h, term_v)[2:N - 2, :]
+            keep_ref[here, :] = pltpu.roll(jnp.where(odd_core, term_v, term_h), N - 2, 0)[0:INNER, :]
+            send_ref[here, :] = pltpu.roll(jnp.where(odd_core, term_h, term_v), N - 2, 0)[0:INNER, :]
             return carry
 
         lax.fori_loop(0, size, plane, 0, unroll=4)
@@ -523,7 +524,7 @@
         in_specs=[smem] + [whole()] * 2 + [field_x, field_x, sigma_x, sigma_x, field_y, field_y, sigma_y, sigma_y],
         out_specs=[whole()] * 4,
         out_shape=[sds(X_ROWS, NZ), sds(X_ROWS, NZ), sds(Y_ROWS, NZ), sds(Y_ROWS, NZ)],
-        scratch_shapes=[pltpu.VMEM((X_ROWS, NZ), f32)] * 2 + [pltpu.VMEM((Y_ROWS, NZ), f32)] * 2,
+        scratch_shapes=[pltpu.VMEM((X_ROWS + 8, NZ), f32)] * 2 + [pltpu.VMEM((Y_ROWS, NZ), f32)] * 2,
         compiler_params=params(14),
         cost_estimate=cost(10**6, 12 * 2**20),
         name="strips",
@@ -539,7 +540,7 @@
         out_specs=[whole()] * (3 + 2 * len(PIECES)),
         out_shape=[
             pltpu.VMEM((NF, ROWS, NZ), f32), pltpu.VMEM((4, CELLS, NZ), f32), pltpu.VMEM((NF, CELLS, NZ), f32),
-        ] + [sds(size * INNER, NZ) for size in PIECES] * 2,
+        ] + [sds(size, NZ) for size in PIECE_ROWS] * 2,
         scratch_shapes=[pltpu.VMEM((NF, ROWS, NZ), f32)],
         compiler_params=params(24),
         cost_estimate=cost(60 * NF * CELLS * NZ, 40 * 2**20),
@@ -577,7 +578,7 @@
         boundary_kernel,
         in_specs=[smem] + [whole()] * 16,
         out_specs=[whole()] * 4,
-        out_shape=[pltpu.VMEM((NF, 4 * N, NZ), f32)] * 2 + [sds(8 * N + PIECES[1] * INNER, NZ)] * 2,
+        out_shape=[pltpu.VMEM((NF, 4 * N, NZ), f32)] * 2 + [sds(8 * N + PIECE_ROWS[1], NZ)] * 2,
         compiler_params=params(8),
         cost_estimate=cost(1000, 1000),
         name="boundary",

time: 60.9 us -> 60.9 us (level)
  no operation moved by 1% of the time
where the time goes in v6:
time: 60.9 us; the launch traced here: 60.6 us
  starting transfers between devices  29.9 us (49%)
  Pallas kernels  22.8 us (37%)
  waiting for transfers between devices  6.31 us (10%)
  between operations  1.45 us (2%)
    ppermute x6, starting transfers between devices, swap(): return lax.ppermute(value, 'sub', swap_pairs(axis, odd))  20.2 us
    pallas_call x1, Pallas kernels, on_device(): pl.pallas_call(solve_kernel, in_specs=[smem] + [whole()] * 5, out_specs=[...  11.3 us
    ppermute x6, starting transfers between devices, swap_freq(): return lax.ppermute(value, 'freq', [(i, i ^ flip) for i in range(4)])  9.73 us
    ppermute x6, waiting for transfers between devices, swap_freq(): return lax.ppermute(value, 'freq', [(i, i ^ flip) for i in range(4)])  4.71 us
    pallas_call x1, Pallas kernels, on_device(): pl.pallas_call(strip_kernel, grid=(2,), in_specs=[smem] + [whole()] * 2 +...  3.8 us
    pallas_call x1, Pallas kernels, on_device(): pl.pallas_call(field_kernel, grid=(steps,), in_specs=[whole()] * 3, out_s...  2.31 us
    pallas_call x1, Pallas kernels, on_device(): pl.pallas_call(boundary_kernel, in_specs=[smem] + [whole()] * 16, out_spe...  2.27 us
    ppermute x6, waiting for transfers between devices, swap(): return lax.ppermute(value, 'sub', swap_pairs(axis, odd))  1.6 us
  transfers between devices with their start and end apart: 12, of which 4 were waited for; matrix products, arithmetic and copies ran while one was open for 0% of the time, Pallas kernels for 29%

profile of v6, /device:TPU:71, one launch (start us, length us, event | category | flops | bytes accessed | tf_op | source)
XLA Modules:
  0.0 60.6 jit_solution(16376539934830788985)
XLA Ops:
  1.3 0.0 copy-start
  1.3 0.0 copy-start.1
  1.3 0.0 copy-start.2
  1.3 0.0 copy-start.3
  1.3 3.8 %strips.1 = (f32[888,128]{1,0:T(8,128)S(1)}, f32[888,128]{1,0:T(8,128)S(1)}, f32[832,128]{1,0:T(8,128)S(1)}, f32[832,128]{1,0:T(8,128)S(1)}) custom-call(s32[1]{0:T(128)S(6)} %copy.10.freq_ref, s32[1,4]{1,0:T(1,128)} %links_ref.5, s32[32,32]{1,0:T(8,128)} %bitcast.27, f32[6,1024,128]{2,1,0:T(8,128)} %bitcast.12, f32[6,1024,128]{2,1,0:T(8,128)} %bitcast.15, ...), custom_call_target="tpu_custom_call" | custom-call | flops 1000000 | bytes 12582912 | tf_op jit(solution)/shard_map/strips/pallas_call | solution.py:521
  5.1 1.4 %collective-permute-start = (f32[888,128]{1,0:T(8,128)S(1)}, f32[888,128]{1,0:T(8,128)S(1)}, u32[]{:S(2)}, u32[]{:S(2)}) collective-permute-start(f32[888,128]{1,0:T(8,128)S(1)} %get-tuple-element.34), channel_id=1, source_target_pairs={{0,4},{4,0},{8,12},{12,8},{16,20},{20,16},{24,28},{28,24},{32,36},... | collective-permute-start | bytes 1363976 | tf_op jit(solution)/shard_map/ppermute | solution.py:486
  6.5 4.1 %collective-permute-start.1 = (f32[888,128]{1,0:T(8,128)S(1)}, f32[888,128]{1,0:T(8,128)S(1)}, u32[]{:S(2)}, u32[]{:S(2)}) collective-permute-start(f32[888,128]{1,0:T(8,128)S(1)} %get-tuple-element.35), channel_id=1, source_target_pairs={{4,8},{8,4},{12,16},{16,12},{20,24},{24,20},{36,40},{40,36},{44,48... | collective-permute-start | bytes 1363976 | tf_op jit(solution)/shard_map/ppermute | solution.py:486
  10.6 0.9 %collective-permute-start.2 = (f32[832,128]{1,0:T(8,128)S(1)}, f32[832,128]{1,0:T(8,128)S(1)}, u32[]{:S(2)}, u32[]{:S(2)}) collective-permute-start(f32[832,128]{1,0:T(8,128)S(1)} %get-tuple-element.32.py0_ref), channel_id=1, source_target_pairs={{0,32},{4,36},{8,40},{12,44},{16,48},{20,52},{24,56},{28,60},{32,0... | collective-permute-start | bytes 1277960 | tf_op jit(solution)/shard_map/ppermute | solution.py:486
  11.5 8.0 %collective-permute-start.3 = (f32[832,128]{1,0:T(8,128)S(1)}, f32[832,128]{1,0:T(8,128)S(1)}, u32[]{:S(2)}, u32[]{:S(2)}) collective-permute-start(f32[832,128]{1,0:T(8,128)S(1)} %get-tuple-element.33.py1_ref), channel_id=1, source_target_pairs={{32,64},{36,68},{40,72},{44,76},{48,80},{52,84},{56,88},{60,92},{6... | collective-permute-start | bytes 1277960 | tf_op jit(solution)/shard_map/ppermute | solution.py:486
  19.5 0.0 copy-done
  19.5 0.0 copy-done.1
  19.5 0.0 copy-done.2
  19.5 0.0 copy-done.3
  19.5 11.3 %solve.1 = (f32[12,1360,128]{2,1,0:T(8,128)S(1)}, f32[4,1024,128]{2,1,0:T(8,128)S(1)}, f32[12,1024,128]{2,1,0:T(8,128)S(1)}, f32[704,128]{1,0:T(8,128)S(1)}, f32...) custom-call(s32[1]{0:T(128)S(6)} %copy.10.freq_ref, s32[32,32]{1,0:T(8,128)} %bitcast.28, ...), custom_call_target="tpu_custom_call" | custom-call | flops 94371840 | bytes 41943040 | tf_op jit(solution)/shard_map/solve/pallas_call | solution.py:537
  30.8 1.9 %collective-permute-start.8 = (f32[704,128]{1,0:T(8,128)S(1)}, f32[704,128]{1,0:T(8,128)S(1)}, u32[]{:S(2)}, u32[]{:S(2)}) collective-permute-start(f32[704,128]{1,0:T(8,128)S(1)} %get-tuple-element.43), channel_id=1, source_target_pairs={{0,1},{1,0},{2,3},{3,2},{4,5},{5,4},{6,7},{7,6},{8,9},{9,8},{10,11... | collective-permute-start | bytes 1081352 | tf_op jit(solution)/shard_map/ppermute | solution.py:490
  32.7 0.0 collective-permute-done.rx0_ref
  32.7 0.0 collective-permute-done.1.rx1_ref
  32.7 0.8 %edges.1 = (f32[72,128]{1,0:T(8,128)S(1)}, f32[72,128]{1,0:T(8,128)S(1)}) custom-call(s32[1,4]{1,0:T(1,128)} %links_ref.5, f32[4,1024,128]{2,1,0:T(8,128)S(1)} %get-tuple-element.28.ab_ref, f32[888,128]{1,0:T(8,128)S(1)} %collective-permute-done.rx0_ref, f32[888,128]{1,0:T(8,128)S(1)} %collective-permute-done.1.rx1_ref), custom_call_target="tpu_custom_call" | custom-call | flops 1000 | bytes 1000 | tf_op jit(solution)/shard_map/edges/pallas_call | solution.py:552
  33.5 0.1 collective-permute-start.4
  33.6 5.8 %collective-permute-start.5 = (f32[72,128]{1,0:T(8,128)S(1)}, f32[72,128]{1,0:T(8,128)S(1)}, u32[]{:S(2)}, u32[]{:S(2)}) collective-permute-start(f32[72,128]{1,0:T(8,128)S(1)} %get-tuple-element.37), channel_id=1, source_target_pairs={{32,64},{36,68},{40,72},{44,76},{48,80},{52,84},{56,88},{60,92},{6... | collective-permute-start | bytes 110600 | tf_op jit(solution)/shard_map/ppermute | solution.py:486
  39.4 0.0 collective-permute-done.8
  39.4 0.1 add.13
  39.4 0.8 %collective-permute-start.9 = (f32[704,128]{1,0:T(8,128)S(1)}, f32[704,128]{1,0:T(8,128)S(1)}, u32[]{:S(2)}, u32[]{:S(2)}) collective-permute-start(f32[704,128]{1,0:T(8,128)S(1)} %add.13), channel_id=1, source_target_pairs={{0,2},{1,3},{2,0},{3,1},{4,6},{5,7},{6,4},{7,5},{8,10},{9,11},{10,... | collective-permute-start | bytes 1081352 | tf_op jit(solution)/shard_map/ppermute | solution.py:490
  40.3 1.0 %gather.1 = (f32[4,128,128]{2,1,0:T(8,128)S(1)}, f32[12,128,128]{2,1,0:T(8,128)S(1)}) custom-call(f32[4,1024,128]{2,1,0:T(8,128)S(1)} %get-tuple-element.28.ab_ref, f32[12,1024,128]{2,1,0:T(8,128)S(1)} %get-tuple-element.29.w_ref), custom_call_target="tpu_custom_call" | custom-call | flops 1000 | bytes 1000 | tf_op jit(solution)/shard_map/gather/pallas_call | solution.py:568
  41.3 0.0 collective-permute-done.2.ry0_ref
  41.3 0.0 collective-permute-done.3.ry1_ref
  41.3 0.0 collective-permute-done.4.rt0_ref
  41.3 1.6 %collective-permute-done.5.rt1_ref = f32[72,128]{1,0:T(8,128)S(1)} collective-permute-done((f32[72,128]{1,0:T(8,128)S(1)}, f32[72,128]{1,0:T(8,128)S(1)}, u32[]{:S(2)}, u32[]{:S(2)}) %collective-permute-start.5) | collective-permute-done | bytes 36896 | tf_op jit(solution)/shard_map/ppermute | solution.py:486
  42.9 2.3 %boundary.1 = (f32[12,128,128]{2,1,0:T(8,128)S(1)}, f32[12,128,128]{2,1,0:T(8,128)S(1)}, f32[344,128]{1,0:T(8,128)S(1)}, f32[344,128]{1,0:T(8,128)S(1)}) custom-call(s32[1]{0:T(128)S(6)} %copy.10.freq_ref, s32[1,4]{1,0:T(1,128)} %links_ref.5, f32[12,1360,128]{2,1,0:T(8,128)S(1)} %get-tuple-element.27.u_ref, f32[4,1024,128]{2,1,0:T(8,128)S(1)} %get-tuple-element.28.ab_ref, ...), custom_call_target="tpu_custom_call" | custom-call | flops 1000 | bytes 1000 | tf_op jit(solution)/shard_map/boundary/pallas_call | solution.py:577
  45.2 2.5 %collective-permute-start.6 = (f32[344,128]{1,0:T(8,128)S(1)}, f32[344,128]{1,0:T(8,128)S(1)}, u32[]{:S(2)}, u32[]{:S(2)}) collective-permute-start(f32[344,128]{1,0:T(8,128)S(1)} %get-tuple-element.41), channel_id=1, source_target_pairs={{0,1},{1,0},{2,3},{3,2},{4,5},{5,4},{6,7},{7,6},{8,9},{9,8},{10,11... | collective-permute-start | bytes 528392 | tf_op jit(solution)/shard_map/ppermute | solution.py:490
  47.7 1.0 %collective-permute-done.6 = f32[344,128]{1,0:T(8,128)S(1)} collective-permute-done((f32[344,128]{1,0:T(8,128)S(1)}, f32[344,128]{1,0:T(8,128)S(1)}, u32[]{:S(2)}, u32[]{:S(2)}) %collective-permute-start.6) | collective-permute-done | bytes 176160 | tf_op jit(solution)/shard_map/ppermute | solution.py:490
  48.8 3.5 %collective-permute-start.7 = (f32[344,128]{1,0:T(8,128)S(1)}, f32[344,128]{1,0:T(8,128)S(1)}, u32[]{:S(2)}, u32[]{:S(2)}) collective-permute-start(f32[344,128]{1,0:T(8,128)S(1)} %add.12), channel_id=1, source_target_pairs={{0,2},{1,3},{2,0},{3,1},{4,6},{5,7},{6,4},{7,5},{8,10},{9,11},{10,... | collective-permute-start | bytes 528392 | tf_op jit(solution)/shard_map/ppermute | solution.py:490
  52.2 2.3 %field.1 = f32[6,1024,128]{2,1,0:T(8,128)} custom-call(f32[12,1024,128]{2,1,0:T(8,128)S(1)} %get-tuple-element.29.w_ref, f32[12,128,128]{2,1,0:T(8,128)S(1)} %get-tuple-element.44.planes_ref, f32[12,128,128]{2,1,0:T(8,128)S(1)} %get-tuple-element.45.rows_ref), custom_call_target="tpu_custom_call" | custom-call | flops 1000 | bytes 1000 | tf_op jit(solution)/shard_map/field/pallas_call | solution.py:587
  54.5 0.0 collective-permute-done.9
  54.5 2.2 %collective-permute-done.7 = f32[344,128]{1,0:T(8,128)S(1)} collective-permute-done((f32[344,128]{1,0:T(8,128)S(1)}, f32[344,128]{1,0:T(8,128)S(1)}, u32[]{:S(2)}, u32[]{:S(2)}) %collective-permute-start.7) | collective-permute-done | bytes 176160 | tf_op jit(solution)/shard_map/ppermute | solution.py:490
  56.8 1.0 %collective-permute-start.10 = (f32[704,128]{1,0:T(8,128)S(1)}, f32[704,128]{1,0:T(8,128)S(1)}, u32[]{:S(2)}, u32[]{:S(2)}) collective-permute-start(f32[704,128]{1,0:T(8,128)S(1)} %add.14.mine_ref), channel_id=1, source_target_pairs={{0,1},{1,0},{2,3},{3,2},{4,5},{5,4},{6,7},{7,6},{8,9},{9,8},{10,11... | collective-permute-start | bytes 1081352 | tf_op jit(solution)/shard_map/ppermute | solution.py:490
  57.8 0.1 collective-permute-start.11
  57.9 1.4 %collective-permute-done.11.other_b_ref = f32[344,128]{1,0:T(8,128)S(1)} collective-permute-done((f32[344,128]{1,0:T(8,128)S(1)}, f32[344,128]{1,0:T(8,128)S(1)}, u32[]{:S(2)}, u32[]{:S(2)}) %collective-permute-start.11) | collective-permute-done | bytes 176160 | tf_op jit(solution)/shard_map/ppermute | solution.py:490
  59.3 0.0 collective-permute-done.10.other_ref
  59.3 1.3 %gradient.1 = (f32[1024,128]{1,0:T(8,128)}, f32[1024,128]{1,0:T(8,128)}) custom-call(f32[704,128]{1,0:T(8,128)S(1)} %add.14.mine_ref, f32[704,128]{1,0:T(8,128)S(1)} %collective-permute-done.10.other_ref, f32[344,128]{1,0:T(8,128)S(1)} %add.15.mine_b_ref, f32[344,128]{1,0:T(8,128)S(1)} %collective-permute-done.11.other_b_ref, ...), custom_call_target="tpu_custom_call" | custom-call | flops 1000 | bytes 1000 | tf_op jit(solution)/shard_map/gradient/pallas_call | solution.py:605
  (3 shorter events, 0.1 us)
Async XLA Ops:
  1.3 18.2 %copy-start = (f32[1,2,3,32,32,128]{5,4,3,2,1,0:T(8,128)S(1)}, f32[1,2,3,32,32,128]{5,4,3,2,1,0:T(8,128)}, u32[]{:S(2)}) copy-start(f32[1,2,3,32,32,128]{5,4,3,2,1,0:T(8,128)} %param.7) | copy-start | bytes 9437188
  1.3 18.2 %copy-start.1 = (f32[1,1,2,3,32,32,128]{6,5,4,3,2,1,0:T(8,128)S(1)}, f32[1,1,2,3,32,32,128]{6,5,4,3,2,1,0:T(8,128)}, u32[]{:S(2)}) copy-start(f32[1,1,2,3,32,32,128]{6,5,4,3,2,1,0:T(8,128)} %param.8) | copy-start | bytes 9437188
  1.3 18.2 %copy-start.2 = (f32[1,32,32,128]{3,2,1,0:T(8,128)S(1)}, f32[1,32,32,128]{3,2,1,0:T(8,128)}, u32[]{:S(2)}) copy-start(f32[1,32,32,128]{3,2,1,0:T(8,128)} %param.9) | copy-start | bytes 1572868
  1.3 18.2 %copy-start.3 = (f32[1,32,32,128]{3,2,1,0:T(8,128)S(1)}, f32[1,32,32,128]{3,2,1,0:T(8,128)}, u32[]{:S(2)}) copy-start(f32[1,32,32,128]{3,2,1,0:T(8,128)} %param.10) | copy-start | bytes 1572868
  5.1 27.5 %collective-permute-start = (f32[888,128]{1,0:T(8,128)S(1)}, f32[888,128]{1,0:T(8,128)S(1)}, u32[]{:S(2)}, u32[]{:S(2)}) collective-permute-start(f32[888,128]{1,0:T(8,128)S(1)} %get-tuple-element.34), channel_id=1, source_target_pairs={{0,4},{4,0},{8,12},{12,8},{16,20},{20,16},{24,28},{28,24},{32,36},... | collective-permute-start | bytes 1363976 | tf_op jit(solution)/shard_map/ppermute | solution.py:486
  6.5 26.2 %collective-permute-start.1 = (f32[888,128]{1,0:T(8,128)S(1)}, f32[888,128]{1,0:T(8,128)S(1)}, u32[]{:S(2)}, u32[]{:S(2)}) collective-permute-start(f32[888,128]{1,0:T(8,128)S(1)} %get-tuple-element.35), channel_id=1, source_target_pairs={{4,8},{8,4},{12,16},{16,12},{20,24},{24,20},{36,40},{40,36},{44,48... | collective-permute-start | bytes 1363976 | tf_op jit(solution)/shard_map/ppermute | solution.py:486
  10.6 30.7 %collective-permute-start.2 = (f32[832,128]{1,0:T(8,128)S(1)}, f32[832,128]{1,0:T(8,128)S(1)}, u32[]{:S(2)}, u32[]{:S(2)}) collective-permute-start(f32[832,128]{1,0:T(8,128)S(1)} %get-tuple-element.32.py0_ref), channel_id=1, source_target_pairs={{0,32},{4,36},{8,40},{12,44},{16,48},{20,52},{24,56},{28,60},{32,0... | collective-permute-start | bytes 1277960 | tf_op jit(solution)/shard_map/ppermute | solution.py:486
  11.5 29.8 %collective-permute-start.3 = (f32[832,128]{1,0:T(8,128)S(1)}, f32[832,128]{1,0:T(8,128)S(1)}, u32[]{:S(2)}, u32[]{:S(2)}) collective-permute-start(f32[832,128]{1,0:T(8,128)S(1)} %get-tuple-element.33.py1_ref), channel_id=1, source_target_pairs={{32,64},{36,68},{40,72},{44,76},{48,80},{52,84},{56,88},{60,92},{6... | collective-permute-start | bytes 1277960 | tf_op jit(solution)/shard_map/ppermute | solution.py:486
  30.8 8.6 %collective-permute-start.8 = (f32[704,128]{1,0:T(8,128)S(1)}, f32[704,128]{1,0:T(8,128)S(1)}, u32[]{:S(2)}, u32[]{:S(2)}) collective-permute-start(f32[704,128]{1,0:T(8,128)S(1)} %get-tuple-element.43), channel_id=1, source_target_pairs={{0,1},{1,0},{2,3},{3,2},{4,5},{5,4},{6,7},{7,6},{8,9},{9,8},{10,11... | collective-permute-start | bytes 1081352 | tf_op jit(solution)/shard_map/ppermute | solution.py:490
  33.5 7.8 %collective-permute-start.4 = (f32[72,128]{1,0:T(8,128)S(1)}, f32[72,128]{1,0:T(8,128)S(1)}, u32[]{:S(2)}, u32[]{:S(2)}) collective-permute-start(f32[72,128]{1,0:T(8,128)S(1)} %get-tuple-element.36), channel_id=1, source_target_pairs={{0,32},{4,36},{8,40},{12,44},{16,48},{20,52},{24,56},{28,60},{32,0... | collective-permute-start | bytes 110600 | tf_op jit(solution)/shard_map/ppermute | solution.py:486
  33.6 9.3 %collective-permute-start.5 = (f32[72,128]{1,0:T(8,128)S(1)}, f32[72,128]{1,0:T(8,128)S(1)}, u32[]{:S(2)}, u32[]{:S(2)}) collective-permute-start(f32[72,128]{1,0:T(8,128)S(1)} %get-tuple-element.37), channel_id=1, source_target_pairs={{32,64},{36,68},{40,72},{44,76},{48,80},{52,84},{56,88},{60,92},{6... | collective-permute-start | bytes 110600 | tf_op jit(solution)/shard_map/ppermute | solution.py:486
  39.4 15.1 %collective-permute-start.9 = (f32[704,128]{1,0:T(8,128)S(1)}, f32[704,128]{1,0:T(8,128)S(1)}, u32[]{:S(2)}, u32[]{:S(2)}) collective-permute-start(f32[704,128]{1,0:T(8,128)S(1)} %add.13), channel_id=1, source_target_pairs={{0,2},{1,3},{2,0},{3,1},{4,6},{5,7},{6,4},{7,5},{8,10},{9,11},{10,... | collective-permute-start | bytes 1081352 | tf_op jit(solution)/shard_map/ppermute | solution.py:490
  45.2 3.5 %collective-permute-start.6 = (f32[344,128]{1,0:T(8,128)S(1)}, f32[344,128]{1,0:T(8,128)S(1)}, u32[]{:S(2)}, u32[]{:S(2)}) collective-permute-start(f32[344,128]{1,0:T(8,128)S(1)} %get-tuple-element.41), channel_id=1, source_target_pairs={{0,1},{1,0},{2,3},{3,2},{4,5},{5,4},{6,7},{7,6},{8,9},{9,8},{10,11... | collective-permute-start | bytes 528392 | tf_op jit(solution)/shard_map/ppermute | solution.py:490
  48.8 8.0 %collective-permute-start.7 = (f32[344,128]{1,0:T(8,128)S(1)}, f32[344,128]{1,0:T(8,128)S(1)}, u32[]{:S(2)}, u32[]{:S(2)}) collective-permute-start(f32[344,128]{1,0:T(8,128)S(1)} %add.12), channel_id=1, source_target_pairs={{0,2},{1,3},{2,0},{3,1},{4,6},{5,7},{6,4},{7,5},{8,10},{9,11},{10,... | collective-permute-start | bytes 528392 | tf_op jit(solution)/shard_map/ppermute | solution.py:490
  56.8 2.5 %collective-permute-start.10 = (f32[704,128]{1,0:T(8,128)S(1)}, f32[704,128]{1,0:T(8,128)S(1)}, u32[]{:S(2)}, u32[]{:S(2)}) collective-permute-start(f32[704,128]{1,0:T(8,128)S(1)} %add.14.mine_ref), channel_id=1, source_target_pairs={{0,1},{1,0},{2,3},{3,2},{4,5},{5,4},{6,7},{7,6},{8,9},{9,8},{10,11... | collective-permute-start | bytes 1081352 | tf_op jit(solution)/shard_map/ppermute | solution.py:490
  57.8 1.5 %collective-permute-start.11 = (f32[344,128]{1,0:T(8,128)S(1)}, f32[344,128]{1,0:T(8,128)S(1)}, u32[]{:S(2)}, u32[]{:S(2)}) collective-permute-start(f32[344,128]{1,0:T(8,128)S(1)} %add.15.mine_b_ref), channel_id=1, source_target_pairs={{0,1},{1,0},{2,3},{3,2},{4,5},{5,4},{6,7},{7,6},{8,9},{9,8},{10,11... | collective-permute-start | bytes 528392 | tf_op jit(solution)/shard_map/ppermute | solution.py:490
